TPU v7x, 32 devices: a whole 2x2x4 slice. The times are simulated.
32 devices in a mesh: ctx: 8 (over z, y), exp: 4 (over x, core).
Axes of the slice: x: 2, y: 2, z: 4, core: 2. Of those that a mesh axis runs over, the one named last changes fastest.
Arguments:
- tokens: bfloat16 [4, 1024, 1536], P('exp', 'ctx'), may hold values from -6 to 6
- cotangent: bfloat16 [4, 1024, 1536], P('exp', 'ctx'), may hold values from -6 to 6
- lengths: int32 [4, 2], P('exp'), may hold values from 512 to 512, as said below
- span_perm: int32 [4, 16], P('exp'), may hold values from 0 to 15, as said below
- routes: int32 [4, 1024, 8], P('exp', 'ctx'), may hold values from 0 to 39, all different within a row; in each aligned block of 128 rows (0 to 127, 128 to 255, ..., all dimensions but the last counted through in order) at most 38 rows name the same one
- norm_attn: float32 [1536], P(('ctx', 'exp')), may hold values from 0.25 to 1.75
- attn_q: float32 [1536, 1536], P(('ctx', 'exp')), may hold values from -0.15625 to 0.15625
- attn_k: float32 [1536, 512], P(('ctx', 'exp')), may hold values from -0.15625 to 0.15625
- attn_v: float32 [1536, 512], P(('ctx', 'exp')), may hold values from -0.15625 to 0.15625
- attn_o: float32 [1536, 1536], P(('ctx', 'exp')), may hold values from -2.5 to 2.5
- router: float32 [1536, 40], P(('ctx', 'exp')), may hold values from -0.078125 to 0.078125
- norm_moe: float32 [1536], P(('ctx', 'exp')), may hold values from 0.25 to 1.75
- expert_in: float32 [1536, 40, 1024], P('ctx', 'exp'), may hold values from -0.15625 to 0.15625
- expert_out: float32 [1536, 40, 512], P('ctx', 'exp'), may hold values from -1 to 1
Outputs:
- output: bfloat16 [4, 1024, 1536], P('exp', 'ctx')
- grad_tokens: float32 [4, 1024, 1536], P('exp', 'ctx')
- grad_norm_attn: float32 [1536], P(('ctx', 'exp'))
- grad_attn_q: float32 [1536, 1536], P(('ctx', 'exp'))
- grad_attn_k: float32 [1536, 512], P(('ctx', 'exp'))
- grad_attn_v: float32 [1536, 512], P(('ctx', 'exp'))
- grad_attn_o: float32 [1536, 1536], P(('ctx', 'exp'))
- grad_router: float32 [1536, 40], P(('ctx', 'exp'))
- grad_norm_moe: float32 [1536], P(('ctx', 'exp'))
- grad_expert_in: float32 [1536, 40, 1024], P('ctx', 'exp')
- grad_expert_out: float32 [1536, 40, 512], P('ctx', 'exp')
Inputs may be any that keep to these rules, and one draw needn't show every extreme that they name: Each group has 2 sequences whose lengths sum to 1024; the longer one has 512 rows or more; in group 0 it has 512. `span_perm`: each row is a permutation; slots 2 d and 2 d + 1 hold spans j and 15 - j for some j. `routes`: each row names 8 different experts; in the 128 rows of one device no expert is named more than 38 times.
All inputs are finite; a program needn't handle non-finite values.
Results may differ from a plain program's by a relative error of at most 0.03.
Values may be sent and summed in bfloat16 or wider, within the bound.
A program may use at most 448 MiB of HBM per device.

v0:
```python
import math

import jax
import jax.numpy as jnp
from jax import lax
from jax.sharding import PartitionSpec as P

D = 1536
HEADS = 24
KV_HEADS = 8
HEAD = 64
HID = 512
TOP = 8
EXP_DEV = 10
SPAN = 64


EPSILON = 1e-06
NEGATIVE = -1e30


def global_rows(perm_row, rows):
    slots = rows // SPAN
    match = slots[:, None] == jnp.arange(perm_row.shape[0], dtype=jnp.int32)[None, :]
    spans = jnp.sum(jnp.where(match, perm_row[None, :], 0), axis=1)
    return spans * SPAN + rows % SPAN


def rotary(tensor, position, sign):
    half = HEAD // 2
    freqs = jnp.exp(jnp.arange(half, dtype=jnp.float32) * (-2.0 * math.log(10000.0) / HEAD))
    angle = position.astype(jnp.float32)[:, None] * freqs[None, :]
    cosine = jnp.cos(angle)[:, None, :]
    sine = sign * jnp.sin(angle)[:, None, :]
    first, second = (tensor[..., :half], tensor[..., half:])
    return jnp.concatenate(
        [first * cosine - second * sine, second * cosine + first * sine], axis=-1
    )


def allowed(query_rows, key_rows, first_len):
    later = key_rows[None, :] <= query_rows[:, None]
    same_seq = (key_rows[None, :] >= first_len) == (query_rows[:, None] >= first_len)
    return later & same_seq


def contract_rows(left, right):
    return lax.dot_general(
        left, right, (((0,), (0,)), ((), ())), preferred_element_type=jnp.float32
    )


def contract_cols(left, right):
    return lax.dot_general(
        left, right, (((1,), (1,)), ((), ())), preferred_element_type=jnp.float32
    )


def block_grads(
    query_block,
    grad_block,
    lse_block,
    drift_block,
    query_rows,
    key_block,
    value_block,
    key_rows,
    first_len,
):
    softmax_scale = HEAD ** (-0.5)
    scores = (
        jnp.einsum("qgrd,kgd->grqk", query_block, key_block, preferred_element_type=jnp.float32)
        * softmax_scale
    )
    mask = allowed(query_rows, key_rows, first_len)[None, None]
    weights = jnp.where(mask, jnp.exp(scores - lse_block.transpose(1, 2, 0)[..., None]), 0.0)
    prob_grad = jnp.einsum(
        "qgrd,kgd->grqk", grad_block, value_block, preferred_element_type=jnp.float32
    )
    score_grad = (weights * (prob_grad - drift_block.transpose(1, 2, 0)[..., None])).astype(
        jnp.bfloat16
    )
    query_grad = None
    key_grad = None
    value_grad = None
    query_grad = (
        jnp.einsum("grqk,kgd->qgrd", score_grad, key_block, preferred_element_type=jnp.float32)
        * softmax_scale
    )
    value_grad = jnp.einsum(
        "grqk,qgrd->kgd",
        weights.astype(jnp.bfloat16),
        grad_block,
        preferred_element_type=jnp.float32,
    )
    key_grad = (
        jnp.einsum("grqk,qgrd->kgd", score_grad, query_block, preferred_element_type=jnp.float32)
        * softmax_scale
    )
    return (query_grad, key_grad, value_grad)


def body(
    tokens,
    cotangent,
    lengths,
    span_perm,
    routes,
    norm_attn,
    attn_q,
    attn_k,
    attn_v,
    attn_o,
    router,
    norm_moe,
    expert_in,
    expert_out,
):
    count = tokens.shape[1]
    repeat = HEADS // KV_HEADS
    experts = EXP_DEV * lax.axis_size("exp")
    capacity = count * TOP * 3 // (2 * experts)
    softmax_scale = HEAD ** (-0.5)
    perm_row = span_perm[0]
    first_len = lengths[0, 0]
    query_rows = global_rows(
        perm_row, lax.axis_index("ctx") * count + jnp.arange(count, dtype=jnp.int32)
    )
    position = query_rows - jnp.where(query_rows >= first_len, first_len, 0)
    gathered = (
        lax.all_gather(norm_attn.astype(jnp.bfloat16), ("ctx", "exp"), axis=0, tiled=True),
        lax.all_gather(attn_q.astype(jnp.bfloat16), ("ctx", "exp"), axis=0, tiled=True),
        lax.all_gather(attn_k.astype(jnp.bfloat16), ("ctx", "exp"), axis=0, tiled=True),
        lax.all_gather(attn_v.astype(jnp.bfloat16), ("ctx", "exp"), axis=0, tiled=True),
        lax.all_gather(attn_o.astype(jnp.bfloat16), ("ctx", "exp"), axis=0, tiled=True),
        lax.all_gather(router.astype(jnp.bfloat16), ("ctx", "exp"), axis=0, tiled=True),
        lax.all_gather(norm_moe.astype(jnp.bfloat16), ("ctx", "exp"), axis=0, tiled=True),
    )
    gain_one, weight_q, weight_k, weight_v, weight_o, weight_r, gain_two = gathered
    weight_in, weight_out = (
        lax.all_gather(expert_in.astype(jnp.bfloat16), "ctx", axis=0, tiled=True),
        lax.all_gather(expert_out.astype(jnp.bfloat16), "ctx", axis=0, tiled=True),
    )
    gain_one_f = gain_one.astype(jnp.float32)
    gain_two_f = gain_two.astype(jnp.float32)
    resid = tokens[0].astype(jnp.float32)
    scale_one = lax.rsqrt(jnp.mean(resid * resid, axis=-1, keepdims=True) + EPSILON)
    normed_one = resid * scale_one
    hidden_one = (normed_one * gain_one_f).astype(jnp.bfloat16)
    query_pre = jnp.dot(hidden_one, weight_q, preferred_element_type=jnp.float32).reshape(
        count, HEADS, HEAD
    )
    queries = (
        rotary(query_pre, position, 1.0).astype(jnp.bfloat16).reshape(count, KV_HEADS, repeat, HEAD)
    )
    key_pre = jnp.dot(hidden_one, weight_k, preferred_element_type=jnp.float32).reshape(
        count, KV_HEADS, HEAD
    )
    keys = rotary(key_pre, position, 1.0).astype(jnp.bfloat16)
    values = (
        jnp.dot(hidden_one, weight_v, preferred_element_type=jnp.float32)
        .astype(jnp.bfloat16)
        .reshape(count, KV_HEADS, HEAD)
    )
    start_state = (
        jnp.full((KV_HEADS, repeat, count), NEGATIVE, jnp.float32),
        jnp.zeros((KV_HEADS, repeat, count), jnp.float32),
        jnp.zeros((KV_HEADS, repeat, count, HEAD), jnp.float32),
    )
    carry = start_state
    key_piece = lax.all_gather(keys, "ctx", axis=0, tiled=True)
    value_piece = lax.all_gather(values, "ctx", axis=0, tiled=True)
    size = key_piece.shape[0]
    block = math.gcd(size, 512)
    number = size // block
    key_blocks = key_piece.reshape(number, block, KV_HEADS, HEAD)
    value_blocks = value_piece.reshape(number, block, KV_HEADS, HEAD)
    offsets = jnp.arange(size, dtype=jnp.int32).reshape(number, block)

    def forward_step(state, inputs):
        highest, total, accum = state
        key_block, value_block, offset = inputs
        key_rows = global_rows(perm_row, offset)
        scores = (
            jnp.einsum("qgrd,kgd->grqk", queries, key_block, preferred_element_type=jnp.float32)
            * softmax_scale
        )
        mask = allowed(query_rows, key_rows, first_len)[None, None]
        scores = jnp.where(mask, scores, NEGATIVE)
        newmax = jnp.maximum(highest, jnp.max(scores, axis=-1))
        weights = jnp.where(mask, jnp.exp(scores - newmax[..., None]), 0.0)
        factor = jnp.exp(highest - newmax)
        total = total * factor + jnp.sum(weights, axis=-1)
        accum = accum * factor[..., None] + jnp.einsum(
            "grqk,kgd->grqd",
            weights.astype(jnp.bfloat16),
            value_block,
            preferred_element_type=jnp.float32,
        )
        return ((newmax, total, accum), None)

    carry, _ = lax.scan(forward_step, carry, (key_blocks, value_blocks, offsets))
    highest, total, accum = carry
    log_total = (highest + jnp.log(total)).transpose(2, 0, 1)
    attended = (accum / total[..., None]).transpose(2, 0, 1, 3)
    attended_b = attended.reshape(count, HEADS * HEAD).astype(jnp.bfloat16)
    middle = resid + jnp.dot(attended_b, weight_o, preferred_element_type=jnp.float32)
    scale_two = lax.rsqrt(jnp.mean(middle * middle, axis=-1, keepdims=True) + EPSILON)
    normed_two = middle * scale_two
    hidden_two = (normed_two * gain_two_f).astype(jnp.bfloat16)
    logits = jnp.dot(hidden_two, weight_r, preferred_element_type=jnp.float32)
    chosen = routes[0]
    picks = chosen[:, :, None] == jnp.arange(experts, dtype=jnp.int32)[None, None, :]
    selected = jnp.sum(jnp.where(picks, logits[:, None, :], 0.0), axis=-1)
    gates = jax.nn.softmax(selected, axis=-1)
    gates_b = gates.astype(jnp.bfloat16)
    flat_picks = picks.reshape(count * TOP, experts).astype(jnp.int32)
    placed = jnp.sum((jnp.cumsum(flat_picks, axis=0) - 1) * flat_picks, axis=-1)
    column = chosen.reshape(-1) * capacity + placed
    hits = (
        column.reshape(count, TOP)[:, :, None]
        == jnp.arange(experts * capacity, dtype=jnp.int32)[None, None, :]
    )
    spread = jnp.any(hits, axis=1).astype(jnp.bfloat16)
    weighted = jnp.sum(
        jnp.where(hits, gates_b.astype(jnp.float32)[:, :, None], 0.0), axis=1
    ).astype(jnp.bfloat16)
    outgoing = contract_rows(spread, hidden_two).astype(jnp.bfloat16).reshape(experts, capacity, D)
    incoming = lax.all_to_all(outgoing, "exp", split_axis=0, concat_axis=1, tiled=True)
    gate_up = jnp.einsum("erd,dec->erc", incoming, weight_in, preferred_element_type=jnp.float32)
    gate_part = gate_up[..., :HID]
    up_part = gate_up[..., HID:]
    sigmoid_gate = jax.nn.sigmoid(gate_part)
    silu_gate = gate_part * sigmoid_gate
    activated = (silu_gate * up_part).astype(jnp.bfloat16)
    produced = jnp.einsum(
        "erh,deh->erd", activated, weight_out, preferred_element_type=jnp.float32
    ).astype(jnp.bfloat16)
    returned = lax.all_to_all(produced, "exp", split_axis=1, concat_axis=0, tiled=True).reshape(
        experts * capacity, D
    )
    mixture = jnp.dot(weighted, returned, preferred_element_type=jnp.float32)
    output = (middle + mixture).astype(jnp.bfloat16)
    upstream = cotangent[0].astype(jnp.float32)
    upstream_b = upstream.astype(jnp.bfloat16)
    sent_grad = (
        contract_rows(weighted, upstream_b).astype(jnp.bfloat16).reshape(experts, capacity, D)
    )
    grad_in = lax.all_to_all(sent_grad, "exp", split_axis=0, concat_axis=1, tiled=True)
    picked = jnp.take(returned, column, axis=0).reshape(count, TOP, D)
    gate_grad = jnp.einsum("tkd,td->tk", picked, upstream_b, preferred_element_type=jnp.float32)
    grad_act = (
        jnp.einsum("erd,deh->erh", grad_in, weight_out, preferred_element_type=jnp.float32)
        .astype(jnp.bfloat16)
        .astype(jnp.float32)
    )
    grad_gate = grad_act * up_part * (sigmoid_gate * (1.0 + gate_part * (1.0 - sigmoid_gate)))
    grad_up = grad_act * silu_gate
    grad_gu = jnp.concatenate([grad_gate, grad_up], axis=-1).astype(jnp.bfloat16)
    grad_weight_out = jnp.einsum(
        "erd,erh->deh", grad_in, activated, preferred_element_type=jnp.float32
    )
    grad_weight_in = jnp.einsum(
        "erd,erc->dec", incoming, grad_gu, preferred_element_type=jnp.float32
    )
    grad_rows = jnp.einsum(
        "erc,dec->erd", grad_gu, weight_in, preferred_element_type=jnp.float32
    ).astype(jnp.bfloat16)
    back_rows = lax.all_to_all(grad_rows, "exp", split_axis=1, concat_axis=0, tiled=True).reshape(
        experts * capacity, D
    )
    expert_sums = (
        lax.psum_scatter(
            grad_weight_in.astype(jnp.bfloat16), "ctx", scatter_dimension=0, tiled=True
        ).astype(jnp.float32),
        lax.psum_scatter(
            grad_weight_out.astype(jnp.bfloat16), "ctx", scatter_dimension=0, tiled=True
        ).astype(jnp.float32),
    )
    centered = gate_grad - jnp.sum(gates * gate_grad, axis=-1, keepdims=True)
    select_grad = gates * centered
    logit_grad = jnp.sum(jnp.where(picks, select_grad[:, :, None], 0.0), axis=1).astype(
        jnp.bfloat16
    )
    grad_router = contract_rows(hidden_two, logit_grad)
    grad_norm_two = jnp.dot(spread, back_rows, preferred_element_type=jnp.float32) + contract_cols(
        logit_grad, weight_r
    )
    grad_gain_two = jnp.sum(grad_norm_two * normed_two, axis=0)
    scaled_two = grad_norm_two * gain_two_f
    grad_middle = upstream + scale_two * (
        scaled_two - normed_two * jnp.mean(scaled_two * normed_two, axis=-1, keepdims=True)
    )
    branch_grad = grad_middle.astype(jnp.bfloat16)
    grad_weight_o = contract_rows(attended_b, branch_grad)
    grad_heads = (
        contract_cols(branch_grad, weight_o)
        .astype(jnp.bfloat16)
        .reshape(count, KV_HEADS, repeat, HEAD)
    )
    drift = jnp.sum(grad_heads.astype(jnp.float32) * attended, axis=-1)
    query_acc = jnp.zeros((count, KV_HEADS, repeat, HEAD), jnp.float32)
    key_piece = lax.all_gather(keys, "ctx", axis=0, tiled=True)
    value_piece = lax.all_gather(values, "ctx", axis=0, tiled=True)
    size = key_piece.shape[0]
    block = math.gcd(size, 512)
    number = size // block
    key_blocks = key_piece.reshape(number, block, KV_HEADS, HEAD)
    value_blocks = value_piece.reshape(number, block, KV_HEADS, HEAD)
    offsets = jnp.arange(size, dtype=jnp.int32).reshape(number, block)

    def backward_step(acc, inputs):
        key_block, value_block, offset = inputs
        part_q, part_k, part_v = block_grads(
            queries,
            grad_heads,
            log_total,
            drift,
            query_rows,
            key_block,
            value_block,
            global_rows(perm_row, offset),
            first_len,
        )
        joined = jnp.concatenate(
            [part_k.reshape(block, KV_HEADS * HEAD), part_v.reshape(block, KV_HEADS * HEAD)],
            axis=-1,
        )
        return (acc + part_q, joined)

    query_acc, joined_parts = lax.scan(
        backward_step, query_acc, (key_blocks, value_blocks, offsets)
    )
    pair_acc = joined_parts.reshape(size, 2 * KV_HEADS * HEAD)
    query_grad, pair_acc = (query_acc, pair_acc)
    pair_own = lax.psum_scatter(
        pair_acc.astype(jnp.bfloat16), "ctx", scatter_dimension=0, tiled=True
    ).astype(jnp.float32)
    key_grad = pair_own[:, : KV_HEADS * HEAD].reshape(count, KV_HEADS, HEAD)
    value_grad = pair_own[:, KV_HEADS * HEAD :].reshape(count, KV_HEADS, HEAD)
    query_grad_b = (
        rotary(query_grad.reshape(count, HEADS, HEAD), position, -1.0)
        .astype(jnp.bfloat16)
        .reshape(count, HEADS * HEAD)
    )
    key_grad_b = (
        rotary(key_grad, position, -1.0).astype(jnp.bfloat16).reshape(count, KV_HEADS * HEAD)
    )
    value_grad_b = value_grad.astype(jnp.bfloat16).reshape(count, KV_HEADS * HEAD)
    grad_weight_q = contract_rows(hidden_one, query_grad_b)
    grad_weight_k = contract_rows(hidden_one, key_grad_b)
    grad_weight_v = contract_rows(hidden_one, value_grad_b)
    grad_hidden_one = (
        contract_cols(query_grad_b, weight_q)
        + contract_cols(key_grad_b, weight_k)
        + contract_cols(value_grad_b, weight_v)
    )
    grad_gain_one = jnp.sum(grad_hidden_one * normed_one, axis=0)
    scaled_one = grad_hidden_one * gain_one_f
    grad_tokens = grad_middle + scale_one * (
        scaled_one - normed_one * jnp.mean(scaled_one * normed_one, axis=-1, keepdims=True)
    )
    attn_sums = (
        lax.psum_scatter(grad_gain_one, ("ctx", "exp"), scatter_dimension=0, tiled=True),
        lax.psum_scatter(grad_weight_q, ("ctx", "exp"), scatter_dimension=0, tiled=True),
        lax.psum_scatter(grad_weight_k, ("ctx", "exp"), scatter_dimension=0, tiled=True),
        lax.psum_scatter(grad_weight_v, ("ctx", "exp"), scatter_dimension=0, tiled=True),
        lax.psum_scatter(grad_weight_o, ("ctx", "exp"), scatter_dimension=0, tiled=True),
        lax.psum_scatter(grad_router, ("ctx", "exp"), scatter_dimension=0, tiled=True),
        lax.psum_scatter(grad_gain_two, ("ctx", "exp"), scatter_dimension=0, tiled=True),
    )
    return (
        output[None],
        grad_tokens[None],
        attn_sums[0],
        attn_sums[1],
        attn_sums[2],
        attn_sums[3],
        attn_sums[4],
        attn_sums[5],
        attn_sums[6],
        expert_sums[0],
        expert_sums[1],
    )


def solution(mesh):
    in_specs = (
        P("exp", "ctx", None),
        P("exp", "ctx", None),
        P("exp", None),
        P("exp", None),
        P("exp", "ctx", None),
        P(("ctx", "exp")),
        P(("ctx", "exp"), None),
        P(("ctx", "exp"), None),
        P(("ctx", "exp"), None),
        P(("ctx", "exp"), None),
        P(("ctx", "exp"), None),
        P(("ctx", "exp")),
        P("ctx", "exp", None),
        P("ctx", "exp", None),
    )
    out_specs = (
        P("exp", "ctx", None),
        P("exp", "ctx", None),
        P(("ctx", "exp")),
        P(("ctx", "exp"), None),
        P(("ctx", "exp"), None),
        P(("ctx", "exp"), None),
        P(("ctx", "exp"), None),
        P(("ctx", "exp"), None),
        P(("ctx", "exp")),
        P("ctx", "exp", None),
        P("ctx", "exp", None),
    )
    return jax.shard_map(body, mesh=mesh, in_specs=in_specs, out_specs=out_specs, check_vma=False)
```

profile of v0, /device:TPU:0, one launch (start us, length us, event | category | flops | bytes accessed | tf_op | source)
XLA Modules:
  0.0 2864.6 jit_solution(9820143960376987260)
XLA Ops:
  12.2 42.2 %all-reduce.5 = (bf16[1536]{0:T(1024)(128)(2,1)S(1)}, bf16[1536]{0:T(1024)(128)(2,1)S(1)}) all-reduce(bf16[1536]{0:T(1024)(128)(2,1)S(1)} %dynamic-update-slice, bf16[1536]{0:T(1024)(128)(2,1)S(1)} %dynamic-update-slice.1), channel_id=1, replica_groups=mesh['ctx'=8,'exp'=4] {'ctx','exp'}, use_global_device_ids=true, to_apply=%add | all-reduce | flops 3072 | bytes 12288
  58.3 10.8 all-gather.10.cloned.1.call-done
  73.3 53.1 %all-gather.16.cloned.1.call-done = bf16[1536,512]{1,0:T(8,128)(2,1)} async-done(((bf16[48,512]{1,0:T(8,128)(2,1)}), bf16[1536,512]{1,0:T(8,128)(2,1)}) %all-gather.16.cloned.1.call-update) | async-done | bytes 1572880 | tf_op jit(solution)/shard_map/all_gather | solution.py:134
  130.6 5.8 convert_element_type.243
  141.1 11.3 reduce-window.6
  155.7 11.9 all-gather.12.cloned.1.call-done
  169.9 38.6 %all-gather.18.cloned.1.call-done = bf16[1024,8,64]{0,2,1:T(8,128)(2,1)} async-done(((bf16[128,8,64]{0,2,1:T(8,128)(2,1)}), bf16[1024,8,64]{0,2,1:T(8,128)(2,1)}) %all-gather.18.cloned.1.call-update) | async-done | bytes 1048592 | tf_op jit(solution)/shard_map/all_gather | solution.py:172
  209.8 64.5 %all-gather.14.cloned.1.call-done = bf16[1536,1536]{1,0:T(8,128)(2,1)} async-done(((bf16[48,1536]{1,0:T(8,128)(2,1)}), bf16[1536,1536]{1,0:T(8,128)(2,1)}) %all-gather.14.cloned.1.call-update) | async-done | bytes 4718608 | tf_op jit(solution)/shard_map/all_gather | solution.py:132
  274.4 6.6 copy.142
  285.0 32.4 %while.32 = (s32[]{:T(128)}, f32[8,3,128]{2,1,0:T(4,128)S(1)}, f32[8,3,128]{2,1,0:T(4,128)S(1)}, f32[8,3,128,64]{2,3,1,0:T(8,128)S(1)}, s32[2,512]{1,0:T(2,128)}...) while((s32[]{:T(128)}, f32[8,3,128]{2,1,0:T(4,128)S(1)}, ...), condition=%wide.region_6.7_spmd.clone, body=%wide.region_2.6_spmd.clone.sunk | while | flops 423941248 | bytes 47548932 | solution.py:202
  289.9 4.8 fusion.195
  294.8 4.4 fusion.196
  306.1 4.8 fusion.195
  311.0 4.4 fusion.196
  318.5 21.7 all-gather.20.cloned.1.call-done
  347.1 6.9 reshape.684
  354.0 5.1 all-to-all-start
  359.1 89.7 %all-gather = bf16[32,48,40]{1,2,0:T(8,128)(2,1)S(1)} all-gather(bf16[1,48,40]{1,2,0:T(8,128)(2,1)S(1)} %convert_bitcast_fusion.1), channel_id=1, replica_groups=mesh['ctx'=8,'exp'=4] {'ctx','exp'}, dimensions={0}, use_global_device_ids=true | all-gather | bytes 126720 | tf_op jit(solution)/shard_map/all_gather | solution.py:136
  453.9 6.7 reshape.686
  460.6 5.0 all-to-all-start.2
  465.6 5.2 copy.220
  470.8 6.7 all_to_all.51
  477.5 44.1 %all-to-all-done.2 = bf16[40,38,1536]{2,1,0:T(8,128)(2,1)} async-done(((bf16[40,38,1536]{2,1,0:T(8,128)(2,1)}), bf16[40,38,1536]{2,1,0:T(8,128)(2,1)}, u32[]{:S(2)}, u32[]{:S(2)}) %all-to-all-start.2) | async-done | bytes 4669472 | tf_op jit(solution)/shard_map/all_to_all | solution.py:249
  521.5 5.2 copy.219
  526.7 6.7 all_to_all.58
  533.4 407.9 %all-gather.22.cloned.1.call-done = bf16[1536,10,1024]{2,0,1:T(8,128)(2,1)} async-done(((bf16[192,10,1024]{2,0,1:T(8,128)(2,1)}), bf16[1536,10,1024]{2,0,1:T(8,128)(2,1)}) %all-gather.22.cloned.1.call-update) | async-done | bytes 31457296 | tf_op jit(solution)/shard_map/all_gather | solution.py:141
  941.3 17.8 fusion.122
  959.1 199.0 %all-gather.24.cloned.1.call-done = bf16[1536,10,512]{2,0,1:T(8,128)(2,1)} async-done(((bf16[192,10,512]{2,0,1:T(8,128)(2,1)}), bf16[1536,10,512]{2,0,1:T(8,128)(2,1)}) %all-gather.24.cloned.1.call-update) | async-done | bytes 15728656 | tf_op jit(solution)/shard_map/all_gather | solution.py:142
  1158.1 13.6 fusion.55
  1171.7 9.2 convolution_convert_fusion.4
  1181.0 5.2 copy.153
  1186.2 6.0 all-to-all-start.1
  1192.2 17.4 convolution_convert_fusion.5
  1209.6 7.3 copy.157
  1216.9 58.6 %all-to-all-done.1 = bf16[10,152,1536]{2,0,1:T(8,128)(2,1)} async-done(((bf16[10,152,1536]{2,0,1:T(8,128)(2,1)}), bf16[10,152,1536]{2,0,1:T(8,128)(2,1)}, u32[]{:S(2)}, u32[]{:S(2)}) %all-to-all-start.1) | async-done | bytes 4669472 | tf_op jit(solution)/shard_map/all_to_all | solution.py:239
  1275.5 5.6 all-to-all-start.3
  1282.1 8.0 copy.155
  1290.1 6.7 reshape.685
  1296.8 67.6 %all-to-all-done.3 = bf16[10,152,1536]{2,0,1:T(8,128)(2,1)} async-done(((bf16[10,152,1536]{2,0,1:T(8,128)(2,1)}), bf16[10,152,1536]{2,0,1:T(8,128)(2,1)}, u32[]{:S(2)}, u32[]{:S(2)}) %all-to-all-start.3) | async-done | bytes 4669472 | tf_op jit(solution)/shard_map/all_to_all | solution.py:269
  1364.4 8.0 copy.159
  1372.3 6.7 reshape.687
  1382.3 10.2 gather_fusion
  1392.5 4.3 fusion.52
  1398.3 4.3 convolution_convert_fusion.6
  1404.7 40.1 %while.33 = (s32[]{:T(128)}, f32[128,8,3,64]{0,3,2,1:T(8,128)}, bf16[2,512,1024]{2,1,0:T(8,128)(2,1)}, bf16[2,512,8,64]{1,3,2,0:T(8,128)(2,1)}, s32[2,512]{1,0:T...) while((s32[]{:T(128)}, f32[128,8,3,64]{0,3,2,1:T(8,128)}, ...), condition=%wide.region_22.23_spmd.clone, body=%wide.region_20.22_spmd.clone.sunk | while | flops 1025808512 | bytes 70716120 | solution.py:331
  1417.8 4.1 fusion.212
  1447.2 10.2 convolution_convert_fusion.1
  1457.5 20.8 copy.193
  1480.2 15.5 convolution_convert_fusion
  1495.7 40.8 %copy.191 = bf16[1536,10240]{1,0:T(8,128)(2,1)} copy(bf16[1536,10240]{0,1:T(8,128)(2,1)} %bitcast.338) | data formatting | bytes 62914560
  1544.4 5.0 fusion.86
  1550.7 4.9 fusion.88
  1555.6 5.2 fusion.124
  1560.8 4.1 fusion.59
  1564.9 45.1 %reduce-scatter.25.cloned.1.call-done = f32[48,40]{1,0:T(8,128)} async-done(((f32[1536,40]{1,0:T(8,128)}), f32[48,40]{1,0:T(8,128)}) %reduce-scatter.25.cloned.1.call-update) | async-done | bytes 7696
  1615.6 45.7 %all-reduce.4 = (f32[1536]{0:T(1024)S(1)}, f32[1536]{0:T(1024)S(1)}) all-reduce(f32[1536]{0:T(1024)S(1)} %get-tuple-element.578, f32[1536]{0:T(1024)S(1)} %copy-done.45), channel_id=3, replica_groups=mesh['ctx'=8,'exp'=4] {'ctx','exp'}, use_global_device_ids=true, to_apply=%region_26.27.clone | all-reduce | flops 3072 | bytes 24576
  1664.2 200.7 %reduce-scatter.29.cloned.1.call-done = bf16[192,5120]{1,0:T(8,128)(2,1)} async-done(((bf16[1536,5120]{1,0:T(8,128)(2,1)}), bf16[192,5120]{1,0:T(8,128)(2,1)}) %reduce-scatter.29.cloned.1.call-update) | async-done | bytes 1966096
  1870.6 491.3 %reduce-scatter.27.cloned.1.call-done = bf16[192,10240]{1,0:T(8,128)(2,1)} async-done(((bf16[1536,10240]{1,0:T(8,128)(2,1)}), bf16[192,10240]{1,0:T(8,128)(2,1)}) %reduce-scatter.27.cloned.1.call-update) | async-done | bytes 3932176
  2361.9 7.2 copy.192
  2369.1 8.3 copy.167
  2377.4 91.2 %reduce-scatter.19.cloned.1.call-done = f32[48,512]{1,0:T(8,128)} async-done(((f32[1536,512]{1,0:T(8,128)}), f32[48,512]{1,0:T(8,128)}) %reduce-scatter.19.cloned.1.call-update) | async-done | bytes 98320 | tf_op jit(solution)/shard_map/reduce_scatter | solution.py:366
  2468.5 106.4 %reduce-scatter.21.cloned.1.call-done = f32[48,512]{1,0:T(8,128)} async-done(((f32[1536,512]{1,0:T(8,128)}), f32[48,512]{1,0:T(8,128)}) %reduce-scatter.21.cloned.1.call-update) | async-done | bytes 98320 | tf_op jit(solution)/shard_map/reduce_scatter | solution.py:367
  2574.9 141.0 %reduce-scatter.17.cloned.1.call-done = f32[48,1536]{1,0:T(8,128)} async-done(((f32[1536,1536]{1,0:T(8,128)}), f32[48,1536]{1,0:T(8,128)}) %reduce-scatter.17.cloned.1.call-update) | async-done | bytes 294928 | tf_op jit(solution)/shard_map/reduce_scatter | solution.py:365
  2715.8 142.0 %reduce-scatter.23.cloned.1.call-done = f32[48,1536]{1,0:T(8,128)} async-done(((f32[1536,1536]{1,0:T(8,128)}), f32[48,1536]{1,0:T(8,128)}) %reduce-scatter.23.cloned.1.call-update) | async-done | bytes 294928 | tf_op jit(solution)/shard_map/reduce_scatter | solution.py:368
  (325 shorter events, 130.0 us)
Async XLA Ops:
  7.2 119.3 %copy-start.2 = (bf16[1,128,1536]{2,1,0:T(8,128)(2,1)S(1)}, bf16[1,128,1536]{2,1,0:T(8,128)(2,1)}, u32[]{:S(2)}) copy-start(bf16[1,128,1536]{2,1,0:T(8,128)(2,1)} %param.18) | copy-start | bytes 1179652
  7.2 62.0 %all-gather.10.cloned.1.call-start = ((), (), s32[]{:S(2)}) async-start(), calls=%async_computation.12 | async-start | bytes 1622016 | tf_op jit(solution)/shard_map/all_gather | solution.py:133
  8.8 117.6 %all-gather.16.cloned.1.call-start = ((), (), s32[]{:S(2)}) async-start(), calls=%async_computation.15 | async-start | bytes 1622016 | tf_op jit(solution)/shard_map/all_gather | solution.py:134
  10.4 118.7 %copy-start.34 = (f32[48,1536]{1,0:T(8,128)S(1)}, f32[48,1536]{1,0:T(8,128)}, u32[]{:S(2)}) copy-start(f32[48,1536]{1,0:T(8,128)} %param.24) | copy-start | bytes 884740
  10.4 157.1 %all-gather.12.cloned.1.call-start = ((), (), s32[]{:S(2)}) async-start(), calls=%async_computation.13 | async-start | bytes 1179648 | tf_op jit(solution)/shard_map/all_gather | solution.py:171
  54.4 226.5 %copy-start.29 = (f32[1536]{0:T(1024)}, f32[1536]{0:T(1024)S(1)}, u32[]{:S(2)}) copy-start(f32[1536]{0:T(1024)S(1)} %convert_element_type.222) | copy-start | bytes 18436
  56.4 224.6 %copy-start.46 = (f32[128]{0:T(128)}, f32[128]{0:T(128)S(1)}, u32[]{:S(2)}) copy-start(f32[128]{0:T(128)S(1)} %add_rsqrt_fusion.1) | copy-start | bytes 1540
  58.3 226.5 %copy-start.32 = (f32[128,32]{0,1:T(8,128)}, f32[128,32]{0,1:T(8,128)S(1)}, u32[]{:S(2)}) copy-start(f32[128,32]{0,1:T(8,128)S(1)} %get-tuple-element.657) | copy-start | bytes 49156
  58.3 71.6 %copy-start.35 = (f32[48,1536]{1,0:T(8,128)S(1)}, f32[48,1536]{1,0:T(8,128)}, u32[]{:S(2)}) copy-start(f32[48,1536]{1,0:T(8,128)} %param.27) | copy-start | bytes 884740
  73.2 135.2 %all-gather.18.cloned.1.call-start = ((), (), s32[]{:S(2)}) async-start(), calls=%async_computation.16 | async-start | bytes 1179648 | tf_op jit(solution)/shard_map/all_gather | solution.py:172
  129.1 145.3 %all-gather.14.cloned.1.call-start = ((), (), s32[]{:S(2)}) async-start(), calls=%async_computation.14 | async-start | bytes 4866048 | tf_op jit(solution)/shard_map/all_gather | solution.py:132
  129.8 210.4 %all-gather.20.cloned.1.call-start = ((), (), s32[]{:S(2)}) async-start(), calls=%async_computation.17 | async-start | bytes 4866048 | tf_op jit(solution)/shard_map/all_gather | solution.py:135
  130.6 810.7 %all-gather.22.cloned.1.call-start = ((), (), s32[]{:S(2)}) async-start(), calls=%async_computation.18 | async-start | bytes 35389440 | tf_op jit(solution)/shard_map/all_gather | solution.py:141
  136.5 4.3 copy-start.39
  136.5 1021.6 %all-gather.24.cloned.1.call-start = ((), (), s32[]{:S(2)}) async-start(), calls=%async_computation.19 | async-start | bytes 17694720 | tf_op jit(solution)/shard_map/all_gather | solution.py:142
  153.5 190.0 %copy-start.37 = (f32[1536]{0:T(1024)}, f32[1536]{0:T(1024)S(1)}, u32[]{:S(2)}) copy-start(f32[1536]{0:T(1024)S(1)} %convert_element_type.236) | copy-start | bytes 18436
  294.7 4.6 copy-start
  310.9 4.6 copy-start
  317.4 29.7 %copy-start.20 = (f32[8,3,128,64]{2,3,1,0:T(8,128)}, f32[8,3,128,64]{2,3,1,0:T(8,128)S(1)}, u32[]{:S(2)}) copy-start(f32[8,3,128,64]{2,3,1,0:T(8,128)S(1)} %get-tuple-element.318) | copy-start | bytes 2359300
  318.5 28.6 copy-start.17
  343.4 1054.6 %copy-start.5 = (f32[128,1536]{1,0:T(8,128)}, f32[128,1536]{1,0:T(8,128)S(1)}, u32[]{:S(2)}) copy-start(f32[128,1536]{1,0:T(8,128)S(1)} %get-tuple-element.659) | copy-start | bytes 2359300
  343.6 105.6 %copy-start.11 = (bf16[128,1536]{1,0:T(8,128)(2,1)}, bf16[128,1536]{1,0:T(8,128)(2,1)S(1)}, u32[]{:S(2)}) copy-start(bf16[128,1536]{1,0:T(8,128)(2,1)S(1)} %multiply_convert_fusion.1) | copy-start | bytes 1179652
  354.0 5.1 copy-start.48
  354.0 96.4 %copy-start.24 = (bf16[1,128,1536]{2,1,0:T(8,128)(2,1)S(1)}, bf16[1,128,1536]{2,1,0:T(8,128)(2,1)}, u32[]{:S(2)}) copy-start(bf16[1,128,1536]{2,1,0:T(8,128)(2,1)} %param.19) | copy-start | bytes 1179652
  354.0 106.6 %all-to-all-start = ((bf16[40,38,1536]{2,1,0:T(8,128)(2,1)}), bf16[40,38,1536]{2,1,0:T(8,128)(2,1)}, u32[]{:S(2)}, u32[]{:S(2)}) async-start(bf16[40,38,1536]{2,1,0:T(8,128)(2,1)} %reshape.684), calls=%async_computation | async-start | bytes 9830400 | tf_op jit(solution)/shard_map/all_to_all | solution.py:229
  449.5 11.0 copy-start.53
  449.6 11.0 copy-start.55
  450.4 10.2 copy-start.16
  460.6 61.0 %all-to-all-start.2 = ((bf16[40,38,1536]{2,1,0:T(8,128)(2,1)}), bf16[40,38,1536]{2,1,0:T(8,128)(2,1)}, u32[]{:S(2)}, u32[]{:S(2)}) async-start(bf16[40,38,1536]{2,1,0:T(8,128)(2,1)} %reshape.686), calls=%async_computation.2 | async-start | bytes 9830400 | tf_op jit(solution)/shard_map/all_to_all | solution.py:249
  1171.7 9.2 copy-start.7
  1186.2 6.0 copy-start.13
  1186.2 89.3 %all-to-all-start.1 = ((bf16[10,152,1536]{2,0,1:T(8,128)(2,1)}), bf16[10,152,1536]{2,0,1:T(8,128)(2,1)}, u32[]{:S(2)}, u32[]{:S(2)}) async-start(bf16[10,152,1536]{2,0,1:T(8,128)(2,1)} %copy.153), calls=%async_computation.1 | async-start | bytes 14942208 | tf_op jit(solution)/shard_map/all_to_all | solution.py:239
  1216.9 64.2 %copy-start.40 = (s32[1,128,8]{1,2,0:T(8,128)S(1)}, s32[1,128,8]{1,2,0:T(8,128)}, u32[]{:S(2)}) copy-start(s32[1,128,8]{1,2,0:T(8,128)} %param.22) | copy-start | bytes 12292
  1216.9 64.4 %copy-start.59 = (pred[128,8]{0,1:T(8,128)(4,1)S(1)}, pred[128,8]{0,1:T(8,128)(4,1)}, u32[]{:S(2)}) copy-start(pred[128,8]{0,1:T(8,128)(4,1)} %get-tuple-element.638) | copy-start | bytes 3076
  1216.9 64.6 %copy-start.44 = (s32[1024]{0:T(1024)S(1)}, s32[1024]{0:T(1024)}, u32[]{:S(2)}) copy-start(s32[1024]{0:T(1024)} %copy-done.43) | copy-start | bytes 12292
  1275.5 88.9 %all-to-all-start.3 = ((bf16[10,152,1536]{2,0,1:T(8,128)(2,1)}), bf16[10,152,1536]{2,0,1:T(8,128)(2,1)}, u32[]{:S(2)}, u32[]{:S(2)}) async-start(bf16[10,152,1536]{2,0,1:T(8,128)(2,1)} %copy.157), calls=%async_computation.3 | async-start | bytes 14942208 | tf_op jit(solution)/shard_map/all_to_all | solution.py:269
  1281.0 255.6 %reduce-scatter.15.cloned.1.call-start = ((), (), s32[]{:S(2)}) async-start(), calls=%async_computation.20 | async-start | bytes 2359296 | tf_op jit(solution)/shard_map/reduce_scatter | solution.py:336
  1382.3 10.2 copy-start.25
  1392.5 4.4 copy-start.54
  1392.5 4.4 copy-start.56
  1392.5 4.5 copy-start.38
  1392.5 4.5 copy-start.58
  1398.1 5.5 copy-start.21
  1398.3 6.4 copy-start.9
  1404.7 40.2 %copy-start.42 = (bf16[128,40]{0,1:T(8,128)(2,1)S(1)}, bf16[128,40]{0,1:T(8,128)(2,1)}, u32[]{:S(2)}) copy-start(bf16[128,40]{0,1:T(8,128)(2,1)} %copy-done.41) | copy-start | bytes 30724
  1404.9 7.2 copy-start.49
  1404.9 7.2 copy-start.28
  1404.9 7.2 copy-start.51
  1407.1 8.0 copy-start.1
  1424.7 7.2 copy-start.49
  1424.7 7.2 copy-start.28
  1424.7 7.2 copy-start.51
  1426.9 8.0 copy-start.1
  1444.8 165.3 %reduce-scatter.25.cloned.1.call-start = ((), (), s32[]{:S(2)}) async-start(), calls=%async_computation.25 | async-start | bytes 811008
  1447.2 417.7 %reduce-scatter.29.cloned.1.call-start = ((), (), s32[]{:S(2)}) async-start(), calls=%async_computation.27 | async-start | bytes 17694720
  1478.3 883.6 %reduce-scatter.27.cloned.1.call-start = ((), (), s32[]{:S(2)}) async-start(), calls=%async_computation.26 | async-start | bytes 35389440
  1536.5 932.0 %reduce-scatter.19.cloned.1.call-start = ((), (), s32[]{:S(2)}) async-start(), calls=%async_computation.22 | async-start | bytes 3244032 | tf_op jit(solution)/shard_map/reduce_scatter | solution.py:366
  1536.6 4.5 copy-start.31
  1540.8 1034.0 %reduce-scatter.21.cloned.1.call-start = ((), (), s32[]{:S(2)}) async-start(), calls=%async_computation.23 | async-start | bytes 3244032 | tf_op jit(solution)/shard_map/reduce_scatter | solution.py:367
  1543.5 1172.4 %reduce-scatter.17.cloned.1.call-start = ((), (), s32[]{:S(2)}) async-start(), calls=%async_computation.21 | async-start | bytes 9732096 | tf_op jit(solution)/shard_map/reduce_scatter | solution.py:365
  1549.5 1308.3 %reduce-scatter.23.cloned.1.call-start = ((), (), s32[]{:S(2)}) async-start(), calls=%async_computation.24 | async-start | bytes 9732096 | tf_op jit(solution)/shard_map/reduce_scatter | solution.py:368
  1555.6 5.2 copy-start.6
  1555.6 55.9 %copy-start.12 = (bf16[1536,512]{1,0:T(8,128)(2,1)S(1)}, bf16[1536,512]{1,0:T(8,128)(2,1)}, u32[]{:S(2)}) copy-start(bf16[1536,512]{1,0:T(8,128)(2,1)} %all-gather.10.cloned.1.call-done) | copy-start | bytes 4718596
  1564.9 50.6 %copy-start.45 = (f32[1536]{0:T(1024)S(1)}, f32[1536]{0:T(1024)}, u32[]{:S(2)}) copy-start(f32[1536]{0:T(1024)} %get-tuple-element.576) | copy-start | bytes 18436
  (25 other events, 47.5 us)
Sparse Core Ops, SparseCore 0:
  11.5 57.6 all-gather.9
  72.6 53.8 all-gather.15
  129.1 38.4 all-gather.11
  170.0 38.4 all-gather.17
  211.8 62.5 all-gather.13
  277.7 62.4 all-gather.19
  342.3 598.9 all-gather.21
  943.5 214.5 all-gather.23
  1444.9 65.0 reduce-scatter.14
  1515.6 94.4 reduce-scatter.24
  1613.7 251.1 reduce-scatter.28
  1868.6 493.2 reduce-scatter.26
  2367.9 100.5 reduce-scatter.18
  2474.4 100.4 reduce-scatter.20
  2581.2 134.5 reduce-scatter.16
  2723.2 134.5 reduce-scatter.22
where the time goes:
time: 2870 us; the launch traced here: 2860 us
  waiting for transfers between devices  2200 us (77%)
  local copies, waits for them, and re-layouts  203 us (7%)
  matrix products  184 us (6%)
  blocking collectives  178 us (6%)
  other arithmetic  66 us (2%)
    unnamed x19, waiting for transfers between devices  737 us
    all_gather x1, waiting for transfers between devices, body(): lax.all_gather(expert_in.astype(jnp.bfloat16), 'ctx', axis=0, tiled=True)  408 us
    all_gather x1, waiting for transfers between devices, body(): lax.all_gather(expert_out.astype(jnp.bfloat16), 'ctx', axis=0, tiled=True)  199 us
    reduce_scatter x1, waiting for transfers between devices, body(): lax.psum_scatter(grad_weight_o, ('ctx', 'exp'), scatter_dimension=0, tile...  142 us
    reduce_scatter x1, waiting for transfers between devices, body(): lax.psum_scatter(grad_weight_q, ('ctx', 'exp'), scatter_dimension=0, tile...  141 us
    reduce_scatter x1, waiting for transfers between devices, body(): lax.psum_scatter(grad_weight_v, ('ctx', 'exp'), scatter_dimension=0, tile...  106 us
    unnamed x117, local copies, waits for them, and re-layouts  92.2 us
    reduce_scatter x1, waiting for transfers between devices, body(): lax.psum_scatter(grad_weight_k, ('ctx', 'exp'), scatter_dimension=0, tile...  91.2 us
  transfers between devices with their start and end apart: 20, of which 18 were waited for; matrix products, arithmetic and copies ran while one was open for 11% of the time, Pallas kernels for 0%

commit v1 on v0

--- a/solution.py
+++ b/solution.py
@@ -3,6 +3,8 @@
 import jax
 import jax.numpy as jnp
 from jax import lax
+from jax.experimental import pallas as pl
+from jax.experimental.pallas import tpu as pltpu
 from jax.sharding import PartitionSpec as P
 
 D = 1536
@@ -100,7 +102,7 @@
     return (query_grad, key_grad, value_grad)
 
 
-def body(
+def body_general(
     tokens,
     cotangent,
     lengths,
@@ -384,34 +386,482 @@
     )
 
 
+def rotate(tensor, cosine, sine):
+    half = HEAD // 2
+    first, second = (tensor[..., :half], tensor[..., half:])
+    return jnp.concatenate(
+        [first * cosine - second * sine, second * cosine + first * sine], axis=-1
+    )
+
+
+def unit_kernel(first_ref, gate_ref, up_ref, down_ref, unit_ref):
+    half = gate_ref.shape[-1]
+    unit_ref[0, :, :half] = gate_ref[0].astype(unit_ref.dtype)
+    unit_ref[0, :, half : 2 * half] = up_ref[0].astype(unit_ref.dtype)
+    unit_ref[0, :, 2 * half :] = down_ref[0].astype(unit_ref.dtype)
+
+
+def take_units(first, number, win, wout):
+    depth, half = win.shape[1], HID // 2
+    return pl.pallas_call(
+        unit_kernel,
+        grid_spec=pltpu.PrefetchScalarGridSpec(
+            num_scalar_prefetch=1,
+            grid=(number,),
+            in_specs=[
+                pl.BlockSpec(
+                    (1, depth, half), lambda j, f: ((f[0] + j) // 2, 0, lax.rem(f[0] + j, 2))
+                ),
+                pl.BlockSpec(
+                    (1, depth, half), lambda j, f: ((f[0] + j) // 2, 0, 2 + lax.rem(f[0] + j, 2))
+                ),
+                pl.BlockSpec(
+                    (1, depth, half), lambda j, f: ((f[0] + j) // 2, 0, lax.rem(f[0] + j, 2))
+                ),
+            ],
+            out_specs=pl.BlockSpec((1, depth, 3 * half), lambda j, f: (j, 0, 0)),
+        ),
+        out_shape=jax.ShapeDtypeStruct((number, depth, 3 * half), jnp.bfloat16),
+        name="take_units",
+    )(first.reshape(1), win, win, wout)
+
+
+def expert_kernel(depth, meta, x_ref, g_ref, gate_ref, *refs):
+    parts, (y_ref, d_ref), outs = refs[:8], refs[8:10], refs[10:18]
+    weight, du_ref, act_ref = refs[18:]
+    bf16, f32 = jnp.bfloat16, jnp.float32
+    j = pl.program_id(0)
+    shift, z, y, base = meta[0], meta[1], meta[2], meta[3]
+    half = HID // 2
+    offsets = [
+        pl.multiple_of(((z ^ (i % 4)) * 2 + (y ^ (i // 4))) * depth, 64) for i in range(8)
+    ]
+    for part, offset in zip(parts, offsets):
+        weight[pl.ds(offset, depth), :] = part[0]
+    expert = base + (j + shift) // 2
+    first = jnp.logical_or(j == 0, lax.rem(j + shift, 2) == 0)
+    keep = jnp.where(first, 0.0, 1.0)
+    pairs, _, rows, _ = x_ref.shape
+    step = 2
+
+    def forward(i, carry):
+        at = pl.ds(i * step, step)
+        flat = pl.ds(pl.multiple_of(i * step * rows, 32), step * rows)
+        x = x_ref[at, 0].reshape(step * rows, D)
+        g = g_ref[at, 0].reshape(step * rows, D)
+        gate = gate_ref[0, flat, :]
+        u = jnp.dot(x, weight[:, : 2 * half], preferred_element_type=f32)
+        raw = jnp.dot(g, weight[:, 2 * half :], preferred_element_type=f32)
+        u1, u2 = u[:, :half], u[:, half:]
+        sig = jax.nn.sigmoid(u1)
+        silu = u1 * sig
+        act = (silu * u2).astype(bf16).astype(f32)
+        dgate = jnp.sum(raw * act, axis=-1, keepdims=True)
+        dact = raw * gate
+        du1 = dact * u2 * (sig * (1.0 + u1 * (1.0 - sig)))
+        du = jnp.concatenate([du1, dact * silu], axis=-1).astype(bf16)
+        act_gated = (act * gate).astype(bf16)
+        du_ref[flat, :] = du
+        act_ref[flat, :] = act_gated
+        made = contract_cols(act_gated, weight[:, 2 * half :])
+        back = contract_cols(du, weight[:, : 2 * half])
+        lane = lax.broadcasted_iota(jnp.int32, (step * rows, 128), 1)
+        tail = jnp.where(lane == expert, dgate, 0.0)
+
+        @pl.when(first)
+        def _():
+            y_ref[at, 0] = made.astype(bf16).reshape(step, rows, D)
+            d_ref[at, 0, :, :D] = back.astype(bf16).reshape(step, rows, D)
+            d_ref[at, 0, :, D:] = tail.astype(bf16).reshape(step, rows, 128)
+
+        @pl.when(jnp.logical_not(first))
+        def _():
+            old_y = y_ref[at, 0].reshape(step * rows, D).astype(f32)
+            y_ref[at, 0] = (made + old_y).astype(bf16).reshape(step, rows, D)
+            old_d = d_ref[at, 0].reshape(step * rows, D + 128).astype(f32)
+            d_ref[at, 0, :, :D] = (back + old_d[:, :D]).astype(bf16).reshape(step, rows, D)
+            d_ref[at, 0, :, D:] = (tail + old_d[:, D:]).astype(bf16).reshape(step, rows, 128)
+
+        return carry
+
+    lax.fori_loop(0, pairs // step, forward, 0)
+
+    def gradient(i, carry):
+        at = pl.ds(pl.multiple_of(i * 256, 256), 256)
+        x = x_ref[:, 0, :, at].reshape(pairs * rows, 256)
+        g = g_ref[:, 0, :, at].reshape(pairs * rows, 256)
+        weight[at, : 2 * half] = contract_rows(x, du_ref[...]).astype(bf16)
+        weight[at, 2 * half :] = contract_rows(g, act_ref[...]).astype(bf16)
+        return carry
+
+    lax.fori_loop(0, D // 256, gradient, 0)
+    for out, offset in zip(outs, offsets):
+        out[0] = weight[pl.ds(offset, depth), :]
+
+
+def run_experts(meta, row_in, row_up, slot_gate, parts):
+    pairs, held, rows, _ = row_in.shape
+    units, depth, columns = parts[0].shape
+    held_block = lambda width: pl.BlockSpec(
+        (pairs, 1, rows, width), lambda j, m: (0, (j + m[0]) // 2, 0, 0)
+    )
+    unit_block = pl.BlockSpec((1, depth, columns), lambda j, m: (j, 0, 0))
+    bf16 = jnp.bfloat16
+    total = units * pairs * rows * D * columns * 6
+    return pl.pallas_call(
+        lambda *refs: expert_kernel(depth, *refs),
+        grid_spec=pltpu.PrefetchScalarGridSpec(
+            num_scalar_prefetch=1,
+            grid=(units,),
+            in_specs=[
+                held_block(D),
+                held_block(D),
+                pl.BlockSpec((1, pairs * rows, 1), lambda j, m: ((j + m[0]) // 2, 0, 0)),
+            ]
+            + [unit_block] * 8,
+            out_specs=[held_block(D), held_block(D + 128)] + [unit_block] * 8,
+            scratch_shapes=[
+                pltpu.VMEM((D, columns), bf16),
+                pltpu.VMEM((pairs * rows, HID), bf16),
+                pltpu.VMEM((pairs * rows, HID // 2), bf16),
+            ],
+        ),
+        out_shape=[
+            jax.ShapeDtypeStruct((pairs, held, rows, D), bf16),
+            jax.ShapeDtypeStruct((pairs, held, rows, D + 128), bf16),
+        ]
+        + [jax.ShapeDtypeStruct((units, depth, columns), bf16)] * 8,
+        compiler_params=pltpu.CompilerParams(vmem_limit_bytes=56 * 2**20),
+        cost_estimate=pl.CostEstimate(
+            flops=total, bytes_accessed=60 * 2**20, transcendentals=units * pairs * rows * HID
+        ),
+        name="experts",
+    )(meta, row_in, row_up, slot_gate, *parts)
+
+
+def spread_kernel(z_ref, low_ref, high_ref, in_ref, out_ref):
+    half = low_ref.shape[-1] // 3
+    for h, ref in enumerate((low_ref, high_ref)):
+        for p in range(2):
+            at = p * 2 * half + h * half
+            in_ref[0, :, at : at + half] = ref[0, :, p * half : (p + 1) * half].astype(in_ref.dtype)
+        out_ref[0, :, h * half : (h + 1) * half] = ref[0, :, 2 * half :].astype(out_ref.dtype)
+
+
+def place_units(z_index, units, number):
+    depth, columns = units.shape[1:]
+
+    def pick(h):
+        def index(i, z):
+            unit = 2 * i + h
+            return ((unit // number) ^ z[0]) * number + lax.rem(unit, number), 0, 0
+
+        return pl.BlockSpec((1, depth, columns), index)
+
+    return pl.pallas_call(
+        spread_kernel,
+        grid_spec=pltpu.PrefetchScalarGridSpec(
+            num_scalar_prefetch=1,
+            grid=(EXP_DEV,),
+            in_specs=[pick(0), pick(1)],
+            out_specs=[
+                pl.BlockSpec((1, depth, 2 * HID), lambda i, z: (i, 0, 0)),
+                pl.BlockSpec((1, depth, HID), lambda i, z: (i, 0, 0)),
+            ],
+        ),
+        out_shape=[
+            jax.ShapeDtypeStruct((EXP_DEV, depth, 2 * HID), jnp.float32),
+            jax.ShapeDtypeStruct((EXP_DEV, depth, HID), jnp.float32),
+        ],
+        name="place_units",
+    )(z_index.reshape(1), units, units)
+
+
+def body_heads(
+    tokens,
+    cotangent,
+    lengths,
+    span_perm,
+    routes,
+    norm_attn,
+    attn_q,
+    attn_k,
+    attn_v,
+    attn_o,
+    router,
+    norm_moe,
+    expert_in,
+    expert_out,
+):
+    bf16, f32 = jnp.bfloat16, jnp.float32
+    ctx_axes, tok_axes, all_axes = ("z", "y"), ("z", "exp"), ("z", "y", "exp")
+    n_z, n_y, n_exp = (lax.axis_size(a) for a in all_axes)
+    n_ctx = n_z * n_y
+    count = tokens.shape[1]
+    group = count * n_ctx
+    repeat = HEADS // KV_HEADS
+    width = repeat * HEAD
+    experts = EXP_DEV * n_exp
+    capacity = count * TOP * 3 // (2 * experts)
+    slots = -(-capacity // 8) * 8
+    own = attn_q.shape[0]
+    softmax_scale = HEAD ** (-0.5)
+    z_index = lax.axis_index("z")
+
+    units = 2 * EXP_DEV // n_z
+    y_index = lax.axis_index("y")
+    win = expert_in.transpose(1, 0, 2)
+    wout = expert_out.transpose(1, 0, 2)
+    swap_z = [[(i, i ^ s) for i in range(n_z)] for s in range(n_z)]
+    swap_y = [(i, i ^ 1) for i in range(n_y)]
+    near = [None] * 4
+    for s in (3, 2, 1, 0):
+        near[s] = take_units(units * (z_index ^ s), units, win, wout)
+        if s:
+            near[s] = lax.ppermute(near[s], "z", swap_z[s])
+    parts = near + [lax.ppermute(a, "y", swap_y) for a in near]
+
+    wq, wk, wv = (a.astype(bf16) for a in (attn_q, attn_k, attn_v))
+    wqkv = jnp.concatenate(
+        [
+            wq.reshape(own, n_ctx, width),
+            wk.reshape(own, n_ctx, HEAD),
+            wv.reshape(own, n_ctx, HEAD),
+        ],
+        axis=-1,
+    )
+    own_qkv = wqkv
+    wqkv = lax.all_to_all(
+        wqkv.transpose(1, 0, 2), ctx_axes, split_axis=0, concat_axis=0, tiled=True
+    )
+    wqkv = lax.all_gather(wqkv, "exp", axis=1).reshape(D, width + 2 * HEAD)
+    wo = lax.all_gather(attn_o.astype(bf16), "exp", axis=0, tiled=True)
+    small = jnp.concatenate(
+        [
+            router.astype(bf16),
+            norm_attn.astype(bf16)[:, None],
+            norm_moe.astype(bf16)[:, None],
+            jnp.zeros((own, 128 - experts - 2), bf16),
+        ],
+        axis=1,
+    )
+    small = lax.all_gather(small, all_axes, axis=0, tiled=True)
+    weight_r = small[:, :experts]
+    gain_one_f = small[:, experts].astype(f32)
+    gain_two_f = small[:, experts + 1].astype(f32)
+
+    token_all = lax.all_gather(tokens[0], ctx_axes, axis=0, tiled=True)
+    upstream_blocks = lax.all_gather(cotangent[0], tok_axes, axis=0)
+    route_blocks = lax.all_gather(routes[0], tok_axes, axis=0)
+    perm_row = span_perm[0]
+    first_len = lengths[0, 0]
+    rows = global_rows(perm_row, jnp.arange(group, dtype=jnp.int32))
+    position = rows - jnp.where(rows >= first_len, first_len, 0)
+    freqs = jnp.exp(jnp.arange(HEAD // 2, dtype=f32) * (-2.0 * math.log(10000.0) / HEAD))
+    angle = position.astype(f32)[:, None] * freqs[None, :]
+    cosine, sine = (jnp.cos(angle), jnp.sin(angle))
+    resid_all = token_all.astype(f32)
+    normed_all = resid_all * lax.rsqrt(
+        jnp.mean(resid_all * resid_all, axis=-1, keepdims=True) + EPSILON
+    )
+    hidden_all = (normed_all * gain_one_f).astype(bf16)
+    qkv = jnp.dot(hidden_all, wqkv, preferred_element_type=f32)
+    queries = rotate(
+        qkv[:, :width].reshape(group, repeat, HEAD), cosine[:, None], sine[:, None]
+    ).astype(bf16)
+    keys = rotate(qkv[:, width : width + HEAD], cosine, sine).astype(bf16)
+    values = qkv[:, width + HEAD :].astype(bf16)
+    mask = allowed(rows, rows, first_len)[None]
+    scores = (
+        jnp.einsum("qrd,kd->rqk", queries, keys, preferred_element_type=f32) * softmax_scale
+    )
+    scores = jnp.where(mask, scores, NEGATIVE)
+    highest = jnp.max(scores, axis=-1)
+    weights = jnp.exp(scores - highest[..., None])
+    total = jnp.sum(weights, axis=-1)
+    attended = (
+        jnp.einsum("rqk,kd->rqd", weights.astype(bf16), values, preferred_element_type=f32)
+        / total[..., None]
+    )
+    log_total = highest + jnp.log(total)
+    attended_b = attended.transpose(1, 0, 2).reshape(group, width).astype(bf16)
+    branch = lax.psum_scatter(
+        jnp.dot(attended_b, wo, preferred_element_type=f32).astype(bf16),
+        ctx_axes,
+        scatter_dimension=0,
+        tiled=True,
+    )
+    resid = tokens[0].astype(f32)
+    middle = resid + branch.astype(f32)
+    scale_two = lax.rsqrt(jnp.mean(middle * middle, axis=-1, keepdims=True) + EPSILON)
+    normed_two = middle * scale_two
+    hidden_two = (normed_two * gain_two_f).astype(bf16)
+
+    hidden_blocks = lax.all_gather(hidden_two, tok_axes, axis=0)
+    blocks = hidden_blocks.shape[0]
+    held = 3
+    base = lax.axis_index("exp") * EXP_DEV + (units * z_index) // 2
+    shift = (units * z_index) % 2
+    logits = jnp.einsum("btd,de->bte", hidden_blocks, weight_r, preferred_element_type=f32)
+    picks = route_blocks[..., None] == jnp.arange(experts, dtype=jnp.int32)
+    selected = jnp.sum(jnp.where(picks, logits[:, :, None, :], 0.0), axis=-1)
+    gates_blocks = jax.nn.softmax(selected, axis=-1).astype(bf16).astype(f32)
+    held_ids = base + jnp.arange(held, dtype=jnp.int32)
+    held_picks = route_blocks[..., None] == held_ids
+    gate_held = jnp.sum(jnp.where(held_picks, gates_blocks[..., None], 0.0), axis=2)
+    hit = jnp.any(held_picks, axis=2)
+    lower = jnp.tril(jnp.ones((count, count), bf16))
+    rank = jnp.einsum("ts,bse->bte", lower, hit.astype(bf16), preferred_element_type=f32)
+    pairs = blocks // 2
+    side = jnp.arange(2, dtype=jnp.int32)
+    held_first = lambda a: a.reshape(pairs, 2, count, held).transpose(0, 3, 1, 2)
+    here = (
+        held_first(hit)[:, :, None, None]
+        & (
+            held_first(rank)[:, :, None, None]
+            == (jnp.arange(slots, dtype=f32) + 1.0)[None, None, None, :, None, None]
+        )
+        & (side[:, None] == side[None, :])[None, None, :, None, :, None]
+    )
+    spread = here.astype(bf16).reshape(pairs, held * 2 * slots, 2 * count)
+    slot_gate = jnp.sum(
+        jnp.where(here, held_first(gate_held)[:, :, None, None], 0.0), axis=(-2, -1)
+    )
+    slot_gate = slot_gate.transpose(1, 0, 2, 3).reshape(held, blocks * slots, 1)
+
+    def to_rows(a):
+        rows = jnp.einsum(
+            "prt,ptd->prd", spread, a.reshape(pairs, 2 * count, D), preferred_element_type=f32
+        )
+        return rows.astype(bf16).reshape(pairs, held, 2 * slots, D)
+
+    def to_tokens(rows):
+        a = jnp.einsum(
+            "prt,prd->ptd",
+            spread,
+            rows.reshape(pairs, held * 2 * slots, -1),
+            preferred_element_type=f32,
+        )
+        return a.astype(bf16).reshape(blocks, count, -1)
+
+    meta = jnp.stack([shift, z_index, y_index, base]).astype(jnp.int32)
+    made, back, *grads = run_experts(
+        meta, to_rows(hidden_blocks), to_rows(upstream_blocks), slot_gate, parts
+    )
+    back = lax.psum_scatter(to_tokens(back), tok_axes, scatter_dimension=0, tiled=False)
+    back = back.astype(f32)
+    mixture = lax.psum_scatter(to_tokens(made), tok_axes, scatter_dimension=0, tiled=False)
+    output = (middle + mixture.astype(f32)).astype(bf16)
+    back_rows, dgate_own = back[:, :D], back[:, D : D + experts]
+
+    sums = [None] * 4
+    for s in (3, 2, 1, 0):
+        other = lax.ppermute(grads[4 + s], "y", swap_y)
+        sums[s] = (grads[s].astype(f32) + other.astype(f32)).astype(bf16)
+        if s:
+            sums[s] = lax.ppermute(sums[s], "z", swap_z[s])
+    grad_expert_in, grad_expert_out = place_units(z_index, jnp.concatenate(sums), units)
+    grad_expert_in = grad_expert_in.transpose(1, 0, 2)
+    grad_expert_out = grad_expert_out.transpose(1, 0, 2)
+
+    chosen = routes[0]
+    own_picks = chosen[:, :, None] == jnp.arange(experts, dtype=jnp.int32)[None, None, :]
+    own_logits = jnp.dot(hidden_two, weight_r, preferred_element_type=f32)
+    own_selected = jnp.sum(jnp.where(own_picks, own_logits[:, None, :], 0.0), axis=-1)
+    gates = jax.nn.softmax(own_selected, axis=-1)
+    gate_grad = jnp.sum(jnp.where(own_picks, dgate_own[:, None, :], 0.0), axis=-1)
+    select_grad = gates * (gate_grad - jnp.sum(gates * gate_grad, axis=-1, keepdims=True))
+    logit_grad = jnp.sum(jnp.where(own_picks, select_grad[:, :, None], 0.0), axis=1).astype(bf16)
+    grad_router = contract_rows(hidden_two, logit_grad)
+    grad_norm_two = back_rows + contract_cols(logit_grad, weight_r)
+    grad_gain_two = jnp.sum(grad_norm_two * normed_two, axis=0)
+    small_grads = jnp.concatenate(
+        [grad_router, grad_gain_two[:, None], jnp.zeros((D, 128 - experts - 1), f32)], axis=1
+    )
+    small_grads = lax.psum_scatter(small_grads, all_axes, scatter_dimension=0, tiled=True)
+    upstream = cotangent[0].astype(f32)
+    scaled_two = grad_norm_two * gain_two_f
+    grad_middle = upstream + scale_two * (
+        scaled_two - normed_two * jnp.mean(scaled_two * normed_two, axis=-1, keepdims=True)
+    )
+
+    branch_all = lax.all_gather(grad_middle.astype(bf16), ctx_axes, axis=0, tiled=True)
+    grad_wo = contract_rows(attended_b, branch_all).astype(bf16)
+    grad_wo = lax.psum_scatter(grad_wo, "exp", scatter_dimension=0, tiled=True).astype(f32)
+    grad_heads = contract_cols(branch_all, wo).astype(bf16).reshape(group, repeat, HEAD)
+    grad_heads = grad_heads.transpose(1, 0, 2)
+    drift = jnp.sum(grad_heads.astype(f32) * attended, axis=-1)
+    scores = (
+        jnp.einsum("qrd,kd->rqk", queries, keys, preferred_element_type=f32) * softmax_scale
+    )
+    weights = jnp.where(mask, jnp.exp(scores - log_total[..., None]), 0.0)
+    prob_grad = jnp.einsum("rqd,kd->rqk", grad_heads, values, preferred_element_type=f32)
+    score_grad = (weights * (prob_grad - drift[..., None])).astype(bf16)
+    query_grad = (
+        jnp.einsum("rqk,kd->qrd", score_grad, keys, preferred_element_type=f32) * softmax_scale
+    )
+    value_grad = jnp.einsum(
+        "rqk,rqd->kd", weights.astype(bf16), grad_heads, preferred_element_type=f32
+    )
+    key_grad = (
+        jnp.einsum("rqk,qrd->kd", score_grad, queries, preferred_element_type=f32) * softmax_scale
+    )
+    grad_qkv = jnp.concatenate(
+        [
+            rotate(query_grad, cosine[:, None], -sine[:, None]).reshape(group, width),
+            rotate(key_grad, cosine, -sine),
+            value_grad,
+        ],
+        axis=-1,
+    ).astype(bf16)
+    grad_hidden = lax.psum_scatter(
+        contract_cols(grad_qkv, wqkv).astype(bf16), ctx_axes, scatter_dimension=0, tiled=True
+    ).astype(f32)
+    grad_wqkv = contract_rows(hidden_all, grad_qkv).astype(bf16)
+    grad_wqkv = grad_wqkv.reshape(n_ctx, n_exp, own, width + 2 * HEAD).transpose(1, 0, 2, 3)
+    grad_wqkv = lax.psum_scatter(grad_wqkv, "exp", scatter_dimension=0, tiled=False)
+    grad_wqkv = lax.all_to_all(grad_wqkv, ctx_axes, split_axis=0, concat_axis=0, tiled=True)
+    grad_wqkv = grad_wqkv.astype(f32)
+    grad_q = grad_wqkv[:, :, :width].transpose(1, 0, 2).reshape(own, HEADS * HEAD)
+    grad_k = grad_wqkv[:, :, width : width + HEAD].transpose(1, 0, 2).reshape(own, KV_HEADS * HEAD)
+    grad_v = grad_wqkv[:, :, width + HEAD :].transpose(1, 0, 2).reshape(own, KV_HEADS * HEAD)
+    grad_gain_one = jnp.sum(
+        grad_wqkv.transpose(1, 0, 2) * own_qkv.astype(f32), axis=(1, 2)
+    ) / norm_attn.astype(bf16).astype(f32)
+    scale_one = lax.rsqrt(jnp.mean(resid * resid, axis=-1, keepdims=True) + EPSILON)
+    normed_one = resid * scale_one
+    scaled_one = grad_hidden * gain_one_f
+    grad_tokens = grad_middle + scale_one * (
+        scaled_one - normed_one * jnp.mean(scaled_one * normed_one, axis=-1, keepdims=True)
+    )
+    return (
+        output[None],
+        grad_tokens[None],
+        grad_gain_one,
+        grad_q,
+        grad_k,
+        grad_v,
+        grad_wo,
+        small_grads[:, :experts],
+        small_grads[:, experts],
+        grad_expert_in,
+        grad_expert_out,
+    )
+
+
 def solution(mesh):
-    in_specs = (
-        P("exp", "ctx", None),
-        P("exp", "ctx", None),
-        P("exp", None),
-        P("exp", None),
-        P("exp", "ctx", None),
-        P(("ctx", "exp")),
-        P(("ctx", "exp"), None),
-        P(("ctx", "exp"), None),
-        P(("ctx", "exp"), None),
-        P(("ctx", "exp"), None),
-        P(("ctx", "exp"), None),
-        P(("ctx", "exp")),
-        P("ctx", "exp", None),
-        P("ctx", "exp", None),
-    )
-    out_specs = (
-        P("exp", "ctx", None),
-        P("exp", "ctx", None),
-        P(("ctx", "exp")),
-        P(("ctx", "exp"), None),
-        P(("ctx", "exp"), None),
-        P(("ctx", "exp"), None),
-        P(("ctx", "exp"), None),
-        P(("ctx", "exp"), None),
-        P(("ctx", "exp")),
-        P("ctx", "exp", None),
-        P("ctx", "exp", None),
-    )
-    return jax.shard_map(body, mesh=mesh, in_specs=in_specs, out_specs=out_specs, check_vma=False)
+    ctx, exp = mesh.shape["ctx"], mesh.shape["exp"]
+    if ctx == KV_HEADS and exp * EXP_DEV == 40:
+        inner = jax.sharding.Mesh(mesh.devices.reshape(ctx // 2, 2, exp), ("z", "y", "exp"))
+        body, ctx_name, both = body_heads, ("z", "y"), ("z", "y", "exp")
+    else:
+        inner, body, ctx_name, both = mesh, body_general, "ctx", ("ctx", "exp")
+    token = P("exp", ctx_name, None)
+    group = P("exp", None)
+    expert = P(ctx_name, "exp", None)
+    rows, gain = P(both, None), P(both)
+    in_specs = (token, token, group, group, token, gain) + (rows,) * 5 + (gain, expert, expert)
+    out_specs = (token, token, gain) + (rows,) * 5 + (gain, expert, expert)
+    return jax.shard_map(
+        body, mesh=inner, in_specs=in_specs, out_specs=out_specs, check_vma=False
+    )

time: 2870 us -> 1150 us (0.40)
  waiting for transfers between devices: 2200 us -> 678 us
  local copies, waits for them, and re-layouts: 203 us -> 22.2 us
  matrix products: 184 us -> 78.6 us
  Pallas kernels: 0 us -> 82.1 us
    all_gather x8 -> x4, waiting for transfers between devices: 808 us -> 59.1 us  [the longest x1 59.1 us: body_heads(): lax.all_gather(grad_middle.astype(bf16), ctx_axes, axis=0, tiled=True)]
    unnamed x19 -> x13, waiting for transfers between devices: 737 us -> 3.56 us
    ppermute x0 -> x14, waiting for transfers between devices: none -> 215 us  [the longest x4 115 us: body_heads(): other = lax.ppermute(grads[4 + s], 'y', swap_y)]
    all_to_all x4 -> x2, waiting for transfers between devices: 170 us -> 13.1 us  [the longest x1 13.1 us: body_heads(): lax.all_to_all(grad_wqkv, ctx_axes, split_axis=0, concat_axis=0, tiled=True)]
    all_gather x1 -> x4, blocking collectives: 89.7 us -> 183 us  [the longest x1 119 us: body_heads(): route_blocks = lax.all_gather(routes[0], tok_axes, axis=0)]
    reduce_scatter x5, waiting for transfers between devices: 480 us -> 388 us  [the longest x1 129 us: body_heads(): lax.psum_scatter(to_tokens(back), tok_axes, scatter_dimension=0, tiled=Fa...]
    unnamed x2 -> x0, blocking collectives: 87.9 us -> none
    unnamed x117 -> x135, local copies, waits for them, and re-layouts: 92.2 us -> 8.24 us
  transfers between devices with their start and end apart: 20 -> 27, of which waited for: 18 -> 16; matrix products, arithmetic and copies ran while one was open for 11% -> 8% of each run, Pallas kernels for 0% -> 2%
where the time goes in v1:
time: 1150 us
  waiting for transfers between devices  678 us (59%)
  blocking collectives  183 us (16%)
  Pallas kernels  82.1 us (7%)
  matrix products  78.6 us (7%)
  other arithmetic  53.3 us (5%)
  starting transfers between devices  31.2 us (3%)
  local copies, waits for them, and re-layouts  22.2 us (2%)
  between operations  17 us (1%)
    reduce_scatter x1, waiting for transfers between devices, body_heads(): lax.psum_scatter(to_tokens(back), tok_axes, scatter_dimension=0, tiled=Fa...  129 us
    all_gather x1, blocking collectives, body_heads(): route_blocks = lax.all_gather(routes[0], tok_axes, axis=0)  119 us
    ppermute x4, waiting for transfers between devices, body_heads(): other = lax.ppermute(grads[4 + s], 'y', swap_y)  115 us
    reduce_scatter x1, waiting for transfers between devices, body_heads(): lax.psum_scatter(jnp.dot(attended_b, wo, preferred_element_type=f32).asty...  92.7 us
    reduce_scatter x1, waiting for transfers between devices, body_heads(): lax.psum_scatter(to_tokens(made), tok_axes, scatter_dimension=0, tiled=Fa...  87.5 us
    reduce_scatter x1, waiting for transfers between devices, body_heads(): lax.psum_scatter(contract_cols(grad_qkv, wqkv).astype(bf16), ctx_axes, sc...  76.6 us
    ppermute x4, waiting for transfers between devices, body_heads(): parts = near + [lax.ppermute(a, 'y', swap_y) for a in near]  66.7 us
    all_gather x1, waiting for transfers between devices, body_heads(): lax.all_gather(grad_middle.astype(bf16), ctx_axes, axis=0, tiled=True)  59.1 us
  transfers between devices with their start and end apart: 27, of which 16 were waited for; matrix products, arithmetic and copies ran while one was open for 8% of the time, Pallas kernels for 2%

profile of v1, /device:TPU:0, one launch (start us, length us, event | category | flops | bytes accessed | tf_op | source)
XLA Modules:
  0.0 1146.0 jit_solution(820529453832534922)
XLA Ops:
  13.0 7.3 all-to-all-start
  21.0 45.0 %all_gather.31 = bf16[1536,128]{1,0:T(8,128)(2,1)S(1)} all-gather(bf16[48,128]{1,0:T(8,128)(2,1)S(1)} %maximum_maximum_fusion.1), channel_id=1, replica_groups=mesh['z'=4,'y'=2,'exp'=4] {'z','y','exp'}, dimensions={0}, use_global_device_ids=true | all-gather | bytes 405504 | tf_op jit(solution)/shard_map/all_gather | solution.py:648
  66.6 8.6 all_gather.34
  75.4 2.0 compare_and_fusion
  77.5 11.1 all-gather.1
  88.8 3.0 fusion.8
  95.2 3.1 fusion.4
  98.4 4.4 fusion.5
  102.9 5.5 fusion.43
  109.2 2.7 convolution_convert_fusion.4
  112.5 92.7 %reduce-scatter.10.cloned.1.call-done = bf16[128,1536]{1,0:T(8,128)(2,1)} async-done(((bf16[1024,1536]{1,0:T(8,128)(2,1)}), bf16[128,1536]{1,0:T(8,128)(2,1)}) %reduce-scatter.10.cloned.1.call-update) | async-done | bytes 393232 | tf_op jit(solution)/shard_map/reduce_scatter | solution.py:688
  207.0 1.9 multiply_convert_fusion.1
  209.0 4.5 take_units.5
  214.6 4.5 take_units.6
  220.1 4.5 take_units.7
  224.6 2.3 collective-permute-start.2
  226.9 4.5 take_units.4.refs_4_
  232.6 118.6 %all_gather.35 = s32[16,128,8]{1,2,0:T(8,128)S(1)} all-gather(s32[1,128,8]{1,2,0:T(8,128)S(1)} %copy-done.47), channel_id=1, replica_groups=mesh['z'=4,'y'=2,'exp'=4] {'z','exp'}, dimensions={0}, use_global_device_ids=true | all-gather | bytes 69632 | tf_op jit(solution)/shard_map/all_gather | solution.py:655
  353.0 1.6 and.112
  355.5 1.8 collective-permute-start.4
  357.5 1.8 collective-permute-start.6
  359.3 7.2 convolution_convert_fusion.2
  366.5 4.7 fusion.47
  372.3 6.2 fusion.17
  379.8 7.1 convolution_convert_fusion.3
  386.9 4.0 collective-permute-done.4.refs_9_
  390.9 31.6 %collective-permute-done.5.refs_10_ = bf16[5,192,768]{2,1,0:T(8,128)(2,1)} collective-permute-done((bf16[5,192,768]{2,1,0:T(8,128)(2,1)}, bf16[5,192,768]{2,1,0:T(8,128)(2,1)}, u32[]{:S(2)}, u32[]{:S(2)}) %collective-permute-start.5) | collective-permute-done | bytes 1474592 | tf_op jit(solution)/shard_map/ppermute | solution.py:622
  422.5 31.1 %collective-permute-done.6.refs_11_ = bf16[5,192,768]{2,1,0:T(8,128)(2,1)} collective-permute-done((bf16[5,192,768]{2,1,0:T(8,128)(2,1)}, bf16[5,192,768]{2,1,0:T(8,128)(2,1)}, u32[]{:S(2)}, u32[]{:S(2)}) %collective-permute-start.6) | collective-permute-done | bytes 1474592 | tf_op jit(solution)/shard_map/ppermute | solution.py:622
  453.6 54.8 %experts.1 = (bf16[8,3,80,1536]{3,2,1,0:T(8,128)(2,1)}, bf16[8,3,80,1664]{3,2,1,0:T(8,128)(2,1)}, bf16[5,192,768]{2,1,0:T(8,128)(2,1)}, bf16[5,192,768]{2,1,0:T(...) custom-call(s32[4]{0:T(128)} %pad_add_fusion.refs_0_, ...), custom_call_target="tpu_custom_call" | custom-call | flops 22649241600 | bytes 62914560 | tf_op jit(solution)/shard_map/experts/pallas_call | solution.py:511
  508.4 7.8 convolution_convert_fusion
  517.5 128.6 %reduce-scatter.14.cloned.1.call-done = bf16[1,128,1664]{2,1,0:T(8,128)(2,1)} async-done(((bf16[16,128,1664]{2,1,0:T(8,128)(2,1)}), bf16[1,128,1664]{2,1,0:T(8,128)(2,1)}) %reduce-scatter.14.cloned.1.call-update) | async-done | bytes 426000 | tf_op jit(solution)/shard_map/reduce_scatter | solution.py:751
  649.5 1.8 multiply_reduce_fusion
  652.2 1.8 fusion.105
  654.7 59.1 %all-gather.10.cloned.1.call-done = bf16[1024,1536]{1,0:T(8,128)(2,1)} async-done(((bf16[128,1536]{1,0:T(8,128)(2,1)}), bf16[1024,1536]{1,0:T(8,128)(2,1)}) %all-gather.10.cloned.1.call-update) | async-done | bytes 3145744 | tf_op jit(solution)/shard_map/all_gather | solution.py:788
  713.8 3.2 convolution_convert_fusion.8
  717.2 7.1 multiply_convert_fusion
  725.6 2.0 fusion.19
  727.6 6.2 fusion.23
  739.6 3.6 convolution_convert_fusion.7
  743.3 4.8 convolution_convert_fusion.5
  748.3 7.2 convolution_convert_fusion.1
  759.7 31.4 %collective-permute-done.8 = bf16[5,192,768]{2,1,0:T(8,128)(2,1)S(1)} collective-permute-done((bf16[5,192,768]{2,1,0:T(8,128)(2,1)}, bf16[5,192,768]{2,1,0:T(8,128)(2,1)S(1)}, u32[]{:S(2)}, u32[]{:S(2)}) %collective-permute-start.8) | collective-permute-done | bytes 1474592 | tf_op jit(solution)/shard_map/ppermute | solution.py:759
  791.1 1.5 add_convert_fusion.2
  794.1 28.6 %collective-permute-done.10 = bf16[5,192,768]{2,1,0:T(8,128)(2,1)S(1)} collective-permute-done((bf16[5,192,768]{2,1,0:T(8,128)(2,1)}, bf16[5,192,768]{2,1,0:T(8,128)(2,1)S(1)}, u32[]{:S(2)}, u32[]{:S(2)}) %collective-permute-start.10) | collective-permute-done | bytes 1474592 | tf_op jit(solution)/shard_map/ppermute | solution.py:759
  822.7 1.5 add_convert_fusion.1
  824.2 2.0 collective-permute-start.11
  826.2 29.5 %collective-permute-done.12 = bf16[5,192,768]{2,1,0:T(8,128)(2,1)S(1)} collective-permute-done((bf16[5,192,768]{2,1,0:T(8,128)(2,1)}, bf16[5,192,768]{2,1,0:T(8,128)(2,1)S(1)}, u32[]{:S(2)}, u32[]{:S(2)}) %collective-permute-start.12) | collective-permute-done | bytes 1474592 | tf_op jit(solution)/shard_map/ppermute | solution.py:759
  855.7 1.5 add_convert_fusion
  857.2 1.9 collective-permute-start.13
  859.7 25.7 %collective-permute-done.7 = bf16[5,192,768]{2,1,0:T(8,128)(2,1)} collective-permute-done((bf16[5,192,768]{2,1,0:T(8,128)(2,1)}, bf16[5,192,768]{2,1,0:T(8,128)(2,1)}, u32[]{:S(2)}, u32[]{:S(2)}) %collective-permute-start.7) | collective-permute-done | bytes 1474592 | tf_op jit(solution)/shard_map/ppermute | solution.py:759
  885.4 2.2 add_convert_fusion.3
  887.6 2.4 dynamic-slice_bitcast_fusion
  889.9 4.3 all-to-all-start.1
  894.2 32.8 %collective-permute-done.11 = bf16[5,192,768]{2,1,0:T(8,128)(2,1)} collective-permute-done((bf16[5,192,768]{2,1,0:T(8,128)(2,1)}, bf16[5,192,768]{2,1,0:T(8,128)(2,1)}, u32[]{:S(2)}, u32[]{:S(2)}) %collective-permute-start.11) | collective-permute-done | bytes 1474592 | tf_op jit(solution)/shard_map/ppermute | solution.py:762
  927.0 5.6 pad_maximum_fusion.low_ref.high_ref
  932.6 9.3 place_units.1
  942.6 2.2 reduce-scatter.20.cloned.1.call-done
  947.6 13.1 %all-to-all-done.1 = bf16[8,48,320]{2,1,0:T(8,128)(2,1)S(1)} async-done(((bf16[8,48,320]{2,1,0:T(8,128)(2,1)}), bf16[8,48,320]{2,1,0:T(8,128)(2,1)S(1)}, u32[]{:S(2)}, u32[]{:S(2)}) %all-to-all-start.1) | async-done | bytes 245792 | tf_op jit(solution)/shard_map/all_to_all | solution.py:823
  963.2 1.7 fusion.45
  966.0 2.3 reduce-scatter.18.cloned.1.call-done
  968.4 1.6 convert_element_type.254
  970.0 76.6 %reduce-scatter.16.cloned.1.call-done = bf16[128,1536]{1,0:T(8,128)(2,1)} async-done(((bf16[1024,1536]{1,0:T(8,128)(2,1)}), bf16[128,1536]{1,0:T(8,128)(2,1)}) %reduce-scatter.16.cloned.1.call-update) | async-done | bytes 393232 | tf_op jit(solution)/shard_map/reduce_scatter | solution.py:817
  1047.9 87.5 %reduce-scatter.12.cloned.1.call-done = bf16[1,128,1536]{2,1,0:T(8,128)(2,1)} async-done(((bf16[16,128,1536]{2,1,0:T(8,128)(2,1)}), bf16[1,128,1536]{2,1,0:T(8,128)(2,1)}) %reduce-scatter.12.cloned.1.call-update) | async-done | bytes 393232 | tf_op jit(solution)/shard_map/reduce_scatter | solution.py:753
  1135.4 2.7 fusion.40
  (261 shorter events, 49.7 us)
Async XLA Ops:
  8.0 12.4 %copy-start.48 = (f32[48,40]{0,1:T(8,128)S(1)}, f32[48,40]{0,1:T(8,128)}, u32[]{:S(2)}) copy-start(f32[48,40]{0,1:T(8,128)} %param.24) | copy-start | bytes 23044
  8.0 12.5 %copy-start.60 = (f32[48]{0:T(128)S(1)}, f32[48]{0:T(128)}, u32[]{:S(2)}) copy-start(f32[48]{0:T(128)} %param.19) | copy-start | bytes 580
  8.0 12.6 %copy-start.59 = (f32[48]{0:T(128)S(1)}, f32[48]{0:T(128)}, u32[]{:S(2)}) copy-start(f32[48]{0:T(128)} %param.25) | copy-start | bytes 580
  8.0 12.7 %copy-start.35 = (f32[48,1536]{1,0:T(8,128)S(1)}, f32[48,1536]{1,0:T(8,128)}, u32[]{:S(2)}) copy-start(f32[48,1536]{1,0:T(8,128)} %param.23) | copy-start | bytes 884740
  8.1 12.8 %copy-start.58 = (s32[1,16]{1,0:T(1,128)S(1)}, s32[1,16]{1,0:T(1,128)}, u32[]{:S(2)}) copy-start(s32[1,16]{1,0:T(1,128)} %param.17) | copy-start | bytes 196
  8.1 67.2 %copy-start.54 = (s32[1,2]{1,0:T(1,128)S(1)}, s32[1,2]{1,0:T(1,128)}, u32[]{:S(2)}) copy-start(s32[1,2]{1,0:T(1,128)} %param.16) | copy-start | bytes 28
  8.1 80.7 %all-gather.12.cloned.1.call-start = ((), (), s32[]{:S(2)}) async-start(), calls=%async_computation.15 | async-start | bytes 3538944 | tf_op jit(solution)/shard_map/all_gather | solution.py:653
  10.0 11.0 copy-start.17
  11.1 9.9 copy-start.25
  12.2 8.8 copy-start.27
  13.0 64.4 %all-to-all-start = ((bf16[8,48,320]{2,1,0:T(8,128)(2,1)}), bf16[8,48,320]{2,1,0:T(8,128)(2,1)S(1)}, u32[]{:S(2)}, u32[]{:S(2)}) async-start(bf16[8,48,320]{2,1,0:T(8,128)(2,1)} %copy.152), calls=%async_computation | async-start | bytes 589824 | tf_op jit(solution)/shard_map/all_to_all | solution.py:634
  20.3 184.9 %reduce-scatter.10.cloned.1.call-start = ((), (), s32[]{:S(2)}) async-start(), calls=%async_computation.8 | async-start | bytes 3538944 | tf_op jit(solution)/shard_map/reduce_scatter | solution.py:688
  66.1 22.6 %copy-start.2 = (bf16[1536,128]{1,0:T(8,128)(2,1)}, bf16[1536,128]{1,0:T(8,128)(2,1)S(1)}, u32[]{:S(2)}) copy-start(bf16[1536,128]{1,0:T(8,128)(2,1)S(1)} %all_gather.31) | copy-start | bytes 1179652
  75.4 18.2 %copy-start.45 = (f32[1024]{0:T(1024)}, f32[1024]{0:T(1024)S(1)}, u32[]{:S(2)}) copy-start(f32[1024]{0:T(1024)S(1)} %get-tuple-element.60) | copy-start | bytes 12292
  75.4 18.2 %copy-start.55 = (f32[32]{0:T(128)}, f32[32]{0:T(128)S(1)}, u32[]{:S(2)}) copy-start(f32[32]{0:T(128)S(1)} %multiply_exponential_fusion) | copy-start | bytes 388
  102.9 6.2 copy-start.16
  111.9 93.3 %copy-start = (bf16[1,128,1536]{2,1,0:T(8,128)(2,1)S(1)}, bf16[1,128,1536]{2,1,0:T(8,128)(2,1)}, u32[]{:S(2)}) copy-start(bf16[1,128,1536]{2,1,0:T(8,128)(2,1)} %param.14) | copy-start | bytes 1179652
  111.9 247.4 %all-gather.8.cloned.1.call-start = ((), (), s32[]{:S(2)}) async-start(), calls=%async_computation.9 | async-start | bytes 6684672 | tf_op jit(solution)/shard_map/all_gather | solution.py:654
  112.5 254.1 %all-gather.14.cloned.1.call-start = ((), (), s32[]{:S(2)}) async-start(), calls=%async_computation.16 | async-start | bytes 6684672 | tf_op jit(solution)/shard_map/all_gather | solution.py:700
  208.9 437.2 %reduce-scatter.14.cloned.1.call-start = ((), (), s32[]{:S(2)}) async-start(), calls=%async_computation.11 | async-start | bytes 7241728 | tf_op jit(solution)/shard_map/reduce_scatter | solution.py:751
  213.5 142.0 %collective-permute-start = (bf16[5,192,768]{2,1,0:T(8,128)(2,1)}, bf16[5,192,768]{2,1,0:T(8,128)(2,1)}, u32[]{:S(2)}, u32[]{:S(2)}) collective-permute-start(bf16[5,192,768]{2,1,0:T(8,128)(2,1)} %take_units.5), channel_id=1, source_target_pairs={{0,8},{8,0},{16,24},{24,16},{1,9},{9,1},{17,25},{25,17},{2,10},{10... | collective-permute-start | bytes 4423688 | tf_op jit(solution)/shard_map/ppermute | solution.py:621
  219.1 138.2 %collective-permute-start.1 = (bf16[5,192,768]{2,1,0:T(8,128)(2,1)}, bf16[5,192,768]{2,1,0:T(8,128)(2,1)}, u32[]{:S(2)}, u32[]{:S(2)}) collective-permute-start(bf16[5,192,768]{2,1,0:T(8,128)(2,1)} %take_units.6), channel_id=1, source_target_pairs={{0,16},{8,24},{16,0},{24,8},{1,17},{9,25},{17,1},{25,9},{2,18},{10... | collective-permute-start | bytes 4423688 | tf_op jit(solution)/shard_map/ppermute | solution.py:621
  224.6 132.9 %collective-permute-start.2 = (bf16[5,192,768]{2,1,0:T(8,128)(2,1)}, bf16[5,192,768]{2,1,0:T(8,128)(2,1)}, u32[]{:S(2)}, u32[]{:S(2)}) collective-permute-start(bf16[5,192,768]{2,1,0:T(8,128)(2,1)} %take_units.7), channel_id=1, source_target_pairs={{0,24},{8,16},{16,8},{24,0},{1,25},{9,17},{17,9},{25,1},{2,26},{10... | collective-permute-start | bytes 4423688 | tf_op jit(solution)/shard_map/ppermute | solution.py:621
  226.8 5.8 copy-start.47
  231.3 155.5 %collective-permute-start.3 = (bf16[5,192,768]{2,1,0:T(8,128)(2,1)}, bf16[5,192,768]{2,1,0:T(8,128)(2,1)}, u32[]{:S(2)}, u32[]{:S(2)}) collective-permute-start(bf16[5,192,768]{2,1,0:T(8,128)(2,1)} %take_units.4.refs_4_), channel_id=1, source_target_pairs={{0,4},{4,0},{1,5},{5,1},{2,6},{6,2},{3,7},{7,3},{8,12},{12,8},{9,1... | collective-permute-start | bytes 4423688 | tf_op jit(solution)/shard_map/ppermute | solution.py:622
  355.5 35.4 %collective-permute-start.4 = (bf16[5,192,768]{2,1,0:T(8,128)(2,1)}, bf16[5,192,768]{2,1,0:T(8,128)(2,1)}, u32[]{:S(2)}, u32[]{:S(2)}) collective-permute-start(bf16[5,192,768]{2,1,0:T(8,128)(2,1)} %collective-permute-done.refs_5_), channel_id=1, source_target_pairs={{0,4},{4,0},{1,5},{5,1},{2,6},{6,2},{3,7},{7,3},{8,12},{12,8},{9,1... | collective-permute-start | bytes 4423688 | tf_op jit(solution)/shard_map/ppermute | solution.py:622
  357.3 65.2 %collective-permute-start.5 = (bf16[5,192,768]{2,1,0:T(8,128)(2,1)}, bf16[5,192,768]{2,1,0:T(8,128)(2,1)}, u32[]{:S(2)}, u32[]{:S(2)}) collective-permute-start(bf16[5,192,768]{2,1,0:T(8,128)(2,1)} %collective-permute-done.1.refs_6_), channel_id=1, source_target_pairs={{0,4},{4,0},{1,5},{5,1},{2,6},{6,2},{3,7},{7,3},{8,12},{12,8},{9,1... | collective-permute-start | bytes 4423688 | tf_op jit(solution)/shard_map/ppermute | solution.py:622
  357.5 96.1 %collective-permute-start.6 = (bf16[5,192,768]{2,1,0:T(8,128)(2,1)}, bf16[5,192,768]{2,1,0:T(8,128)(2,1)}, u32[]{:S(2)}, u32[]{:S(2)}) collective-permute-start(bf16[5,192,768]{2,1,0:T(8,128)(2,1)} %collective-permute-done.2.refs_7_), channel_id=1, source_target_pairs={{0,4},{4,0},{1,5},{5,1},{2,6},{6,2},{3,7},{7,3},{8,12},{12,8},{9,1... | collective-permute-start | bytes 4423688 | tf_op jit(solution)/shard_map/ppermute | solution.py:622
  359.3 7.2 copy-start.3
  516.2 133.2 %copy-start.5 = (bf16[128,1536]{1,0:T(8,128)(2,1)S(1)}, bf16[128,1536]{1,0:T(8,128)(2,1)}, u32[]{:S(2)}) copy-start(bf16[128,1536]{1,0:T(8,128)(2,1)} %reduce-scatter.10.cloned.1.call-done) | copy-start | bytes 1179652
  516.2 135.9 %copy-start.8 = (bf16[1,128,1536]{2,1,0:T(8,128)(2,1)S(1)}, bf16[1,128,1536]{2,1,0:T(8,128)(2,1)}, u32[]{:S(2)}) copy-start(bf16[1,128,1536]{2,1,0:T(8,128)(2,1)} %param.15) | copy-start | bytes 1179652
  516.3 197.5 %all-gather.10.cloned.1.call-start = ((), (), s32[]{:S(2)}) async-start(), calls=%async_computation.12 | async-start | bytes 3538944 | tf_op jit(solution)/shard_map/all_gather | solution.py:788
  647.8 6.8 copy-start.38
  649.5 67.6 %copy-start.43 = (bf16[128,40]{0,1:T(8,128)(2,1)}, bf16[128,40]{0,1:T(8,128)(2,1)S(1)}, u32[]{:S(2)}) copy-start(bf16[128,40]{0,1:T(8,128)(2,1)S(1)} %select_reduce_fusion.1) | copy-start | bytes 30724
  654.0 233.6 %all-reduce.3.cloned.1.call-start = ((), (), s32[]{:S(2)}) async-start(), calls=%async_computation.18 | async-start | bytes 2359296
  654.6 62.6 %copy-start.7 = (pred[1024,1024]{0,1:T(8,128)(4,1)S(1)}, pred[1024,1024]{0,1:T(8,128)(4,1)}, u32[]{:S(2)}) copy-start(pred[1024,1024]{0,1:T(8,128)(4,1)} %compare_and_fusion) | copy-start | bytes 3145732
  717.2 7.1 copy-start.37
  727.6 6.3 copy-start.46
  727.6 6.3 copy-start.56
  727.6 6.9 copy-start.24
  727.6 6.9 copy-start.34
  727.6 7.5 copy-start.11
  727.6 7.5 copy-start.52
  738.0 206.8 %reduce-scatter.20.cloned.1.call-start = ((), (), s32[]{:S(2)}) async-start(), calls=%async_computation.17 | async-start | bytes 811008
  739.5 228.8 %reduce-scatter.18.cloned.1.call-start = ((), (), s32[]{:S(2)}) async-start(), calls=%async_computation.14 | async-start | bytes 737280 | tf_op jit(solution)/shard_map/reduce_scatter | solution.py:790
  743.2 303.4 %reduce-scatter.16.cloned.1.call-start = ((), (), s32[]{:S(2)}) async-start(), calls=%async_computation.13 | async-start | bytes 3538944 | tf_op jit(solution)/shard_map/reduce_scatter | solution.py:817
  748.1 387.4 %reduce-scatter.12.cloned.1.call-start = ((), (), s32[]{:S(2)}) async-start(), calls=%async_computation.10 | async-start | bytes 6684672 | tf_op jit(solution)/shard_map/reduce_scatter | solution.py:753
  755.5 35.5 %copy-start.21 = (bf16[5,192,768]{2,1,0:T(8,128)(2,1)S(1)}, bf16[5,192,768]{2,1,0:T(8,128)(2,1)}, u32[]{:S(2)}) copy-start(bf16[5,192,768]{2,1,0:T(8,128)(2,1)} %get-tuple-element.27) | copy-start | bytes 4423684
  755.6 67.1 %copy-start.20 = (bf16[5,192,768]{2,1,0:T(8,128)(2,1)S(1)}, bf16[5,192,768]{2,1,0:T(8,128)(2,1)}, u32[]{:S(2)}) copy-start(bf16[5,192,768]{2,1,0:T(8,128)(2,1)} %get-tuple-element.29) | copy-start | bytes 4423684
  755.6 35.5 %collective-permute-start.8 = (bf16[5,192,768]{2,1,0:T(8,128)(2,1)}, bf16[5,192,768]{2,1,0:T(8,128)(2,1)S(1)}, u32[]{:S(2)}, u32[]{:S(2)}) collective-permute-start(bf16[5,192,768]{2,1,0:T(8,128)(2,1)} %get-tuple-element.28), channel_id=1, source_target_pairs={{0,4},{4,0},{1,5},{5,1},{2,6},{6,2},{3,7},{7,3},{8,12},{12,8},{9,1... | collective-permute-start | bytes 4423688 | tf_op jit(solution)/shard_map/ppermute | solution.py:759
  756.2 66.5 %collective-permute-start.10 = (bf16[5,192,768]{2,1,0:T(8,128)(2,1)}, bf16[5,192,768]{2,1,0:T(8,128)(2,1)S(1)}, u32[]{:S(2)}, u32[]{:S(2)}) collective-permute-start(bf16[5,192,768]{2,1,0:T(8,128)(2,1)} %get-tuple-element.30), channel_id=1, source_target_pairs={{0,4},{4,0},{1,5},{5,1},{2,6},{6,2},{3,7},{7,3},{8,12},{12,8},{9,1... | collective-permute-start | bytes 4423688 | tf_op jit(solution)/shard_map/ppermute | solution.py:759
  757.7 98.0 %collective-permute-start.12 = (bf16[5,192,768]{2,1,0:T(8,128)(2,1)}, bf16[5,192,768]{2,1,0:T(8,128)(2,1)S(1)}, u32[]{:S(2)}, u32[]{:S(2)}) collective-permute-start(bf16[5,192,768]{2,1,0:T(8,128)(2,1)} %get-tuple-element.32), channel_id=1, source_target_pairs={{0,4},{4,0},{1,5},{5,1},{2,6},{6,2},{3,7},{7,3},{8,12},{12,8},{9,1... | collective-permute-start | bytes 4423688 | tf_op jit(solution)/shard_map/ppermute | solution.py:759
  758.2 127.1 %collective-permute-start.7 = (bf16[5,192,768]{2,1,0:T(8,128)(2,1)}, bf16[5,192,768]{2,1,0:T(8,128)(2,1)}, u32[]{:S(2)}, u32[]{:S(2)}) collective-permute-start(bf16[5,192,768]{2,1,0:T(8,128)(2,1)} %get-tuple-element.26), channel_id=1, source_target_pairs={{0,4},{4,0},{1,5},{5,1},{2,6},{6,2},{3,7},{7,3},{8,12},{12,8},{9,1... | collective-permute-start | bytes 4423688 | tf_op jit(solution)/shard_map/ppermute | solution.py:759
  792.6 63.1 %copy-start.19 = (bf16[5,192,768]{2,1,0:T(8,128)(2,1)S(1)}, bf16[5,192,768]{2,1,0:T(8,128)(2,1)}, u32[]{:S(2)}) copy-start(bf16[5,192,768]{2,1,0:T(8,128)(2,1)} %get-tuple-element.31) | copy-start | bytes 4423684
  792.6 101.6 %collective-permute-start.9 = (bf16[5,192,768]{2,1,0:T(8,128)(2,1)}, bf16[5,192,768]{2,1,0:T(8,128)(2,1)}, u32[]{:S(2)}, u32[]{:S(2)}) collective-permute-start(bf16[5,192,768]{2,1,0:T(8,128)(2,1)} %add_convert_fusion.2), channel_id=1, source_target_pairs={{0,8},{8,0},{16,24},{24,16},{1,9},{9,1},{17,25},{25,17},{2,10},{10... | collective-permute-start | bytes 4423688 | tf_op jit(solution)/shard_map/ppermute | solution.py:762
  824.2 34.9 %copy-start.61 = (u32[32]{0:T(128)S(1)}, u32[32]{0:T(128)}, u32[]{:S(2)}) copy-start(u32[32]{0:T(128)} %constant.128) | copy-start | bytes 388
  824.2 102.8 %collective-permute-start.11 = (bf16[5,192,768]{2,1,0:T(8,128)(2,1)}, bf16[5,192,768]{2,1,0:T(8,128)(2,1)}, u32[]{:S(2)}, u32[]{:S(2)}) collective-permute-start(bf16[5,192,768]{2,1,0:T(8,128)(2,1)} %add_convert_fusion.1), channel_id=1, source_target_pairs={{0,16},{8,24},{16,0},{24,8},{1,17},{9,25},{17,1},{25,9},{2,18},{10... | collective-permute-start | bytes 4423688 | tf_op jit(solution)/shard_map/ppermute | solution.py:762
  857.2 69.8 %collective-permute-start.13 = (bf16[5,192,768]{2,1,0:T(8,128)(2,1)}, bf16[5,192,768]{2,1,0:T(8,128)(2,1)}, u32[]{:S(2)}, u32[]{:S(2)}) collective-permute-start(bf16[5,192,768]{2,1,0:T(8,128)(2,1)} %add_convert_fusion), channel_id=1, source_target_pairs={{0,24},{8,16},{16,8},{24,0},{1,25},{9,17},{17,9},{25,1},{2,26},{10... | collective-permute-start | bytes 4423688 | tf_op jit(solution)/shard_map/ppermute | solution.py:762
  889.9 70.7 %all-to-all-start.1 = ((bf16[8,48,320]{2,1,0:T(8,128)(2,1)}), bf16[8,48,320]{2,1,0:T(8,128)(2,1)S(1)}, u32[]{:S(2)}, u32[]{:S(2)}) async-start(bf16[8,48,320]{2,1,0:T(8,128)(2,1)} %dynamic-slice_bitcast_fusion), calls=%async_computation.5 | async-start | bytes 589824 | tf_op jit(solution)/shard_map/all_to_all | solution.py:823
  932.6 9.3 copy-start.62
  941.9 21.3 %copy-start.18 = (bf16[48,8,192]{2,1,0:T(8,128)(2,1)S(1)}, bf16[48,8,192]{2,1,0:T(8,128)(2,1)}, u32[]{:S(2)}) copy-start(bf16[48,8,192]{2,1,0:T(8,128)(2,1)} %copy-done.17) | copy-start | bytes 442372
  941.9 21.3 %copy-start.26 = (bf16[48,8,64]{2,1,0:T(8,128)(2,1)S(1)}, bf16[48,8,64]{2,1,0:T(8,128)(2,1)}, u32[]{:S(2)}) copy-start(bf16[48,8,64]{2,1,0:T(8,128)(2,1)} %copy-done.25) | copy-start | bytes 147460
  941.9 193.5 %copy-start.9 = (bf16[1,128,1536]{2,1,0:T(8,128)(2,1)S(1)}, bf16[1,128,1536]{2,1,0:T(8,128)(2,1)}, u32[]{:S(2)}) copy-start(bf16[1,128,1536]{2,1,0:T(8,128)(2,1)} %param.15) | copy-start | bytes 1179652
  941.9 193.5 %copy-start.13 = (f32[128,1536]{1,0:T(8,128)S(1)}, f32[128,1536]{1,0:T(8,128)}, u32[]{:S(2)}) copy-start(f32[128,1536]{1,0:T(8,128)} %copy-done.12) | copy-start | bytes 2359300
  (28 other events, 62.8 us)
Sparse Core Ops, SparseCore 0:
  11.1 69.2 all-gather.11
  112.0 93.1 reduce-scatter.9
  654.1 59.6 all-gather.9
  738.1 35.8 all-reduce.2
  780.3 164.3 reduce-scatter.19
  947.3 21.0 reduce-scatter.17
  972.4 74.2 reduce-scatter.15
  1051.1 84.2 reduce-scatter.11
Sparse Core Ops, SparseCore 1:
  114.7 69.6 all-gather.7
  209.0 155.0 all-gather.13
  516.3 129.7 reduce-scatter.13

commit v2 on v1

--- a/solution.py
+++ b/solution.py
@@ -426,6 +426,80 @@
     )(first.reshape(1), win, win, wout)
 
 
+def dispatch_kernel(base, hid_ref, mark_ref, router_ref, rows_ref, up_ref, gate_ref, spread_ref, gates_ref):
+    bf16, f32 = jnp.bfloat16, jnp.float32
+    count = hid_ref.shape[1]
+    _, held, rows, _ = rows_ref.shape
+    slots = rows // 2
+    both = 2 * count
+    x = hid_ref[...].reshape(both, D)
+    logits = jnp.dot(x, router_ref[...], preferred_element_type=f32)
+    routes = mark_ref[:, :, D:].reshape(both, 128).astype(f32)
+    lane = lax.broadcasted_iota(jnp.int32, (both, 128), 1).astype(f32)
+    picks = jnp.zeros((both, 128), f32)
+    for i in range(TOP):
+        picks = jnp.where(routes[:, i : i + 1] == lane, 1.0, picks)
+    masked = jnp.where(picks > 0.0, logits, NEGATIVE)
+    top = jnp.max(masked, axis=-1, keepdims=True)
+    gates = jnp.where(picks > 0.0, jnp.exp(masked - top), 0.0)
+    gates = gates / jnp.sum(gates, axis=-1, keepdims=True)
+    gates_ref[...] = gates.reshape(2, count, 128)
+    which = lax.broadcasted_iota(jnp.int32, (8, 128), 0)
+    columns = lax.broadcasted_iota(jnp.int32, (8, 128), 1)
+    chosen = jnp.where(columns == which + base[0], 1.0, 0.0).astype(bf16)
+    hit = contract_cols(chosen, picks.astype(bf16))
+    gate = contract_cols(chosen, gates.astype(bf16))
+    earlier = lax.broadcasted_iota(jnp.int32, (both, both), 0)
+    later = lax.broadcasted_iota(jnp.int32, (both, both), 1)
+    upto = jnp.where((earlier <= later) & (earlier // count == later // count), 1.0, 0.0)
+    rank = jnp.dot(hit.astype(bf16), upto.astype(bf16), preferred_element_type=f32)
+    row = lax.broadcasted_iota(jnp.int32, (rows, both), 0)
+    token = lax.broadcasted_iota(jnp.int32, (rows, both), 1)
+    side = row // slots
+    wanted = jnp.where(side == token // count, row - side * slots + 1, -1).astype(f32)
+    for e in range(held):
+        here = jnp.where((rank[e : e + 1] == wanted) & (hit[e : e + 1] > 0.0), 1.0, 0.0)
+        gate_ref[0, e] = jnp.sum(here * gate[e : e + 1], axis=-1, keepdims=True)
+        here = here.astype(bf16)
+        spread_ref[0, e * rows : (e + 1) * rows, :] = here
+        rows_ref[0, e] = jnp.dot(here, x, preferred_element_type=f32).astype(bf16)
+        up_ref[0, e] = jnp.dot(
+            here, mark_ref[:, :, :D].reshape(both, D), preferred_element_type=f32
+        ).astype(bf16)
+
+
+def dispatch(base, hidden, marked, router, held, slots):
+    blocks, count, _ = hidden.shape
+    pairs = blocks // 2
+    bf16, f32 = jnp.bfloat16, jnp.float32
+    pair = lambda *shape: pl.BlockSpec((1,) + shape, lambda p, b: (p,) + (0,) * len(shape))
+    two = lambda width: pl.BlockSpec((2, count, width), lambda p, b: (p, 0, 0))
+    return pl.pallas_call(
+        dispatch_kernel,
+        grid_spec=pltpu.PrefetchScalarGridSpec(
+            num_scalar_prefetch=1,
+            grid=(pairs,),
+            in_specs=[two(D), two(D + 128), pl.BlockSpec((D, 128), lambda p, b: (0, 0))],
+            out_specs=[
+                pair(held, 2 * slots, D),
+                pair(held, 2 * slots, D),
+                pair(held, 2 * slots, 1),
+                pair(held * 2 * slots, 2 * count),
+                two(128),
+            ],
+        ),
+        out_shape=[
+            jax.ShapeDtypeStruct((pairs, held, 2 * slots, D), bf16),
+            jax.ShapeDtypeStruct((pairs, held, 2 * slots, D), bf16),
+            jax.ShapeDtypeStruct((pairs, held, 2 * slots, 1), f32),
+            jax.ShapeDtypeStruct((pairs, held * 2 * slots, 2 * count), bf16),
+            jax.ShapeDtypeStruct((blocks, count, 128), f32),
+        ],
+        compiler_params=pltpu.CompilerParams(vmem_limit_bytes=48 * 2**20),
+        name="dispatch",
+    )(base.reshape(1).astype(jnp.int32), hidden, marked, router)
+
+
 def expert_kernel(depth, meta, x_ref, g_ref, gate_ref, *refs):
     parts, (y_ref, d_ref), outs = refs[:8], refs[8:10], refs[10:18]
     weight, du_ref, act_ref = refs[18:]
@@ -437,7 +511,7 @@
         pl.multiple_of(((z ^ (i % 4)) * 2 + (y ^ (i // 4))) * depth, 64) for i in range(8)
     ]
     for part, offset in zip(parts, offsets):
-        weight[pl.ds(offset, depth), :] = part[0]
+        weight[pl.ds(offset, depth), :] = part[0] if len(part.shape) == 3 else part[0, 0]
     expert = base + (j + shift) // 2
     first = jnp.logical_or(j == 0, lax.rem(j + shift, 2) == 0)
     keep = jnp.where(first, 0.0, 1.0)
@@ -449,7 +523,7 @@
         flat = pl.ds(pl.multiple_of(i * step * rows, 32), step * rows)
         x = x_ref[at, 0].reshape(step * rows, D)
         g = g_ref[at, 0].reshape(step * rows, D)
-        gate = gate_ref[0, flat, :]
+        gate = gate_ref[at, 0].reshape(step * rows, 1)
         u = jnp.dot(x, weight[:, : 2 * half], preferred_element_type=f32)
         raw = jnp.dot(g, weight[:, 2 * half :], preferred_element_type=f32)
         u1, u2 = u[:, :half], u[:, half:]
@@ -499,13 +573,17 @@
         out[0] = weight[pl.ds(offset, depth), :]
 
 
-def run_experts(meta, row_in, row_up, slot_gate, parts):
+def run_experts(meta, row_in, row_up, slot_gate, own_part, near_parts, far_parts):
     pairs, held, rows, _ = row_in.shape
-    units, depth, columns = parts[0].shape
+    units, depth, columns = own_part.shape
     held_block = lambda width: pl.BlockSpec(
         (pairs, 1, rows, width), lambda j, m: (0, (j + m[0]) // 2, 0, 0)
     )
     unit_block = pl.BlockSpec((1, depth, columns), lambda j, m: (j, 0, 0))
+
+    def part_block(i):
+        return pl.BlockSpec((1, 1, depth, columns), lambda j, m: (i, j, 0, 0))
+
     bf16 = jnp.bfloat16
     total = units * pairs * rows * D * columns * 6
     return pl.pallas_call(
@@ -516,9 +594,10 @@
             in_specs=[
                 held_block(D),
                 held_block(D),
-                pl.BlockSpec((1, pairs * rows, 1), lambda j, m: ((j + m[0]) // 2, 0, 0)),
+                held_block(1),
+                unit_block,
             ]
-            + [unit_block] * 8,
+            + [part_block(i) for i in (0, 1, 2, 0, 1, 2, 3)],
             out_specs=[held_block(D), held_block(D + 128)] + [unit_block] * 8,
             scratch_shapes=[
                 pltpu.VMEM((D, columns), bf16),
@@ -536,7 +615,7 @@
             flops=total, bytes_accessed=60 * 2**20, transcendentals=units * pairs * rows * HID
         ),
         name="experts",
-    )(meta, row_in, row_up, slot_gate, *parts)
+    )(meta, row_in, row_up, slot_gate, own_part, *[near_parts] * 3, *[far_parts] * 4)
 
 
 def spread_kernel(z_ref, low_ref, high_ref, in_ref, out_ref):
@@ -577,6 +656,574 @@
     )(z_index.reshape(1), units, units)
 
 
+MESH = pl.DeviceIdType.MESH
+
+
+def greet(peers):
+    barrier = pltpu.get_barrier_semaphore()
+    for peer in peers:
+        pl.semaphore_signal(barrier, inc=1, device_id=peer, device_id_type=MESH)
+    pl.semaphore_wait(barrier, len(peers))
+
+
+def send(src, dst, sems, at, peer):
+    copy = pltpu.make_async_remote_copy(
+        src_ref=src,
+        dst_ref=dst,
+        send_sem=sems[0].at[at],
+        recv_sem=sems[1].at[at],
+        device_id=peer,
+        device_id_type=MESH,
+    )
+    copy.start()
+    return copy
+
+
+def dma_pair(number):
+    return [pltpu.SemaphoreType.DMA((number,)), pltpu.SemaphoreType.DMA((number,))]
+
+
+def z_peers():
+    z = lax.axis_index("z")
+    return [{"z": z ^ s} for s in (3, 2, 1)]
+
+
+def siblings(axes):
+    return [{a: 1 - lax.axis_index(a)} for a in axes]
+
+
+class Scatter:
+    def __init__(self, part, axes, chunks, refs):
+        self.part, self.axes, self.chunks = part, axes, chunks
+        depth = len(axes)
+        self.own, self.came = refs[0], refs[1 : 1 + depth]
+        self.sums, self.far = refs[1 + depth : 1 + 2 * depth], refs[1 + 2 * depth]
+        self.load_sem = refs[2 + 2 * depth]
+        sems = refs[3 + 2 * depth :]
+        self.sems = [sems[2 * i : 2 * i + 2] for i in range(depth + 1)]
+        self.z = lax.axis_index("z")
+        self.mine = [lax.axis_index(a) for a in axes]
+        self.rows = part.shape[-2] // chunks
+        self.flying = [[None] * chunks for _ in axes]
+        self.over_z = [None] * chunks
+
+    @staticmethod
+    def scratch(part, axes, chunks):
+        n_z, rows, width, kind = part.shape[0], part.shape[-2], part.shape[-1], part.dtype
+        depth = len(axes)
+
+        def buffer(i):
+            return pltpu.VMEM((chunks, n_z) + (2,) * i + (rows // chunks, width), kind)
+
+        shapes = [buffer(depth - 1)] + [buffer(i) for i in range(depth)] * 2
+        shapes += [pltpu.VMEM((chunks, n_z - 1, rows // chunks, width), kind)]
+        shapes += [pltpu.SemaphoreType.DMA((chunks,))]
+        for _ in range(depth):
+            shapes += dma_pair(chunks)
+        return shapes + dma_pair(chunks * (n_z - 1))
+
+    def start(self):
+        level = len(self.axes) - 1
+        lead = (slice(None),) * len(self.axes)
+        mine = self.mine[-1]
+        self.loads = []
+        for c in range(self.chunks):
+            at = pl.ds(c * self.rows, self.rows)
+            self.flying[level][c] = send(
+                self.part.at[lead + (1 - mine, at)],
+                self.came[level].at[c],
+                self.sems[level],
+                c,
+                {self.axes[-1]: 1 - mine},
+            )
+            load = pltpu.make_async_copy(
+                self.part.at[lead + (mine, at)], self.own.at[c], self.load_sem.at[c]
+            )
+            load.start()
+            self.loads.append(load)
+
+    def fold(self, level, c):
+        self.flying[level][c].wait_recv()
+        if level == len(self.axes) - 1:
+            self.loads[c].wait()
+            held = self.own[c]
+        else:
+            held = self.sums[level + 1][
+                (c,) + (slice(None),) * (level + 1) + (self.mine[level],)
+            ]
+        total = held.astype(jnp.float32) + self.came[level][c].astype(jnp.float32)
+        self.sums[level][c] = total.astype(held.dtype)
+        if level > 0:
+            mine = self.mine[level - 1]
+            self.flying[level - 1][c] = send(
+                self.sums[level].at[(c,) + (slice(None),) * level + (1 - mine,)],
+                self.came[level - 1].at[c],
+                self.sems[level - 1],
+                c,
+                {self.axes[level - 1]: 1 - mine},
+            )
+        else:
+            self.over_z[c] = [
+                send(
+                    self.sums[0].at[c, self.z ^ s],
+                    self.far.at[c, s - 1],
+                    self.sems[-1],
+                    c * 3 + s - 1,
+                    {"z": self.z ^ s},
+                )
+                for s in (3, 2, 1)
+            ]
+
+    def total(self, c):
+        for copy in self.over_z[c]:
+            copy.wait_recv()
+        total = self.sums[0][c, self.z].astype(jnp.float32)
+        for s in range(3):
+            total = total + self.far[c, s].astype(jnp.float32)
+        return total
+
+    def run(self, use):
+        depth = len(self.axes)
+        for step in range(self.chunks + depth):
+            for level in range(depth - 1, -1, -1):
+                c = step - (depth - 1 - level)
+                if 0 <= c < self.chunks:
+                    self.fold(level, c)
+            c = step - depth
+            if 0 <= c < self.chunks:
+                use(c, pl.ds(c * self.rows, self.rows), self.total(c))
+
+    def finish(self):
+        for copy in sum(self.flying + self.over_z, []):
+            copy.wait_send()
+
+
+class Gather:
+    def __init__(self, own, out, axes, chunks, refs):
+        self.own, self.out, self.axes, self.chunks = own, out, axes, chunks
+        self.keep_sem = refs[0]
+        self.sems = [refs[1 + 2 * i : 3 + 2 * i] for i in range(len(axes) + 1)]
+        self.z = lax.axis_index("z")
+        self.mine = tuple(lax.axis_index(a) for a in axes)
+        self.rows = own.shape[0] // chunks
+        self.keeps, self.over_z, self.over = [], {}, [{} for _ in axes]
+
+    @staticmethod
+    def scratch(axes, chunks):
+        shapes = [pltpu.SemaphoreType.DMA((chunks,))] + dma_pair(3 * chunks)
+        for i in range(len(axes)):
+            shapes += dma_pair(4 * 2**i * chunks)
+        return shapes
+
+    def pass_on(self, level, c, s, flips, src):
+        at = pl.ds(c * self.rows, self.rows)
+        places = tuple(
+            1 - m if i < len(flips) and flips[i] else m for i, m in enumerate(self.mine)
+        )
+        where = self.out.at[(self.z ^ s,) + places + (at,)]
+        number = s
+        for f in flips:
+            number = number * 2 + f
+        axis = self.axes[level]
+        self.over[level][c, s, flips] = send(
+            where if src is None else src,
+            where,
+            self.sems[level + 1],
+            number * self.chunks + c,
+            {axis: 1 - self.mine[level]},
+        )
+
+    def start(self, c):
+        at = pl.ds(c * self.rows, self.rows)
+        own, place = self.own.at[at], self.out.at[(self.z,) + self.mine + (at,)]
+        for s in (3, 2, 1):
+            self.over_z[c, s] = send(
+                own, place, self.sems[0], (s - 1) * self.chunks + c, {"z": self.z ^ s}
+            )
+        for level in range(len(self.axes)):
+            self.pass_on(level, c, 0, (0,) * level, own)
+        keep = pltpu.make_async_copy(own, place, self.keep_sem.at[c])
+        keep.start()
+        self.keeps.append(keep)
+
+    def forward(self, c):
+        for s in (1, 2, 3):
+            self.over_z[c, s].wait_recv()
+            for level in range(len(self.axes)):
+                self.pass_on(level, c, s, (0,) * level, None)
+
+    def spread(self, c):
+        for level in range(len(self.axes) - 1):
+            for (chunk, s, flips), copy in list(self.over[level].items()):
+                if chunk == c:
+                    copy.wait_recv()
+                    for later in range(level + 1, len(self.axes)):
+                        self.pass_on(
+                            later, c, s, flips + (1,) + (0,) * (later - level - 1), None
+                        )
+
+    def finish(self):
+        for keep in self.keeps:
+            keep.wait()
+        for copy in self.over[-1].values():
+            copy.wait_recv()
+        for copies in [self.over_z] + self.over:
+            for copy in copies.values():
+                copy.wait_send()
+
+
+VMEM_SPEC = pl.BlockSpec(memory_space=pltpu.VMEM)
+ANY_SPEC = pl.BlockSpec(memory_space=pl.ANY)
+
+
+def exchange(kernel, name, number, inputs, specs, outs, out_specs, scratch):
+    sizes = [len(inputs), len(outs)] + [len(s) for s in scratch]
+
+    def run(*refs):
+        groups, at = [], 0
+        for size in sizes:
+            groups.append(refs[at : at + size])
+            at += size
+        kernel(*groups)
+
+    return pl.pallas_call(
+        run,
+        out_shape=outs,
+        in_specs=specs,
+        out_specs=out_specs,
+        scratch_shapes=sum(scratch, []),
+        compiler_params=pltpu.CompilerParams(
+            collective_id=number, has_side_effects=True, vmem_limit_bytes=48 * 2**20
+        ),
+        name=name,
+    )(*inputs)
+
+
+def share_inputs(tokens, slices, wo, units):
+    count, own = tokens.shape[0], wo.shape[0]
+    number = units[0].shape[0]
+    columns = slices.shape[-1]
+    chunks = 2
+
+    def kernel(ins, outs, token_refs, other):
+        tok, cut, wo_ref, unit_refs = ins[0], ins[1], ins[2], ins[3:]
+        tok_out, cut_out, wo_out, near_out, far_out = outs
+        keep, ctx_sems, exp_sems, wo_sems = other[0], other[1:3], other[3:5], other[5:7]
+        near_sems, far_sems = other[7:9], other[9:11]
+        z, y, x, k = (lax.axis_index(a) for a in ("z", "y", "x", "k"))
+        ctx_peers = [
+            ((z ^ s, y ^ t), s * 2 + t) for s in (3, 2, 1, 0) for t in (1, 0) if s or t
+        ]
+        exp_peers = [((x ^ a, k ^ b), a * 2 + b) for a in (1, 0) for b in (1, 0) if a or b]
+        greet(
+            [{"z": p, "y": q} for (p, q), _ in ctx_peers]
+            + [{"x": p, "k": q} for (p, q), _ in exp_peers]
+        )
+        gather = Gather(tok, tok_out, ("y",), chunks, token_refs)
+        over_ctx = [
+            send(cut.at[p, q], cut_out.at[z, y, x, k], ctx_sems, i - 1, {"z": p, "y": q})
+            for (p, q), i in ctx_peers
+        ]
+        for c in range(chunks):
+            gather.start(c)
+        over_wo = [
+            send(wo_ref, wo_out.at[x, k], wo_sems, i - 1, {"x": p, "k": q})
+            for (p, q), i in exp_peers
+        ]
+        over_near, over_far = {}, []
+        for j in range(number):
+            for i in (3, 2, 1):
+                over_near[i, j] = send(
+                    unit_refs[i].at[j],
+                    near_out.at[i - 1, j],
+                    near_sems,
+                    (i - 1) * number + j,
+                    {"z": z ^ i},
+                )
+            over_far.append(
+                send(unit_refs[0].at[j], far_out.at[0, j], far_sems, j, {"y": 1 - y})
+            )
+        keeps = [
+            pltpu.make_async_copy(cut.at[z, y], cut_out.at[z, y, x, k], keep.at[0]),
+            pltpu.make_async_copy(wo_ref, wo_out.at[x, k], keep.at[1]),
+        ]
+        for copy in keeps:
+            copy.start()
+        for copy in over_ctx:
+            copy.wait_recv()
+        keeps[0].wait()
+        mine = cut_out.at[:, :, x, k]
+        over_exp = [
+            send(mine, mine, exp_sems, i - 1, {"x": p, "k": q}) for (p, q), i in exp_peers
+        ]
+        for c in range(chunks):
+            gather.forward(c)
+        for j in range(number):
+            for i in (1, 2, 3):
+                over_near[i, j].wait_recv()
+                over_far.append(
+                    send(
+                        near_out.at[i - 1, j],
+                        far_out.at[i, j],
+                        far_sems,
+                        i * number + j,
+                        {"y": 1 - y},
+                    )
+                )
+        for copy in over_exp + over_wo + over_far:
+            copy.wait_recv()
+        keeps[1].wait()
+        gather.finish()
+        for copy in over_ctx + over_exp + over_wo + list(over_near.values()) + over_far:
+            copy.wait_send()
+
+    bf16 = jnp.bfloat16
+    return exchange(
+        kernel,
+        "share_inputs",
+        1,
+        (tokens, slices, wo, *units),
+        [ANY_SPEC] * 7,
+        [
+            jax.ShapeDtypeStruct((4, 2, count, D), bf16),
+            jax.ShapeDtypeStruct((4, 2, 2, 2, own, columns), bf16),
+            jax.ShapeDtypeStruct((2, 2, own, D), bf16),
+            jax.ShapeDtypeStruct((3,) + units[0].shape, bf16),
+            jax.ShapeDtypeStruct((4,) + units[0].shape, bf16),
+        ],
+        [ANY_SPEC] * 5,
+        [
+            Gather.scratch(("y",), chunks),
+            [pltpu.SemaphoreType.DMA((2,))]
+            + dma_pair(7)
+            + dma_pair(3)
+            + dma_pair(3)
+            + dma_pair(3 * number)
+            + dma_pair(4 * number),
+        ],
+    )
+
+
+def middle_step(part, tokens, marked, gain):
+    count, chunks, wide = tokens.shape[0], 4, marked.shape[-1]
+    bf16, f32 = jnp.bfloat16, jnp.float32
+
+    def kernel(ins, outs, scatter_refs, hidden_refs, marked_refs, own):
+        part_ref, tok, marked_ref, gain_ref = ins
+        middle_ref, hidden_out, marked_out = outs
+        greet(z_peers() + siblings(("y", "x", "k")))
+        scatter = Scatter(part_ref, ("y",), chunks, scatter_refs)
+        hidden = Gather(own[0], hidden_out, ("x", "k"), chunks, hidden_refs)
+        other = Gather(marked_ref, marked_out, ("x", "k"), 1, marked_refs)
+        scatter.start()
+        other.start(0)
+
+        def use(c, at, total):
+            middle = tok[at, :].astype(f32) + total
+            middle_ref[at, :] = middle
+            scale = lax.rsqrt(jnp.mean(middle * middle, axis=-1, keepdims=True) + EPSILON)
+            own[0][at, :] = (middle * scale * gain_ref[...]).astype(bf16)
+            hidden.start(c)
+
+        scatter.run(use)
+        other.forward(0)
+        for c in range(chunks):
+            hidden.forward(c)
+            if c == 0:
+                other.spread(0)
+            hidden.spread(c)
+        other.finish()
+        hidden.finish()
+        scatter.finish()
+
+    blocks = (4, 2, 2, count)
+    return exchange(
+        kernel,
+        "middle_step",
+        2,
+        (part, tokens, marked, gain),
+        [ANY_SPEC, VMEM_SPEC, ANY_SPEC, VMEM_SPEC],
+        [
+            jax.ShapeDtypeStruct((count, D), f32),
+            jax.ShapeDtypeStruct(blocks + (D,), bf16),
+            jax.ShapeDtypeStruct(blocks + (wide,), bf16),
+        ],
+        [VMEM_SPEC, ANY_SPEC, ANY_SPEC],
+        [
+            Scatter.scratch(part, ("y",), chunks),
+            Gather.scratch(("x", "k"), chunks),
+            Gather.scratch(("x", "k"), 1),
+            [pltpu.VMEM((count, D), bf16)],
+        ],
+    )
+
+
+def router_step(part, middle, cotangent, gates, router, gain):
+    count, chunks = middle.shape[0], 4
+    bf16, f32 = jnp.bfloat16, jnp.float32
+
+    def kernel(ins, outs, scatter_refs, gather_refs, own):
+        part_ref, middle_ref, up_ref, gates_ref, router_ref, gain_ref = ins
+        logit_ref, gain_out, grad_ref, branch_out = outs
+        greet(z_peers() + siblings(("y", "x", "k")))
+        scatter = Scatter(part_ref, ("x", "k"), chunks, scatter_refs)
+        gather = Gather(own[0], branch_out, ("y",), chunks, gather_refs)
+        scatter.start()
+        gain_out[...] = jnp.zeros_like(gain_out)
+
+        def use(c, at, total):
+            gate, gate_grad = gates_ref[at, :], total[:, D:]
+            inner = jnp.sum(gate * gate_grad, axis=-1, keepdims=True)
+            logit_grad = (gate * (gate_grad - inner)).astype(bf16)
+            logit_ref[at, :] = logit_grad
+            grad = total[:, :D] + contract_cols(logit_grad, router_ref[...])
+            middle = middle_ref[at, :]
+            scale = lax.rsqrt(jnp.mean(middle * middle, axis=-1, keepdims=True) + EPSILON)
+            normed = middle * scale
+            gain_out[...] += jnp.sum(grad * normed, axis=0, keepdims=True)
+            scaled = grad * gain_ref[...]
+            result = up_ref[at, :].astype(f32) + scale * (
+                scaled - normed * jnp.mean(scaled * normed, axis=-1, keepdims=True)
+            )
+            grad_ref[at, :] = result
+            own[0][at, :] = result.astype(bf16)
+            gather.start(c)
+
+        scatter.run(use)
+        for c in range(chunks):
+            gather.forward(c)
+        gather.finish()
+        scatter.finish()
+
+    return exchange(
+        kernel,
+        "router_step",
+        3,
+        (part, middle, cotangent, gates, router, gain),
+        [ANY_SPEC] + [VMEM_SPEC] * 5,
+        [
+            jax.ShapeDtypeStruct((count, 128), bf16),
+            jax.ShapeDtypeStruct((1, D), f32),
+            jax.ShapeDtypeStruct((count, D), f32),
+            jax.ShapeDtypeStruct((4, 2, count, D), bf16),
+        ],
+        [VMEM_SPEC] * 3 + [ANY_SPEC],
+        [
+            Scatter.scratch(part, ("x", "k"), chunks),
+            Gather.scratch(("y",), chunks),
+            [pltpu.VMEM((count, D), bf16)],
+        ],
+    )
+
+
+def last_step(part, mixed, tokens, middle, grad_middle, gain, qkv_part, wo_part, small_part):
+    count, chunks = tokens.shape[0], 4
+    own, columns = qkv_part.shape[-2:]
+    bf16, f32 = jnp.bfloat16, jnp.float32
+
+    def kernel(ins, outs, part_refs, mixed_refs, other):
+        part_ref, mixed_ref, tok, middle_ref, grad_ref, gain_ref, qkv, wo, small = ins
+        out_ref, tokens_ref, qkv_out, wo_out, small_out = outs
+        qkv_came, qkv_sum, wo_came, small_came = other[:4]
+        sems = [other[4 + 2 * i : 6 + 2 * i] for i in range(4)]
+        names = ("z", "y", "x", "k")
+        z, y, x, k = (lax.axis_index(a) for a in names)
+        everyone = [
+            ((z ^ (i // 8), y ^ (i // 4 % 2), x ^ (i // 2 % 2), k ^ (i % 2)), i)
+            for i in range(31, 0, -1)
+        ]
+        of_ctx = [(p, i // 4) for p, i in everyone if i % 4 == 0]
+        of_exp = [(p, i) for p, i in everyone if i < 4]
+        place = lambda p: dict(zip(names, p))
+        greet([place(p) for p, _ in everyone])
+        first = Scatter(part_ref, ("y",), chunks, part_refs)
+        second = Scatter(mixed_ref, ("x", "k"), chunks, mixed_refs)
+        first.start()
+        second.start()
+        over_qkv = [
+            send(qkv.at[p[2], p[3]], qkv_came.at[i - 1], sems[0], i - 1, place(p))
+            for p, i in of_exp
+        ]
+        over_wo = [
+            send(wo.at[p[2], p[3]], wo_came.at[i - 1], sems[1], i - 1, place(p))
+            for p, i in of_exp
+        ]
+
+        def use_first(c, at, total):
+            resid = tok[at, :].astype(f32)
+            scale = lax.rsqrt(jnp.mean(resid * resid, axis=-1, keepdims=True) + EPSILON)
+            normed = resid * scale
+            scaled = total * gain_ref[...]
+            tokens_ref[at, :] = grad_ref[at, :] + scale * (
+                scaled - normed * jnp.mean(scaled * normed, axis=-1, keepdims=True)
+            )
+
+        def use_second(c, at, total):
+            out_ref[at, :] = (middle_ref[at, :] + total).astype(bf16)
+
+        first.run(use_first)
+        total = qkv[x, k].astype(f32)
+        for copy, (_, i) in zip(over_qkv, of_exp):
+            copy.wait_recv()
+            total = total + qkv_came[i - 1].astype(f32)
+        qkv_sum[...] = total.astype(bf16)
+        qkv_out[z, y] = qkv_sum[z, y]
+        over_ctx = [
+            send(qkv_sum.at[p[0], p[1]], qkv_out.at[z, y], sems[2], i - 1, place(p))
+            for p, i in of_ctx
+        ]
+        over_small = [
+            send(small.at[p], small_came.at[i - 1], sems[3], i - 1, place(p)) for p, i in everyone
+        ]
+        second.run(use_second)
+        total = wo[x, k].astype(f32)
+        for copy, (_, i) in zip(over_wo, of_exp):
+            copy.wait_recv()
+            total = total + wo_came[i - 1].astype(f32)
+        wo_out[...] = total
+        total = small[z, y, x, k].astype(f32)
+        for copy, (_, i) in zip(over_small, everyone):
+            copy.wait_recv()
+            total = total + small_came[i - 1].astype(f32)
+        small_out[...] = total
+        for copy in over_ctx:
+            copy.wait_recv()
+        first.finish()
+        second.finish()
+        for copy in over_qkv + over_wo + over_ctx + over_small:
+            copy.wait_send()
+
+    return exchange(
+        kernel,
+        "last_step",
+        4,
+        (part, mixed, tokens, middle, grad_middle, gain, qkv_part, wo_part, small_part),
+        [ANY_SPEC] * 2 + [VMEM_SPEC] * 7,
+        [
+            jax.ShapeDtypeStruct((count, D), bf16),
+            jax.ShapeDtypeStruct((count, D), f32),
+            jax.ShapeDtypeStruct((4, 2, own, columns), bf16),
+            jax.ShapeDtypeStruct((own, D), f32),
+            jax.ShapeDtypeStruct((own, 128), f32),
+        ],
+        [VMEM_SPEC] * 5,
+        [
+            Scatter.scratch(part, ("y",), chunks),
+            Scatter.scratch(mixed, ("x", "k"), chunks),
+            [
+                pltpu.VMEM((3, 4, 2, own, columns), bf16),
+                pltpu.VMEM((4, 2, own, columns), bf16),
+                pltpu.VMEM((3, own, D), bf16),
+                pltpu.VMEM((31, own, 128), bf16),
+            ]
+            + dma_pair(3)
+            + dma_pair(3)
+            + dma_pair(7)
+            + dma_pair(31),
+        ],
+    )
+
+
 def body_heads(
     tokens,
     cotangent,
@@ -594,9 +1241,10 @@
     expert_out,
 ):
     bf16, f32 = jnp.bfloat16, jnp.float32
-    ctx_axes, tok_axes, all_axes = ("z", "y"), ("z", "exp"), ("z", "y", "exp")
-    n_z, n_y, n_exp = (lax.axis_size(a) for a in all_axes)
+    n_z, n_y = (lax.axis_size(a) for a in ("z", "y"))
+    n_exp = lax.axis_size("x") * lax.axis_size("k")
     n_ctx = n_z * n_y
+    exp_index = lax.axis_index("x") * lax.axis_size("k") + lax.axis_index("k")
     count = tokens.shape[1]
     group = count * n_ctx
     repeat = HEADS // KV_HEADS
@@ -614,15 +1262,10 @@
     wout = expert_out.transpose(1, 0, 2)
     swap_z = [[(i, i ^ s) for i in range(n_z)] for s in range(n_z)]
     swap_y = [(i, i ^ 1) for i in range(n_y)]
-    near = [None] * 4
-    for s in (3, 2, 1, 0):
-        near[s] = take_units(units * (z_index ^ s), units, win, wout)
-        if s:
-            near[s] = lax.ppermute(near[s], "z", swap_z[s])
-    parts = near + [lax.ppermute(a, "y", swap_y) for a in near]
+    near = [take_units(units * (z_index ^ s), units, win, wout) for s in range(4)]
 
     wq, wk, wv = (a.astype(bf16) for a in (attn_q, attn_k, attn_v))
-    wqkv = jnp.concatenate(
+    own_qkv = jnp.concatenate(
         [
             wq.reshape(own, n_ctx, width),
             wk.reshape(own, n_ctx, HEAD),
@@ -630,29 +1273,32 @@
         ],
         axis=-1,
     )
-    own_qkv = wqkv
-    wqkv = lax.all_to_all(
-        wqkv.transpose(1, 0, 2), ctx_axes, split_axis=0, concat_axis=0, tiled=True
-    )
-    wqkv = lax.all_gather(wqkv, "exp", axis=1).reshape(D, width + 2 * HEAD)
-    wo = lax.all_gather(attn_o.astype(bf16), "exp", axis=0, tiled=True)
     small = jnp.concatenate(
         [
             router.astype(bf16),
             norm_attn.astype(bf16)[:, None],
             norm_moe.astype(bf16)[:, None],
-            jnp.zeros((own, 128 - experts - 2), bf16),
+            jnp.zeros((own, 64 - experts - 2), bf16),
         ],
         axis=1,
     )
-    small = lax.all_gather(small, all_axes, axis=0, tiled=True)
-    weight_r = small[:, :experts]
-    gain_one_f = small[:, experts].astype(f32)
-    gain_two_f = small[:, experts + 1].astype(f32)
-
-    token_all = lax.all_gather(tokens[0], ctx_axes, axis=0, tiled=True)
-    upstream_blocks = lax.all_gather(cotangent[0], tok_axes, axis=0)
-    route_blocks = lax.all_gather(routes[0], tok_axes, axis=0)
+    slices = jnp.concatenate(
+        [own_qkv.transpose(1, 0, 2), jnp.broadcast_to(small, (n_ctx, own, 64))], axis=-1
+    )
+    token_all, slices, wo, near_parts, far_parts = share_inputs(
+        tokens[0], slices.reshape(n_z, n_y, own, -1), attn_o.astype(bf16), near
+    )
+    token_all = token_all.reshape(group, D)
+    slices = slices.reshape(D, -1)
+    wo = wo.reshape(width, D)
+    wqkv, small = slices[:, : width + 2 * HEAD], slices[:, width + 2 * HEAD :]
+    weight_r = jnp.concatenate([small[:, :experts], jnp.zeros((D, 128 - experts), bf16)], axis=1)
+    gain_one_f = small[:, experts].astype(f32)[None, :]
+    gain_two_f = small[:, experts + 1].astype(f32)[None, :]
+    marked = jnp.concatenate(
+        [cotangent[0], routes[0].astype(bf16), jnp.zeros((count, 128 - TOP), bf16)], axis=1
+    )
+
     perm_row = span_perm[0]
     first_len = lengths[0, 0]
     rows = global_rows(perm_row, jnp.arange(group, dtype=jnp.int32))
@@ -685,55 +1331,22 @@
     )
     log_total = highest + jnp.log(total)
     attended_b = attended.transpose(1, 0, 2).reshape(group, width).astype(bf16)
-    branch = lax.psum_scatter(
-        jnp.dot(attended_b, wo, preferred_element_type=f32).astype(bf16),
-        ctx_axes,
-        scatter_dimension=0,
-        tiled=True,
-    )
-    resid = tokens[0].astype(f32)
-    middle = resid + branch.astype(f32)
-    scale_two = lax.rsqrt(jnp.mean(middle * middle, axis=-1, keepdims=True) + EPSILON)
-    normed_two = middle * scale_two
-    hidden_two = (normed_two * gain_two_f).astype(bf16)
-
-    hidden_blocks = lax.all_gather(hidden_two, tok_axes, axis=0)
+    branch = jnp.dot(attended_b, wo, preferred_element_type=f32).astype(bf16)
+    middle, hidden_blocks, marked_blocks = middle_step(
+        branch.reshape(n_z, n_y, count, D), tokens[0], marked, gain_two_f
+    )
+    hidden_blocks = hidden_blocks.reshape(-1, count, D)
+    marked_blocks = marked_blocks.reshape(-1, count, D + 128)
+
     blocks = hidden_blocks.shape[0]
     held = 3
-    base = lax.axis_index("exp") * EXP_DEV + (units * z_index) // 2
+    base = exp_index * EXP_DEV + (units * z_index) // 2
     shift = (units * z_index) % 2
-    logits = jnp.einsum("btd,de->bte", hidden_blocks, weight_r, preferred_element_type=f32)
-    picks = route_blocks[..., None] == jnp.arange(experts, dtype=jnp.int32)
-    selected = jnp.sum(jnp.where(picks, logits[:, :, None, :], 0.0), axis=-1)
-    gates_blocks = jax.nn.softmax(selected, axis=-1).astype(bf16).astype(f32)
-    held_ids = base + jnp.arange(held, dtype=jnp.int32)
-    held_picks = route_blocks[..., None] == held_ids
-    gate_held = jnp.sum(jnp.where(held_picks, gates_blocks[..., None], 0.0), axis=2)
-    hit = jnp.any(held_picks, axis=2)
-    lower = jnp.tril(jnp.ones((count, count), bf16))
-    rank = jnp.einsum("ts,bse->bte", lower, hit.astype(bf16), preferred_element_type=f32)
     pairs = blocks // 2
-    side = jnp.arange(2, dtype=jnp.int32)
-    held_first = lambda a: a.reshape(pairs, 2, count, held).transpose(0, 3, 1, 2)
-    here = (
-        held_first(hit)[:, :, None, None]
-        & (
-            held_first(rank)[:, :, None, None]
-            == (jnp.arange(slots, dtype=f32) + 1.0)[None, None, None, :, None, None]
-        )
-        & (side[:, None] == side[None, :])[None, None, :, None, :, None]
-    )
-    spread = here.astype(bf16).reshape(pairs, held * 2 * slots, 2 * count)
-    slot_gate = jnp.sum(
-        jnp.where(here, held_first(gate_held)[:, :, None, None], 0.0), axis=(-2, -1)
-    )
-    slot_gate = slot_gate.transpose(1, 0, 2, 3).reshape(held, blocks * slots, 1)
-
-    def to_rows(a):
-        rows = jnp.einsum(
-            "prt,ptd->prd", spread, a.reshape(pairs, 2 * count, D), preferred_element_type=f32
-        )
-        return rows.astype(bf16).reshape(pairs, held, 2 * slots, D)
+    row_in, row_up, slot_gate, spread, gates_blocks = dispatch(
+        base, hidden_blocks, marked_blocks, weight_r, held, slots
+    )
+    gates = lax.dynamic_index_in_dim(gates_blocks, z_index * n_exp + exp_index, 0, keepdims=False)
 
     def to_tokens(rows):
         a = jnp.einsum(
@@ -746,48 +1359,44 @@
 
     meta = jnp.stack([shift, z_index, y_index, base]).astype(jnp.int32)
     made, back, *grads = run_experts(
-        meta, to_rows(hidden_blocks), to_rows(upstream_blocks), slot_gate, parts
-    )
-    back = lax.psum_scatter(to_tokens(back), tok_axes, scatter_dimension=0, tiled=False)
-    back = back.astype(f32)
-    mixture = lax.psum_scatter(to_tokens(made), tok_axes, scatter_dimension=0, tiled=False)
-    output = (middle + mixture.astype(f32)).astype(bf16)
-    back_rows, dgate_own = back[:, :D], back[:, D : D + experts]
-
+        meta, row_in, row_up, slot_gate, near[0], near_parts, far_parts
+    )
+    logit_grad, grad_gain_two, grad_middle, branch_all = router_step(
+        to_tokens(back).reshape(n_z, 2, 2, count, D + 128),
+        middle,
+        cotangent[0],
+        gates,
+        weight_r,
+        gain_two_f,
+    )
+    branch_all = branch_all.reshape(group, D)
+
+    swap_z = [[(i, i ^ s) for i in range(n_z)] for s in range(n_z)]
+    swap_y = [(i, i ^ 1) for i in range(n_y)]
     sums = [None] * 4
     for s in (3, 2, 1, 0):
         other = lax.ppermute(grads[4 + s], "y", swap_y)
         sums[s] = (grads[s].astype(f32) + other.astype(f32)).astype(bf16)
-        if s:
-            sums[s] = lax.ppermute(sums[s], "z", swap_z[s])
+    sums, branch_all = lax.optimization_barrier((sums, branch_all))
+    for s in (3, 2, 1):
+        sums[s] = lax.ppermute(sums[s], "z", swap_z[s])
     grad_expert_in, grad_expert_out = place_units(z_index, jnp.concatenate(sums), units)
     grad_expert_in = grad_expert_in.transpose(1, 0, 2)
     grad_expert_out = grad_expert_out.transpose(1, 0, 2)
 
-    chosen = routes[0]
-    own_picks = chosen[:, :, None] == jnp.arange(experts, dtype=jnp.int32)[None, None, :]
-    own_logits = jnp.dot(hidden_two, weight_r, preferred_element_type=f32)
-    own_selected = jnp.sum(jnp.where(own_picks, own_logits[:, None, :], 0.0), axis=-1)
-    gates = jax.nn.softmax(own_selected, axis=-1)
-    gate_grad = jnp.sum(jnp.where(own_picks, dgate_own[:, None, :], 0.0), axis=-1)
-    select_grad = gates * (gate_grad - jnp.sum(gates * gate_grad, axis=-1, keepdims=True))
-    logit_grad = jnp.sum(jnp.where(own_picks, select_grad[:, :, None], 0.0), axis=1).astype(bf16)
-    grad_router = contract_rows(hidden_two, logit_grad)
-    grad_norm_two = back_rows + contract_cols(logit_grad, weight_r)
-    grad_gain_two = jnp.sum(grad_norm_two * normed_two, axis=0)
+    hidden_two = lax.dynamic_index_in_dim(
+        hidden_blocks, z_index * n_exp + exp_index, 0, keepdims=False
+    )
     small_grads = jnp.concatenate(
-        [grad_router, grad_gain_two[:, None], jnp.zeros((D, 128 - experts - 1), f32)], axis=1
-    )
-    small_grads = lax.psum_scatter(small_grads, all_axes, scatter_dimension=0, tiled=True)
-    upstream = cotangent[0].astype(f32)
-    scaled_two = grad_norm_two * gain_two_f
-    grad_middle = upstream + scale_two * (
-        scaled_two - normed_two * jnp.mean(scaled_two * normed_two, axis=-1, keepdims=True)
-    )
-
-    branch_all = lax.all_gather(grad_middle.astype(bf16), ctx_axes, axis=0, tiled=True)
+        [
+            contract_rows(hidden_two, logit_grad)[:, : 128 - 1],
+            grad_gain_two.reshape(D, 1),
+        ],
+        axis=1,
+    )
+    small_grads = small_grads.astype(bf16).reshape(n_z, n_y, 2, 2, own, 128)
+
     grad_wo = contract_rows(attended_b, branch_all).astype(bf16)
-    grad_wo = lax.psum_scatter(grad_wo, "exp", scatter_dimension=0, tiled=True).astype(f32)
     grad_heads = contract_cols(branch_all, wo).astype(bf16).reshape(group, repeat, HEAD)
     grad_heads = grad_heads.transpose(1, 0, 2)
     drift = jnp.sum(grad_heads.astype(f32) * attended, axis=-1)
@@ -814,26 +1423,27 @@
         ],
         axis=-1,
     ).astype(bf16)
-    grad_hidden = lax.psum_scatter(
-        contract_cols(grad_qkv, wqkv).astype(bf16), ctx_axes, scatter_dimension=0, tiled=True
-    ).astype(f32)
+    grad_hidden = contract_cols(grad_qkv, wqkv).astype(bf16).reshape(n_z, n_y, count, D)
     grad_wqkv = contract_rows(hidden_all, grad_qkv).astype(bf16)
     grad_wqkv = grad_wqkv.reshape(n_ctx, n_exp, own, width + 2 * HEAD).transpose(1, 0, 2, 3)
-    grad_wqkv = lax.psum_scatter(grad_wqkv, "exp", scatter_dimension=0, tiled=False)
-    grad_wqkv = lax.all_to_all(grad_wqkv, ctx_axes, split_axis=0, concat_axis=0, tiled=True)
-    grad_wqkv = grad_wqkv.astype(f32)
+    output, grad_tokens, grad_wqkv, grad_wo, small_grads = last_step(
+        grad_hidden,
+        to_tokens(made).reshape(n_z, 2, 2, count, D),
+        tokens[0],
+        middle,
+        grad_middle,
+        gain_one_f,
+        grad_wqkv.reshape(2, 2, n_z, n_y, own, width + 2 * HEAD),
+        grad_wo.reshape(2, 2, own, D),
+        small_grads,
+    )
+    grad_wqkv = grad_wqkv.reshape(n_ctx, own, width + 2 * HEAD).astype(f32)
     grad_q = grad_wqkv[:, :, :width].transpose(1, 0, 2).reshape(own, HEADS * HEAD)
     grad_k = grad_wqkv[:, :, width : width + HEAD].transpose(1, 0, 2).reshape(own, KV_HEADS * HEAD)
     grad_v = grad_wqkv[:, :, width + HEAD :].transpose(1, 0, 2).reshape(own, KV_HEADS * HEAD)
     grad_gain_one = jnp.sum(
         grad_wqkv.transpose(1, 0, 2) * own_qkv.astype(f32), axis=(1, 2)
     ) / norm_attn.astype(bf16).astype(f32)
-    scale_one = lax.rsqrt(jnp.mean(resid * resid, axis=-1, keepdims=True) + EPSILON)
-    normed_one = resid * scale_one
-    scaled_one = grad_hidden * gain_one_f
-    grad_tokens = grad_middle + scale_one * (
-        scaled_one - normed_one * jnp.mean(scaled_one * normed_one, axis=-1, keepdims=True)
-    )
     return (
         output[None],
         grad_tokens[None],
@@ -843,7 +1453,7 @@
         grad_v,
         grad_wo,
         small_grads[:, :experts],
-        small_grads[:, experts],
+        small_grads[:, 127],
         grad_expert_in,
         grad_expert_out,
     )
@@ -851,14 +1461,15 @@
 
 def solution(mesh):
     ctx, exp = mesh.shape["ctx"], mesh.shape["exp"]
-    if ctx == KV_HEADS and exp * EXP_DEV == 40:
-        inner = jax.sharding.Mesh(mesh.devices.reshape(ctx // 2, 2, exp), ("z", "y", "exp"))
-        body, ctx_name, both = body_heads, ("z", "y"), ("z", "y", "exp")
+    if ctx == KV_HEADS and exp == 4:
+        names = ("z", "y", "x", "k")
+        inner = jax.sharding.Mesh(mesh.devices.reshape(4, 2, 2, 2), names)
+        body, ctx_name, exp_name, both = body_heads, names[:2], names[2:], names
     else:
-        inner, body, ctx_name, both = mesh, body_general, "ctx", ("ctx", "exp")
-    token = P("exp", ctx_name, None)
-    group = P("exp", None)
-    expert = P(ctx_name, "exp", None)
+        inner, body, ctx_name, exp_name, both = mesh, body_general, "ctx", "exp", ("ctx", "exp")
+    token = P(exp_name, ctx_name, None)
+    group = P(exp_name, None)
+    expert = P(ctx_name, exp_name, None)
     rows, gain = P(both, None), P(both)
     in_specs = (token, token, group, group, token, gain) + (rows,) * 5 + (gain, expert, expert)
     out_specs = (token, token, gain) + (rows,) * 5 + (gain, expert, expert)

time: 1150 us -> 973 us (0.85)
  Pallas kernels: 82.1 us -> 825 us
  waiting for transfers between devices: 678 us -> 0.02 us
  blocking collectives: 183 us -> 0 us
  starting transfers between devices: 31.2 us -> 8.56 us
  matrix products: 78.6 us -> 58.6 us
  between operations: 17 us -> 2.02 us
    pallas_call x0 -> x5, Pallas kernels: none -> 743 us  [the longest x4 727 us: exchange(): pl.pallas_call(run, out_shape=outs, in_specs=specs, out_specs=out_specs,...]
    reduce_scatter x5 -> x0, waiting for transfers between devices: 388 us -> none  [the longest x1 129 us: body_heads(): lax.psum_scatter(to_tokens(back), tok_axes, scatter_dimension=0, tiled=Fa...]
    all_gather x4 -> x0, blocking collectives: 183 us -> none  [the longest x1 119 us: body_heads(): route_blocks = lax.all_gather(routes[0], tok_axes, axis=0)]
    ppermute x4, waiting for transfers between devices: 115 us -> 0.01 us  [body_heads(): other = lax.ppermute(grads[4 + s], 'y', swap_y)]
    ppermute x7 -> x0, waiting for transfers between devices: 66.7 us -> none  [the longest x4 66.7 us: body_heads(): parts = near + [lax.ppermute(a, 'y', swap_y) for a in near]]
    all_gather x4 -> x0, waiting for transfers between devices: 59.1 us -> none  [the longest x1 59.1 us: body_heads(): lax.all_gather(grad_middle.astype(bf16), ctx_axes, axis=0, tiled=True)]
    ppermute x3, waiting for transfers between devices: 32.8 us -> 0.01 us  [body_heads(): sums[s] = lax.ppermute(sums[s], 'z', swap_z[s])]
    dot_general x6 -> x1, matrix products: 22.1 us -> 2.21 us  [body_heads(): branch = jnp.dot(attended_b, wo, preferred_element_type=f32).astype(bf16)]
  transfers between devices with their start and end apart: 27 -> 7, of which waited for: 16 -> 0; matrix products, arithmetic and copies ran while one was open for 8% -> 4% of each run, Pallas kernels for 2% -> 37%
where the time goes in v2:
time: 973 us; the launch traced here: 964 us
  Pallas kernels  825 us (85%)
  matrix products  58.6 us (6%)
  other arithmetic  43.5 us (4%)
  local copies, waits for them, and re-layouts  26.5 us (3%)
    pallas_call x4, Pallas kernels, exchange(): pl.pallas_call(run, out_shape=outs, in_specs=specs, out_specs=out_specs,...  727 us
    pallas_call x1, Pallas kernels, run_experts(): pl.pallas_call(lambda *refs: expert_kernel(depth, *refs), grid_spec=pltpu...  54.3 us
  transfers between devices with their start and end apart: 7, of which 0 were waited for; matrix products, arithmetic and copies ran while one was open for 4% of the time, Pallas kernels for 37%

profile of v2, /device:TPU:0, one launch (start us, length us, event | category | flops | bytes accessed | tf_op | source)
XLA Modules:
  0.0 963.7 jit_solution(5090178196669169834)
XLA Ops:
  0.7 0.7 select_reduce_fusion
  2.8 0.7 convert_element_type.176
  4.4 0.9 convert_element_type.174
  5.5 0.9 convert_element_type.175
  6.6 1.0 convert_element_type.173
  7.9 1.1 convert_element_type.179.refs_2_
  8.9 4.5 take_units.4.refs_3_.refs_4_
  13.4 4.5 take_units.7.refs_6_
  17.9 4.5 take_units.6.refs_5_
  22.4 4.6 take_units.5.refs_4_
  27.3 1.4 copy-done.1
  28.7 208.2 %share_inputs.1 = (bf16[4,2,128,1536]{3,2,1,0:T(8,128)(2,1)}, bf16[4,2,2,2,48,384]{5,4,3,2,1,0:T(8,128)(2,1)S(1)}, bf16[2,2,48,1536]{3,2,1,0:T(8,128)(2,1)S(1)},...) custom-call(bf16[128,1536]{1,0:T(8,128)(2,1)S(1)} %bitcast.153, bf16[4,2,48,384]{3,2,1,0:T(8,128)(2,1)S(1)} %bitcast.161, ...), custom_call_target="tpu_custom_call" | custom-call | tf_op jit(solution)/shard_map/share_inputs/pallas_call | solution.py:889
  236.9 0.8 copy-done.16
  239.2 2.9 multiply_reduce_fusion
  242.2 0.8 fusion.7
  243.0 1.3 fusion.23
  244.8 1.2 compare_and_fusion
  246.1 1.2 fusion.35
  247.5 5.8 fusion.2
  253.3 7.3 fusion.4
  261.2 7.6 fusion.25
  268.9 2.2 convolution_convert_fusion.2
  271.7 1.9 concatenate.48.refs_2_
  273.6 1.0 copy-done.3
  274.6 1.0 copy-done.10
  275.6 158.5 %middle_step.1 = (f32[128,1536]{1,0:T(8,128)S(1)}, bf16[4,2,2,128,1536]{4,3,2,1,0:T(8,128)(2,1)}, bf16[4,2,2,128,1664]{4,3,2,1,0:T(8,128)(2,1)}) custom-call(bf16[4,2,128,1536]{3,2,1,0:T(8,128)(2,1)S(1)} %bitcast.151, bf16[128,1536]{1,0:T(8,128)(2,1)S(1)} %bitcast.154, bf16[128,1664]{1,0:T(8,128)(2,1)S(1)} %copy-done.10, f32[1,1536]{1,0:T(1,128)S(1)} %reshape.390.refs_3_.refs_5_), custom_call_target="tpu_custom_call" | custom-call | tf_op jit(solution)/shard_map/middle_step/pallas_call | solution.py:889
  434.1 0.9 copy-done.7
  435.7 15.4 %dispatch.1 = (bf16[8,3,80,1536]{3,2,1,0:T(8,128)(2,1)}, bf16[8,3,80,1536]{3,2,1,0:T(8,128)(2,1)}, f32[8,3,80,1]{3,2,1,0:T(8,128)S(1)}, bf16[8,240,256]{2,1,0:T(8,128)(2,1)S(1)}, f32[16,128,128]{2,1,0:T(8,128)S(1)}) custom-call(s32[1]{0:T(128)} %bitcast.22.base, bf16[16,128,1536]{2,1,0:T(8,128)(2,1)} %bitcast.186, bf16[16,128,1664]{2,1,0:T(8,128)(2,1)} %bitcast.188, ...), custom_call_target="tpu_custom_call" | custom-call | tf_op jit(solution)/shard_map/dispatch/pallas_call | solution.py:477
  451.1 1.0 copy-done.18
  452.1 0.9 copy-done.19
  453.1 54.3 %experts.1 = (bf16[8,3,80,1536]{3,2,1,0:T(8,128)(2,1)}, bf16[8,3,80,1664]{3,2,1,0:T(8,128)(2,1)}, bf16[5,192,768]{2,1,0:T(8,128)(2,1)}, bf16[5,192,768]{2,1,0:T(...) custom-call(s32[4]{0:T(128)} %pad_add_fusion.refs_0_, ...), custom_call_target="tpu_custom_call" | custom-call | flops 22649241600 | bytes 62914560 | tf_op jit(solution)/shard_map/experts/pallas_call | solution.py:589
  507.4 1.9 collective-permute-start
  509.5 1.8 collective-permute-start.2
  511.5 7.9 convolution_convert_fusion
  519.4 0.8 dynamic-slice_bitcast_fusion.refs_3_
  520.3 151.6 %router_step.1 = (bf16[128,128]{1,0:T(8,128)(2,1)S(1)}, f32[1,1536]{1,0:T(1,128)S(1)}, f32[128,1536]{1,0:T(8,128)S(1)}, bf16[4,2,128,1536]{3,2,1,0:T(8,128)(2,1)S(1)}) custom-call(bf16[4,2,2,128,1664]{4,3,2,1,0:T(8,128)(2,1)} %bitcast.183, f32[128,1536]{1,0:T(8,128)S(1)} %copy-done.8, bf16[128,1536]{1,0:T(8,128)(2,1)S(1)} %bitcast.160, ...), custom_call_target="tpu_custom_call" | custom-call | tf_op jit(solution)/shard_map/router_step/pallas_call | solution.py:889
  671.9 1.7 copy-done.5
  673.6 0.9 copy-done.14
  675.2 1.3 fusion.27
  676.8 7.3 convolution_convert_fusion.1
  684.1 3.0 add_convert_fusion.3
  687.1 3.1 add_convert_fusion.2
  690.2 3.0 add_convert_fusion.1
  693.3 3.0 add_convert_fusion
  696.3 1.2 convolution_convert_fusion.6
  697.8 6.1 fusion.19
  703.9 7.2 multiply_convert_fusion
  711.1 2.0 fusion.15
  713.2 1.2 fusion.14
  715.3 2.2 convolution_convert_fusion.4
  717.4 3.5 convolution_convert_fusion.3
  720.9 2.4 copy.67
  723.3 1.5 copy.68
  724.9 1.9 collective-permute-start.5
  726.9 2.4 collective-permute-start.6
  729.3 1.8 convolution_convert_fusion.5
  731.1 209.1 %last_step.1 = (bf16[128,1536]{1,0:T(8,128)(2,1)S(1)}, f32[128,1536]{1,0:T(8,128)S(1)}, bf16[4,2,48,320]{3,2,1,0:T(8,128)(2,1)S(1)}, f32[48,1536]{1,0:T(8,128)S(1)}, f32[48,128]{1,0:T(8,128)S(1)}) custom-call(bf16[4,2,128,1536]{3,2,1,0:T(8,128)(2,1)} %bitcast.192, bf16[4,2,2,128,1536]{4,3,2,1,0:T(8,128)(2,1)} %bitcast.184, bf16[128,1536]{1,0:T(8,128)(2,1)S(1)} %bitcast.155, ...), custom_call_target="tpu_custom_call" | custom-call | tf_op jit(solution)/shard_map/last_step/pallas_call | solution.py:889
  941.2 0.7 reshape.387
  942.2 0.9 reshape.385
  943.1 0.7 reshape.386
  945.4 6.3 pad_maximum_fusion.low_ref.high_ref
  951.7 9.3 place_units.1
  960.9 0.7 copy.82
  961.7 0.9 copy.83
  (168 shorter events, 13.1 us)
Async XLA Ops:
  0.7 245.4 %copy-start.56 = (f32[32]{0:T(128)}, f32[32]{0:T(128)S(1)}, u32[]{:S(2)}) copy-start(f32[32]{0:T(128)S(1)} %multiply_exponential_fusion) | copy-start | bytes 388
  2.8 243.3 %copy-start.53 = (f32[1024]{0:T(1024)}, f32[1024]{0:T(1024)S(1)}, u32[]{:S(2)}) copy-start(f32[1024]{0:T(1024)S(1)} %get-tuple-element.140) | copy-start | bytes 12292
  5.5 21.5 %copy-start.33 = (bf16[48,8,64]{2,0,1:T(8,128)(2,1)}, bf16[48,8,64]{2,0,1:T(8,128)(2,1)S(1)}, u32[]{:S(2)}) copy-start(bf16[48,8,64]{2,0,1:T(8,128)(2,1)S(1)} %copy.58) | copy-start | bytes 147460
  6.6 20.4 %copy-start.35 = (bf16[48,8,64]{2,0,1:T(8,128)(2,1)}, bf16[48,8,64]{2,0,1:T(8,128)(2,1)S(1)}, u32[]{:S(2)}) copy-start(bf16[48,8,64]{2,0,1:T(8,128)(2,1)S(1)} %copy.59) | copy-start | bytes 147460
  7.8 19.2 %copy-start.25 = (bf16[48,8,192]{2,0,1:T(8,128)(2,1)}, bf16[48,8,192]{2,0,1:T(8,128)(2,1)S(1)}, u32[]{:S(2)}) copy-start(bf16[48,8,192]{2,0,1:T(8,128)(2,1)S(1)} %copy.57) | copy-start | bytes 442372
  22.4 4.9 copy-start
  22.4 4.9 copy-start.2
  27.3 1.4 copy-start.1
  28.7 209.8 %copy-start.55 = (s32[1,128,8]{1,2,0:T(8,128)S(1)}, s32[1,128,8]{1,2,0:T(8,128)}, u32[]{:S(2)}) copy-start(s32[1,128,8]{1,2,0:T(8,128)} %param.18) | copy-start | bytes 12292
  237.7 5.3 copy-start.12
  238.5 3.6 copy-start.20
  243.0 1.7 copy-start.23
  244.7 15.9 %copy-start.37 = (f32[1024,320]{0,1:T(8,128)}, f32[1024,320]{0,1:T(8,128)S(1)}, u32[]{:S(2)}) copy-start(f32[1024,320]{0,1:T(8,128)S(1)} %fusion.23) | copy-start | bytes 3932164
  246.0 14.6 %copy-start.21 = (pred[1024,1024]{0,1:T(8,128)(4,1)}, pred[1024,1024]{0,1:T(8,128)(4,1)S(1)}, u32[]{:S(2)}) copy-start(pred[1024,1024]{0,1:T(8,128)(4,1)S(1)} %compare_and_fusion) | copy-start | bytes 3145732
  247.3 6.0 copy-start.31
  247.3 6.0 copy-start.44
  247.3 6.0 copy-start.46
  247.4 5.9 copy-start.39
  247.4 5.9 copy-start.41
  253.3 7.4 copy-start.51
  273.6 1.0 copy-start.3
  274.6 1.0 copy-start.10
  434.1 0.9 copy-start.7
  451.1 1.0 copy-start.18
  452.1 0.9 copy-start.19
  507.4 176.8 %collective-permute-start = (bf16[5,192,768]{2,1,0:T(8,128)(2,1)}, bf16[5,192,768]{2,1,0:T(8,128)(2,1)}, u32[]{:S(2)}, u32[]{:S(2)}) collective-permute-start(bf16[5,192,768]{2,1,0:T(8,128)(2,1)} %get-tuple-element.61), channel_id=1, source_target_pairs={{0,4},{4,0},{1,5},{5,1},{2,6},{6,2},{3,7},{7,3},{8,12},{12,8},{9,1... | collective-permute-start | bytes 4423688 | tf_op jit(solution)/shard_map/ppermute | solution.py:1378
  509.3 177.9 %collective-permute-start.1 = (bf16[5,192,768]{2,1,0:T(8,128)(2,1)}, bf16[5,192,768]{2,1,0:T(8,128)(2,1)}, u32[]{:S(2)}, u32[]{:S(2)}) collective-permute-start(bf16[5,192,768]{2,1,0:T(8,128)(2,1)} %get-tuple-element.63), channel_id=1, source_target_pairs={{0,4},{4,0},{1,5},{5,1},{2,6},{6,2},{3,7},{7,3},{8,12},{12,8},{9,1... | collective-permute-start | bytes 4423688 | tf_op jit(solution)/shard_map/ppermute | solution.py:1378
  509.5 180.8 %collective-permute-start.2 = (bf16[5,192,768]{2,1,0:T(8,128)(2,1)}, bf16[5,192,768]{2,1,0:T(8,128)(2,1)}, u32[]{:S(2)}, u32[]{:S(2)}) collective-permute-start(bf16[5,192,768]{2,1,0:T(8,128)(2,1)} %get-tuple-element.65), channel_id=1, source_target_pairs={{0,4},{4,0},{1,5},{5,1},{2,6},{6,2},{3,7},{7,3},{8,12},{12,8},{9,1... | collective-permute-start | bytes 4423688 | tf_op jit(solution)/shard_map/ppermute | solution.py:1378
  511.3 182.0 %collective-permute-start.3 = (bf16[5,192,768]{2,1,0:T(8,128)(2,1)}, bf16[5,192,768]{2,1,0:T(8,128)(2,1)}, u32[]{:S(2)}, u32[]{:S(2)}) collective-permute-start(bf16[5,192,768]{2,1,0:T(8,128)(2,1)} %get-tuple-element.67), channel_id=1, source_target_pairs={{0,4},{4,0},{1,5},{5,1},{2,6},{6,2},{3,7},{7,3},{8,12},{12,8},{9,1... | collective-permute-start | bytes 4423688 | tf_op jit(solution)/shard_map/ppermute | solution.py:1378
  511.5 8.8 copy-start.8
  511.5 8.8 copy-start.11
  520.3 156.5 %copy-start.49 = (f32[3,1024]{1,0:T(4,128)S(1)}, f32[3,1024]{1,0:T(4,128)}, u32[]{:S(2)}) copy-start(f32[3,1024]{1,0:T(4,128)} %copy-done.48) | copy-start | bytes 36868
  520.3 156.5 %copy-start.52 = (f32[3,1024]{1,0:T(4,128)S(1)}, f32[3,1024]{1,0:T(4,128)}, u32[]{:S(2)}) copy-start(f32[3,1024]{1,0:T(4,128)} %copy-done.51) | copy-start | bytes 36868
  671.9 1.7 copy-start.5
  673.5 0.9 copy-start.14
  676.8 7.4 copy-start.30
  684.1 3.0 copy-start.29
  687.1 3.1 copy-start.28
  690.2 3.0 copy-start.27
  693.2 3.1 copy-start.6
  693.2 3.1 copy-start.17
  696.3 1.2 copy-start.38
  696.3 1.2 copy-start.50
  696.3 1.5 copy-start.22
  703.9 7.2 copy-start.40
  703.9 7.2 copy-start.42
  711.1 2.1 copy-start.45
  711.1 2.1 copy-start.47
  713.2 1.3 copy-start.54
  713.2 1.3 copy-start.57
  713.2 1.8 copy-start.32
  713.2 1.8 copy-start.43
  713.2 2.0 copy-start.24
  715.3 2.2 copy-start.13
  723.3 7.8 copy-start.4
  723.3 7.8 copy-start.9
  723.3 7.8 copy-start.15
  724.8 220.6 %collective-permute-start.4 = (bf16[5,192,768]{2,1,0:T(8,128)(2,1)}, bf16[5,192,768]{2,1,0:T(8,128)(2,1)}, u32[]{:S(2)}, u32[]{:S(2)}) collective-permute-start(bf16[5,192,768]{2,1,0:T(8,128)(2,1)} %add_convert_fusion.2), channel_id=1, source_target_pairs={{0,8},{8,0},{16,24},{24,16},{1,9},{9,1},{17,25},{25,17},{2,10},{10... | collective-permute-start | bytes 4423688 | tf_op jit(solution)/shard_map/ppermute | solution.py:1382
  724.9 220.5 %collective-permute-start.5 = (bf16[5,192,768]{2,1,0:T(8,128)(2,1)}, bf16[5,192,768]{2,1,0:T(8,128)(2,1)}, u32[]{:S(2)}, u32[]{:S(2)}) collective-permute-start(bf16[5,192,768]{2,1,0:T(8,128)(2,1)} %add_convert_fusion.1), channel_id=1, source_target_pairs={{0,16},{8,24},{16,0},{24,8},{1,17},{9,25},{17,1},{25,9},{2,18},{10... | collective-permute-start | bytes 4423688 | tf_op jit(solution)/shard_map/ppermute | solution.py:1382
  726.9 218.5 %collective-permute-start.6 = (bf16[5,192,768]{2,1,0:T(8,128)(2,1)}, bf16[5,192,768]{2,1,0:T(8,128)(2,1)}, u32[]{:S(2)}, u32[]{:S(2)}) collective-permute-start(bf16[5,192,768]{2,1,0:T(8,128)(2,1)} %add_convert_fusion), channel_id=1, source_target_pairs={{0,24},{8,16},{16,8},{24,0},{1,25},{9,17},{17,9},{25,1},{2,26},{10... | collective-permute-start | bytes 4423688 | tf_op jit(solution)/shard_map/ppermute | solution.py:1382
  940.2 4.4 copy-start.26
  940.2 4.4 copy-start.34
  940.2 4.4 copy-start.36
  940.2 4.6 copy-start.58
  (2 other events, 1.4 us)

commit v3 on v2

--- a/solution.py
+++ b/solution.py
@@ -392,38 +392,6 @@
     return jnp.concatenate(
         [first * cosine - second * sine, second * cosine + first * sine], axis=-1
     )
-
-
-def unit_kernel(first_ref, gate_ref, up_ref, down_ref, unit_ref):
-    half = gate_ref.shape[-1]
-    unit_ref[0, :, :half] = gate_ref[0].astype(unit_ref.dtype)
-    unit_ref[0, :, half : 2 * half] = up_ref[0].astype(unit_ref.dtype)
-    unit_ref[0, :, 2 * half :] = down_ref[0].astype(unit_ref.dtype)
-
-
-def take_units(first, number, win, wout):
-    depth, half = win.shape[1], HID // 2
-    return pl.pallas_call(
-        unit_kernel,
-        grid_spec=pltpu.PrefetchScalarGridSpec(
-            num_scalar_prefetch=1,
-            grid=(number,),
-            in_specs=[
-                pl.BlockSpec(
-                    (1, depth, half), lambda j, f: ((f[0] + j) // 2, 0, lax.rem(f[0] + j, 2))
-                ),
-                pl.BlockSpec(
-                    (1, depth, half), lambda j, f: ((f[0] + j) // 2, 0, 2 + lax.rem(f[0] + j, 2))
-                ),
-                pl.BlockSpec(
-                    (1, depth, half), lambda j, f: ((f[0] + j) // 2, 0, lax.rem(f[0] + j, 2))
-                ),
-            ],
-            out_specs=pl.BlockSpec((1, depth, 3 * half), lambda j, f: (j, 0, 0)),
-        ),
-        out_shape=jax.ShapeDtypeStruct((number, depth, 3 * half), jnp.bfloat16),
-        name="take_units",
-    )(first.reshape(1), win, win, wout)
 
 
 def dispatch_kernel(base, hid_ref, mark_ref, router_ref, rows_ref, up_ref, gate_ref, spread_ref, gates_ref):
@@ -511,7 +479,7 @@
         pl.multiple_of(((z ^ (i % 4)) * 2 + (y ^ (i // 4))) * depth, 64) for i in range(8)
     ]
     for part, offset in zip(parts, offsets):
-        weight[pl.ds(offset, depth), :] = part[0] if len(part.shape) == 3 else part[0, 0]
+        weight[pl.ds(offset, depth), :] = part[0]
     expert = base + (j + shift) // 2
     first = jnp.logical_or(j == 0, lax.rem(j + shift, 2) == 0)
     keep = jnp.where(first, 0.0, 1.0)
@@ -573,17 +541,13 @@
         out[0] = weight[pl.ds(offset, depth), :]
 
 
-def run_experts(meta, row_in, row_up, slot_gate, own_part, near_parts, far_parts):
+def run_experts(meta, row_in, row_up, slot_gate, parts):
     pairs, held, rows, _ = row_in.shape
-    units, depth, columns = own_part.shape
+    units, depth, columns = parts[0].shape
     held_block = lambda width: pl.BlockSpec(
         (pairs, 1, rows, width), lambda j, m: (0, (j + m[0]) // 2, 0, 0)
     )
     unit_block = pl.BlockSpec((1, depth, columns), lambda j, m: (j, 0, 0))
-
-    def part_block(i):
-        return pl.BlockSpec((1, 1, depth, columns), lambda j, m: (i, j, 0, 0))
-
     bf16 = jnp.bfloat16
     total = units * pairs * rows * D * columns * 6
     return pl.pallas_call(
@@ -595,9 +559,8 @@
                 held_block(D),
                 held_block(D),
                 held_block(1),
-                unit_block,
             ]
-            + [part_block(i) for i in (0, 1, 2, 0, 1, 2, 3)],
+            + [unit_block] * 8,
             out_specs=[held_block(D), held_block(D + 128)] + [unit_block] * 8,
             scratch_shapes=[
                 pltpu.VMEM((D, columns), bf16),
@@ -615,7 +578,7 @@
             flops=total, bytes_accessed=60 * 2**20, transcendentals=units * pairs * rows * HID
         ),
         name="experts",
-    )(meta, row_in, row_up, slot_gate, own_part, *[near_parts] * 3, *[far_parts] * 4)
+    )(meta, row_in, row_up, slot_gate, *parts)
 
 
 def spread_kernel(z_ref, low_ref, high_ref, in_ref, out_ref):
@@ -697,15 +660,14 @@
         self.part, self.axes, self.chunks = part, axes, chunks
         depth = len(axes)
         self.own, self.came = refs[0], refs[1 : 1 + depth]
-        self.sums, self.far = refs[1 + depth : 1 + 2 * depth], refs[1 + 2 * depth]
-        self.load_sem = refs[2 + 2 * depth]
-        sems = refs[3 + 2 * depth :]
+        self.sums = refs[1 + depth : 1 + 2 * depth]
+        self.turn, self.line, self.result, self.load_sem = refs[1 + 2 * depth : 5 + 2 * depth]
+        sems = refs[5 + 2 * depth :]
         self.sems = [sems[2 * i : 2 * i + 2] for i in range(depth + 1)]
         self.z = lax.axis_index("z")
         self.mine = [lax.axis_index(a) for a in axes]
         self.rows = part.shape[-2] // chunks
         self.flying = [[None] * chunks for _ in axes]
-        self.over_z = [None] * chunks
 
     @staticmethod
     def scratch(part, axes, chunks):
@@ -716,11 +678,12 @@
             return pltpu.VMEM((chunks, n_z) + (2,) * i + (rows // chunks, width), kind)
 
         shapes = [buffer(depth - 1)] + [buffer(i) for i in range(depth)] * 2
-        shapes += [pltpu.VMEM((chunks, n_z - 1, rows // chunks, width), kind)]
+        shapes += [buffer(0), pltpu.VMEM((chunks, n_z + 1, rows // chunks, width), kind)]
+        shapes += [pltpu.VMEM((rows // chunks, width), jnp.float32)]
         shapes += [pltpu.SemaphoreType.DMA((chunks,))]
         for _ in range(depth):
             shapes += dma_pair(chunks)
-        return shapes + dma_pair(chunks * (n_z - 1))
+        return shapes + dma_pair(chunks * (n_z + 1))
 
     def start(self):
         level = len(self.axes) - 1
@@ -762,40 +725,87 @@
                 c,
                 {self.axes[level - 1]: 1 - mine},
             )
-        else:
-            self.over_z[c] = [
-                send(
-                    self.sums[0].at[c, self.z ^ s],
-                    self.far.at[c, s - 1],
-                    self.sems[-1],
-                    c * 3 + s - 1,
-                    {"z": self.z ^ s},
-                )
-                for s in (3, 2, 1)
-            ]
+
+    def along(self, c, w, up):
+        slot = w + 1 if up else w
+        return pltpu.make_async_remote_copy(
+            src_ref=self.turn.at[c, w],
+            dst_ref=self.line.at[c, slot],
+            send_sem=self.sems[-1][0].at[w * self.chunks + c],
+            recv_sem=self.sems[-1][1].at[slot * self.chunks + c],
+            device_id={"z": self.z + 1 if up else self.z - 1},
+            device_id_type=MESH,
+        )
+
+    def steps(self):
+        return [(3, True), (0, False), (2, True), (1, False), (1, True), (2, False)]
+
+    def relay(self, c):
+        z = self.z
+        for w, up in self.steps():
+            slot = w + 1 if up else w
+
+            @pl.when((z < w) if up else (z > w))
+            def _(w=w, up=up, slot=slot):
+                inner = (z > 0) if up else (z < 3)
+
+                @pl.when(inner)
+                def _():
+                    self.along(c, w, up).wait_recv()
+                    total = self.sums[0][c, w].astype(jnp.float32) + self.line[c, slot].astype(
+                        jnp.float32
+                    )
+                    self.turn[c, w] = total.astype(self.turn.dtype)
+
+                @pl.when(jnp.logical_not(inner))
+                def _():
+                    self.turn[c, w] = self.sums[0][c, w]
+
+                self.along(c, w, up).start()
 
     def total(self, c):
-        for copy in self.over_z[c]:
-            copy.wait_recv()
-        total = self.sums[0][c, self.z].astype(jnp.float32)
-        for s in range(3):
-            total = total + self.far[c, s].astype(jnp.float32)
-        return total
+        z = self.z
+        self.result[...] = self.sums[0][c, z].astype(jnp.float32)
+        for up in (True, False):
+
+            @pl.when((z > 0) if up else (z < 3))
+            def _(up=up):
+                self.along(c, z, up).wait_recv()
+                self.result[...] += self.line[c, z + 1 if up else z].astype(jnp.float32)
+
+        return self.result[...]
+
+    lag = 2
+
+    def length(self):
+        return self.chunks + len(self.axes) + self.lag
+
+    def advance(self, step, use):
+        depth = len(self.axes)
+        for level in range(depth - 1, -1, -1):
+            c = step - (depth - 1 - level)
+            if 0 <= c < self.chunks:
+                self.fold(level, c)
+        c = step - (depth - 1)
+        if 0 <= c < self.chunks:
+            self.relay(c)
+        c = step - depth - self.lag + 1
+        if 0 <= c < self.chunks:
+            use(c, pl.ds(c * self.rows, self.rows), self.total(c))
 
     def run(self, use):
-        depth = len(self.axes)
-        for step in range(self.chunks + depth):
-            for level in range(depth - 1, -1, -1):
-                c = step - (depth - 1 - level)
-                if 0 <= c < self.chunks:
-                    self.fold(level, c)
-            c = step - depth
-            if 0 <= c < self.chunks:
-                use(c, pl.ds(c * self.rows, self.rows), self.total(c))
+        for step in range(self.length()):
+            self.advance(step, use)
 
     def finish(self):
-        for copy in sum(self.flying + self.over_z, []):
+        for copy in sum(self.flying, []):
             copy.wait_send()
+        for c in range(self.chunks):
+            for w, up in self.steps():
+
+                @pl.when((self.z < w) if up else (self.z > w))
+                def _(w=w, up=up, c=c):
+                    self.along(c, w, up).wait_send()
 
 
 class Gather:
@@ -806,70 +816,111 @@
         self.z = lax.axis_index("z")
         self.mine = tuple(lax.axis_index(a) for a in axes)
         self.rows = own.shape[0] // chunks
-        self.keeps, self.over_z, self.over = [], {}, [{} for _ in axes]
+        self.keeps = []
 
     @staticmethod
     def scratch(axes, chunks):
-        shapes = [pltpu.SemaphoreType.DMA((chunks,))] + dma_pair(3 * chunks)
+        shapes = [pltpu.SemaphoreType.DMA((chunks,)), *dma_pair(8 * chunks)]
         for i in range(len(axes)):
             shapes += dma_pair(4 * 2**i * chunks)
         return shapes
 
-    def pass_on(self, level, c, s, flips, src):
-        at = pl.ds(c * self.rows, self.rows)
+    def block(self, c, w, flips):
         places = tuple(
             1 - m if i < len(flips) and flips[i] else m for i, m in enumerate(self.mine)
         )
-        where = self.out.at[(self.z ^ s,) + places + (at,)]
-        number = s
+        return self.out.at[(w,) + places + (pl.ds(c * self.rows, self.rows),)]
+
+    def along(self, c, w, up, own=False):
+        where = self.block(c, w, ())
+        return pltpu.make_async_remote_copy(
+            src_ref=self.own.at[pl.ds(c * self.rows, self.rows)] if own else where,
+            dst_ref=where,
+            send_sem=self.sems[0][0].at[(w * 2 + int(up)) * self.chunks + c],
+            recv_sem=self.sems[0][1].at[w * self.chunks + c],
+            device_id={"z": self.z + 1 if up else self.z - 1},
+            device_id_type=MESH,
+        )
+
+    def across(self, level, c, w, flips, own=False):
+        where = self.block(c, w, flips)
+        number = w
         for f in flips:
             number = number * 2 + f
-        axis = self.axes[level]
-        self.over[level][c, s, flips] = send(
-            where if src is None else src,
-            where,
-            self.sems[level + 1],
-            number * self.chunks + c,
-            {axis: 1 - self.mine[level]},
+        at = number * self.chunks + c
+        return pltpu.make_async_remote_copy(
+            src_ref=self.own.at[pl.ds(c * self.rows, self.rows)] if own else where,
+            dst_ref=where,
+            send_sem=self.sems[level + 1][0].at[at],
+            recv_sem=self.sems[level + 1][1].at[at],
+            device_id={self.axes[level]: 1 - self.mine[level]},
+            device_id_type=MESH,
         )
 
     def start(self, c):
-        at = pl.ds(c * self.rows, self.rows)
-        own, place = self.own.at[at], self.out.at[(self.z,) + self.mine + (at,)]
-        for s in (3, 2, 1):
-            self.over_z[c, s] = send(
-                own, place, self.sems[0], (s - 1) * self.chunks + c, {"z": self.z ^ s}
-            )
+        z = self.z
+        for up in (True, False):
+
+            @pl.when((z < 3) if up else (z > 0))
+            def _(up=up):
+                self.along(c, z, up, own=True).start()
+
         for level in range(len(self.axes)):
-            self.pass_on(level, c, 0, (0,) * level, own)
-        keep = pltpu.make_async_copy(own, place, self.keep_sem.at[c])
+            self.across(level, c, z, (0,) * level, own=True).start()
+        keep = pltpu.make_async_copy(
+            self.own.at[pl.ds(c * self.rows, self.rows)], self.block(c, z, ()), self.keep_sem.at[c]
+        )
         keep.start()
         self.keeps.append(keep)
 
-    def forward(self, c):
-        for s in (1, 2, 3):
-            self.over_z[c, s].wait_recv()
-            for level in range(len(self.axes)):
-                self.pass_on(level, c, s, (0,) * level, None)
+    def forward(self, c, hops=(1, 2, 3)):
+        z = self.z
+        for t in hops:
+            for up in (True, False):
+
+                @pl.when((z >= t) if up else (z + t <= 3))
+                def _(t=t, up=up):
+                    w = z - t if up else z + t
+                    self.along(c, w, up).wait_recv()
+
+                    @pl.when((z < 3) if up else (z > 0))
+                    def _():
+                        self.along(c, w, up).start()
+
+                    for level in range(len(self.axes)):
+                        self.across(level, c, w, (0,) * level).start()
+
+    def flips(self, level):
+        return [tuple((i >> b) & 1 for b in range(level)) for i in range(2**level)]
 
     def spread(self, c):
         for level in range(len(self.axes) - 1):
-            for (chunk, s, flips), copy in list(self.over[level].items()):
-                if chunk == c:
-                    copy.wait_recv()
+            for s in range(4):
+                for flips in self.flips(level):
+                    w = self.z ^ s
+                    turned = flips + (1,)
+                    self.across(level, c, w, flips).wait_recv()
                     for later in range(level + 1, len(self.axes)):
-                        self.pass_on(
-                            later, c, s, flips + (1,) + (0,) * (later - level - 1), None
-                        )
+                        self.across(later, c, w, turned + (0,) * (later - level - 1)).start()
 
     def finish(self):
+        z, last = self.z, len(self.axes) - 1
         for keep in self.keeps:
             keep.wait()
-        for copy in self.over[-1].values():
-            copy.wait_recv()
-        for copies in [self.over_z] + self.over:
-            for copy in copies.values():
-                copy.wait_send()
+        for c in range(self.chunks):
+            for s in range(4):
+                for flips in self.flips(last):
+                    self.across(last, c, z ^ s, flips).wait_recv()
+                for level in range(last + 1):
+                    for flips in self.flips(level):
+                        self.across(level, c, z ^ s, flips).wait_send()
+            for t in (0, 1, 2, 3):
+                for up in (True, False):
+                    here = ((z >= t) & (z < 3)) if up else ((z + t <= 3) & (z > 0))
+
+                    @pl.when(here)
+                    def _(t=t, up=up, c=c):
+                        self.along(c, z - t if up else z + t, up).wait_send()
 
 
 VMEM_SPEC = pl.BlockSpec(memory_space=pltpu.VMEM)
@@ -899,176 +950,252 @@
     )(*inputs)
 
 
-def share_inputs(tokens, slices, wo, units):
+def share_inputs(tokens, slices, wo, marked, win, wout):
     count, own = tokens.shape[0], wo.shape[0]
-    number = units[0].shape[0]
-    columns = slices.shape[-1]
+    columns, wide = slices.shape[-1], marked.shape[-1]
+    depth, half = win.shape[1], HID // 2
+    number = 2 * win.shape[0] // 4
     chunks = 2
-
-    def kernel(ins, outs, token_refs, other):
-        tok, cut, wo_ref, unit_refs = ins[0], ins[1], ins[2], ins[3:]
-        tok_out, cut_out, wo_out, near_out, far_out = outs
-        keep, ctx_sems, exp_sems, wo_sems = other[0], other[1:3], other[3:5], other[5:7]
-        near_sems, far_sems = other[7:9], other[9:11]
+    bf16 = jnp.bfloat16
+
+    def kernel(ins, outs, token_refs, wo_refs, marked_refs, other):
+        tok, cut, wo_ref, marked_ref, win_ref, wout_ref = ins
+        tok_out, cut_out, wo_out, marked_out = outs[:4]
+        near, far = outs[4:8], outs[8:12]
+        keep, ctx_sems, exp_sems = other[0], other[1:3], other[3:5]
+        near_sems, far_sems, win_in, wout_in, unit = other[5:7], other[7:9], *other[9:12]
         z, y, x, k = (lax.axis_index(a) for a in ("z", "y", "x", "k"))
-        ctx_peers = [
-            ((z ^ s, y ^ t), s * 2 + t) for s in (3, 2, 1, 0) for t in (1, 0) if s or t
+        loads = [
+            pltpu.make_async_copy(win_ref, win_in, keep.at[1]),
+            pltpu.make_async_copy(wout_ref, wout_in, keep.at[2]),
         ]
+        for copy in loads:
+            copy.start()
         exp_peers = [((x ^ a, k ^ b), a * 2 + b) for a in (1, 0) for b in (1, 0) if a or b]
         greet(
-            [{"z": p, "y": q} for (p, q), _ in ctx_peers]
+            [{"z": p, "y": q} for p, q, _ in ctx_peers()]
             + [{"x": p, "k": q} for (p, q), _ in exp_peers]
         )
         gather = Gather(tok, tok_out, ("y",), chunks, token_refs)
+        whole = Gather(wo_ref, wo_out, ("y", "x", "k"), 1, wo_refs)
+        other_rows = Gather(marked_ref, marked_out, ("x", "k"), 1, marked_refs)
         over_ctx = [
             send(cut.at[p, q], cut_out.at[z, y, x, k], ctx_sems, i - 1, {"z": p, "y": q})
-            for (p, q), i in ctx_peers
+            for p, q, i in ctx_peers()
         ]
+        whole.start(0)
         for c in range(chunks):
             gather.start(c)
-        over_wo = [
-            send(wo_ref, wo_out.at[x, k], wo_sems, i - 1, {"x": p, "k": q})
-            for (p, q), i in exp_peers
-        ]
-        over_near, over_far = {}, []
+        other_rows.start(0)
+        copy_own = pltpu.make_async_copy(cut.at[z, y], cut_out.at[z, y, x, k], keep.at[0])
+        copy_own.start()
+
+        def over_z(i, j):
+            return pltpu.make_async_remote_copy(
+                src_ref=unit.at[i, j],
+                dst_ref=near[i].at[j],
+                send_sem=near_sems[0].at[i * number + j],
+                recv_sem=near_sems[1].at[i * number + j],
+                device_id={"z": z ^ i},
+                device_id_type=MESH,
+            )
+
+        def over_y(i, j):
+            return pltpu.make_async_remote_copy(
+                src_ref=near[i].at[j] if i else unit.at[0, j],
+                dst_ref=far[i].at[j],
+                send_sem=far_sems[0].at[i * number + j],
+                recv_sem=far_sems[1].at[i * number + j],
+                device_id={"y": 1 - y},
+                device_id_type=MESH,
+            )
+
+        def own_unit(j):
+            return pltpu.make_async_copy(unit.at[0, j], near[0].at[j], keep.at[3 + j])
+
+        def convert(j):
+            for i in range(4):
+                index = number * (z ^ i) + j
+                e, h = index // 2, lax.rem(index, 2)
+                first = pl.ds(pl.multiple_of(h * half, half), half)
+                second = pl.ds(pl.multiple_of(HID + h * half, half), half)
+                unit[i, j, :, :half] = win_in[e, :, first].astype(bf16)
+                unit[i, j, :, half : 2 * half] = win_in[e, :, second].astype(bf16)
+                unit[i, j, :, 2 * half :] = wout_in[e, :, first].astype(bf16)
+
+        def send_units(j):
+            for i in (3, 2, 1):
+                over_z(i, j).start()
+
+        def pass_units(j):
+            for i in (1, 2, 3):
+                over_z(i, j).wait_recv()
+                over_y(i, j).start()
+
+        for copy in loads:
+            copy.wait()
+        convert(0)
+        send_units(0)
         for j in range(number):
-            for i in (3, 2, 1):
-                over_near[i, j] = send(
-                    unit_refs[i].at[j],
-                    near_out.at[i - 1, j],
-                    near_sems,
-                    (i - 1) * number + j,
-                    {"z": z ^ i},
-                )
-            over_far.append(
-                send(unit_refs[0].at[j], far_out.at[0, j], far_sems, j, {"y": 1 - y})
-            )
-        keeps = [
-            pltpu.make_async_copy(cut.at[z, y], cut_out.at[z, y, x, k], keep.at[0]),
-            pltpu.make_async_copy(wo_ref, wo_out.at[x, k], keep.at[1]),
-        ]
-        for copy in keeps:
-            copy.start()
-        for copy in over_ctx:
+            if j:
+                convert(j)
+            own_unit(j).start()
+            over_y(0, j).start()
+        for t in (1, 2, 3):
+            whole.forward(0, (t,))
+            for c in range(chunks):
+                gather.forward(c, (t,))
+            other_rows.forward(0, (t,))
+            send_units(t)
+            if t == 1:
+                for copy in over_ctx:
+                    copy.wait_recv()
+                copy_own.wait()
+                mine = cut_out.at[:, :, x, k]
+                over_exp = [
+                    send(mine, mine, exp_sems, i - 1, {"x": p, "k": q})
+                    for (p, q), i in exp_peers
+                ]
+            pass_units(t - 1)
+        for j in range(4, number):
+            send_units(j)
+        whole.spread(0)
+        other_rows.spread(0)
+        for j in range(3, number):
+            pass_units(j)
+        for copy in over_exp:
             copy.wait_recv()
-        keeps[0].wait()
-        mine = cut_out.at[:, :, x, k]
-        over_exp = [
-            send(mine, mine, exp_sems, i - 1, {"x": p, "k": q}) for (p, q), i in exp_peers
-        ]
-        for c in range(chunks):
-            gather.forward(c)
+        gather.finish()
+        whole.finish()
+        other_rows.finish()
+        for copy in over_ctx + over_exp:
+            copy.wait_send()
         for j in range(number):
-            for i in (1, 2, 3):
-                over_near[i, j].wait_recv()
-                over_far.append(
-                    send(
-                        near_out.at[i - 1, j],
-                        far_out.at[i, j],
-                        far_sems,
-                        i * number + j,
-                        {"y": 1 - y},
-                    )
-                )
-        for copy in over_exp + over_wo + over_far:
-            copy.wait_recv()
-        keeps[1].wait()
-        gather.finish()
-        for copy in over_ctx + over_exp + over_wo + list(over_near.values()) + over_far:
-            copy.wait_send()
-
-    bf16 = jnp.bfloat16
-    return exchange(
+            own_unit(j).wait()
+            for i in range(4):
+                over_y(i, j).wait_recv()
+                over_y(i, j).wait_send()
+                if i:
+                    over_z(i, j).wait_send()
+
+    units = jax.ShapeDtypeStruct((number, depth, 3 * half), bf16)
+    outs = exchange(
         kernel,
         "share_inputs",
         1,
-        (tokens, slices, wo, *units),
-        [ANY_SPEC] * 7,
+        (tokens, slices, wo, marked, win, wout),
+        [ANY_SPEC] * 6,
         [
             jax.ShapeDtypeStruct((4, 2, count, D), bf16),
             jax.ShapeDtypeStruct((4, 2, 2, 2, own, columns), bf16),
-            jax.ShapeDtypeStruct((2, 2, own, D), bf16),
-            jax.ShapeDtypeStruct((3,) + units[0].shape, bf16),
-            jax.ShapeDtypeStruct((4,) + units[0].shape, bf16),
-        ],
-        [ANY_SPEC] * 5,
+            jax.ShapeDtypeStruct((4, 2, 2, 2, own, D), bf16),
+            jax.ShapeDtypeStruct((4, 2, 2, count, wide), bf16),
+        ]
+        + [units] * 8,
+        [ANY_SPEC] * 12,
         [
             Gather.scratch(("y",), chunks),
-            [pltpu.SemaphoreType.DMA((2,))]
+            Gather.scratch(("y", "x", "k"), 1),
+            Gather.scratch(("x", "k"), 1),
+            [pltpu.SemaphoreType.DMA((3 + number,))]
             + dma_pair(7)
             + dma_pair(3)
-            + dma_pair(3)
-            + dma_pair(3 * number)
-            + dma_pair(4 * number),
+            + dma_pair(4 * number)
+            + dma_pair(4 * number)
+            + [
+                pltpu.VMEM(win.shape, jnp.float32),
+                pltpu.VMEM(wout.shape, jnp.float32),
+                pltpu.VMEM((4, number, depth, 3 * half), bf16),
+            ],
         ],
     )
-
-
-def middle_step(part, tokens, marked, gain):
-    count, chunks, wide = tokens.shape[0], 4, marked.shape[-1]
+    return (*outs[:4], list(outs[4:]))
+
+
+def ctx_peers():
+    z, y = lax.axis_index("z"), lax.axis_index("y")
+    return [(z ^ (i // 2), y ^ (i % 2), i) for i in range(7, 0, -1)]
+
+
+def middle_step(heads, tokens, wo, gain):
+    count, chunks = tokens.shape[0], 4
+    width = heads.shape[-1]
     bf16, f32 = jnp.bfloat16, jnp.float32
 
-    def kernel(ins, outs, scatter_refs, hidden_refs, marked_refs, own):
-        part_ref, tok, marked_ref, gain_ref = ins
-        middle_ref, hidden_out, marked_out = outs
-        greet(z_peers() + siblings(("y", "x", "k")))
-        scatter = Scatter(part_ref, ("y",), chunks, scatter_refs)
-        hidden = Gather(own[0], hidden_out, ("x", "k"), chunks, hidden_refs)
-        other = Gather(marked_ref, marked_out, ("x", "k"), 1, marked_refs)
-        scatter.start()
-        other.start(0)
-
-        def use(c, at, total):
-            middle = tok[at, :].astype(f32) + total
+    def kernel(ins, outs, hidden_refs, other):
+        heads_ref, tok, wo_ref, gain_ref = ins
+        attended_ref, middle_ref, hidden_out = outs
+        own, sems = other[0], other[1:3]
+        z, y = lax.axis_index("z"), lax.axis_index("y")
+        greet(
+            [{"z": p, "y": q} for p, q, _ in ctx_peers()] + siblings(("x", "k"))
+        )
+        hidden = Gather(own, hidden_out, ("x", "k"), chunks, hidden_refs)
+        copies = [
+            send(heads_ref.at[p, q], attended_ref.at[z, y], sems, i - 1, {"z": p, "y": q})
+            for p, q, i in ctx_peers()
+        ]
+        attended_ref[z, y] = heads_ref[z, y]
+        for copy in copies:
+            copy.wait_recv()
+        step = count // chunks
+        for c in range(chunks):
+            at = pl.ds(c * step, step)
+            middle = tok[at, :].astype(f32)
+            for i in range(8):
+                middle = middle + jnp.dot(
+                    attended_ref[i // 2, i % 2, at, :],
+                    wo_ref[i * width : (i + 1) * width, :],
+                    preferred_element_type=f32,
+                )
             middle_ref[at, :] = middle
             scale = lax.rsqrt(jnp.mean(middle * middle, axis=-1, keepdims=True) + EPSILON)
-            own[0][at, :] = (middle * scale * gain_ref[...]).astype(bf16)
+            own[at, :] = (middle * scale * gain_ref[...]).astype(bf16)
             hidden.start(c)
-
-        scatter.run(use)
-        other.forward(0)
         for c in range(chunks):
             hidden.forward(c)
-            if c == 0:
-                other.spread(0)
             hidden.spread(c)
-        other.finish()
         hidden.finish()
-        scatter.finish()
-
-    blocks = (4, 2, 2, count)
+        for copy in copies:
+            copy.wait_send()
+
     return exchange(
         kernel,
         "middle_step",
         2,
-        (part, tokens, marked, gain),
-        [ANY_SPEC, VMEM_SPEC, ANY_SPEC, VMEM_SPEC],
+        (heads, tokens, wo, gain),
+        [VMEM_SPEC] * 4,
         [
+            jax.ShapeDtypeStruct((4, 2, count, width), bf16),
             jax.ShapeDtypeStruct((count, D), f32),
-            jax.ShapeDtypeStruct(blocks + (D,), bf16),
-            jax.ShapeDtypeStruct(blocks + (wide,), bf16),
+            jax.ShapeDtypeStruct((4, 2, 2, count, D), bf16),
         ],
-        [VMEM_SPEC, ANY_SPEC, ANY_SPEC],
+        [VMEM_SPEC, VMEM_SPEC, ANY_SPEC],
         [
-            Scatter.scratch(part, ("y",), chunks),
             Gather.scratch(("x", "k"), chunks),
-            Gather.scratch(("x", "k"), 1),
-            [pltpu.VMEM((count, D), bf16)],
+            [pltpu.VMEM((count, D), bf16)] + dma_pair(7),
         ],
     )
 
 
-def router_step(part, middle, cotangent, gates, router, gain):
+def router_step(part, middle, cotangent, gates, router, gain, wo, bulk):
     count, chunks = middle.shape[0], 4
+    width = wo.shape[0] // 8
     bf16, f32 = jnp.bfloat16, jnp.float32
 
-    def kernel(ins, outs, scatter_refs, gather_refs, own):
-        part_ref, middle_ref, up_ref, gates_ref, router_ref, gain_ref = ins
-        logit_ref, gain_out, grad_ref, branch_out = outs
-        greet(z_peers() + siblings(("y", "x", "k")))
+    def kernel(ins, outs, scatter_refs, other):
+        part_ref, middle_ref, up_ref, gates_ref, router_ref, gain_ref, wo_ref = ins[:7]
+        logit_ref, gain_out, grad_ref, heads_out = outs[:4]
+        turned, sems, bulk_sems = other[0], other[1:3], other[3:5]
+        z, y = lax.axis_index("z"), lax.axis_index("y")
+        greet([{"z": p, "y": q} for p, q, _ in ctx_peers()] + siblings(("x", "k")))
         scatter = Scatter(part_ref, ("x", "k"), chunks, scatter_refs)
-        gather = Gather(own[0], branch_out, ("y",), chunks, gather_refs)
+        copies = []
         scatter.start()
+        bulk_copies = [
+            send(a, b, bulk_sems, i, {"y": 1 - y})
+            for i, (a, b) in enumerate(zip(ins[7:], outs[4:]))
+        ]
         gain_out[...] = jnp.zeros_like(gain_out)
 
         def use(c, at, total):
@@ -1086,46 +1213,63 @@
                 scaled - normed * jnp.mean(scaled * normed, axis=-1, keepdims=True)
             )
             grad_ref[at, :] = result
-            own[0][at, :] = result.astype(bf16)
-            gather.start(c)
+            down = result.astype(bf16)
+            for i in range(8):
+                turned[i // 2, i % 2, at, :] = contract_cols(
+                    down, wo_ref[i * width : (i + 1) * width, :]
+                ).astype(bf16)
+            for p, q, i in ctx_peers():
+                copies.append(
+                    send(
+                        turned.at[p, q, at],
+                        heads_out.at[z, y, at],
+                        sems,
+                        (i - 1) * chunks + c,
+                        {"z": p, "y": q},
+                    )
+                )
+            heads_out[z, y, at, :] = turned[z, y, at, :]
 
         scatter.run(use)
-        for c in range(chunks):
-            gather.forward(c)
-        gather.finish()
+        for copy in copies + bulk_copies:
+            copy.wait_recv()
+        for copy in copies + bulk_copies:
+            copy.wait_send()
         scatter.finish()
 
     return exchange(
         kernel,
         "router_step",
         3,
-        (part, middle, cotangent, gates, router, gain),
-        [ANY_SPEC] + [VMEM_SPEC] * 5,
+        (part, middle, cotangent, gates, router, gain, wo, *bulk),
+        [ANY_SPEC] + [VMEM_SPEC] * 6 + [ANY_SPEC] * len(bulk),
         [
             jax.ShapeDtypeStruct((count, 128), bf16),
             jax.ShapeDtypeStruct((1, D), f32),
             jax.ShapeDtypeStruct((count, D), f32),
-            jax.ShapeDtypeStruct((4, 2, count, D), bf16),
-        ],
-        [VMEM_SPEC] * 3 + [ANY_SPEC],
+            jax.ShapeDtypeStruct((4, 2, count, width), bf16),
+        ]
+        + [jax.ShapeDtypeStruct(a.shape, a.dtype) for a in bulk],
+        [VMEM_SPEC] * 4 + [ANY_SPEC] * len(bulk),
         [
             Scatter.scratch(part, ("x", "k"), chunks),
-            Gather.scratch(("y",), chunks),
-            [pltpu.VMEM((count, D), bf16)],
+            [pltpu.VMEM((4, 2, count, width), bf16)] + dma_pair(7 * chunks) + dma_pair(len(bulk)),
         ],
     )
 
 
-def last_step(part, mixed, tokens, middle, grad_middle, gain, qkv_part, wo_part, small_part):
+def last_step(
+    part, mixed, tokens, middle, grad_middle, gain, qkv_part, wo_part, small_part, bulk
+):
     count, chunks = tokens.shape[0], 4
     own, columns = qkv_part.shape[-2:]
     bf16, f32 = jnp.bfloat16, jnp.float32
 
-    def kernel(ins, outs, part_refs, mixed_refs, other):
-        part_ref, mixed_ref, tok, middle_ref, grad_ref, gain_ref, qkv, wo, small = ins
-        out_ref, tokens_ref, qkv_out, wo_out, small_out = outs
-        qkv_came, qkv_sum, wo_came, small_came = other[:4]
-        sems = [other[4 + 2 * i : 6 + 2 * i] for i in range(4)]
+    def kernel(ins, outs, part_refs, mixed_refs, wo_refs, other):
+        part_ref, mixed_ref, tok, middle_ref, grad_ref, gain_ref, qkv, wo, small = ins[:9]
+        out_ref, tokens_ref, qkv_out, wo_out, small_out = outs[:5]
+        qkv_came, qkv_sum, small_came = other[:3]
+        sems = [other[3 + 2 * i : 5 + 2 * i] for i in range(4)]
         names = ("z", "y", "x", "k")
         z, y, x, k = (lax.axis_index(a) for a in names)
         everyone = [
@@ -1138,17 +1282,14 @@
         greet([place(p) for p, _ in everyone])
         first = Scatter(part_ref, ("y",), chunks, part_refs)
         second = Scatter(mixed_ref, ("x", "k"), chunks, mixed_refs)
+        third = Scatter(wo, ("y", "x", "k"), 1, wo_refs)
         first.start()
         second.start()
+        third.start()
         over_qkv = [
             send(qkv.at[p[2], p[3]], qkv_came.at[i - 1], sems[0], i - 1, place(p))
             for p, i in of_exp
         ]
-        over_wo = [
-            send(wo.at[p[2], p[3]], wo_came.at[i - 1], sems[1], i - 1, place(p))
-            for p, i in of_exp
-        ]
-
         def use_first(c, at, total):
             resid = tok[at, :].astype(f32)
             scale = lax.rsqrt(jnp.mean(resid * resid, axis=-1, keepdims=True) + EPSILON)
@@ -1158,68 +1299,95 @@
                 scaled - normed * jnp.mean(scaled * normed, axis=-1, keepdims=True)
             )
 
+        def use_third(c, at, total):
+            wo_out[at, :] = total
+
         def use_second(c, at, total):
             out_ref[at, :] = (middle_ref[at, :] + total).astype(bf16)
 
-        first.run(use_first)
-        total = qkv[x, k].astype(f32)
-        for copy, (_, i) in zip(over_qkv, of_exp):
-            copy.wait_recv()
-            total = total + qkv_came[i - 1].astype(f32)
-        qkv_sum[...] = total.astype(bf16)
-        qkv_out[z, y] = qkv_sum[z, y]
-        over_ctx = [
-            send(qkv_sum.at[p[0], p[1]], qkv_out.at[z, y], sems[2], i - 1, place(p))
-            for p, i in of_ctx
-        ]
-        over_small = [
-            send(small.at[p], small_came.at[i - 1], sems[3], i - 1, place(p)) for p, i in everyone
-        ]
-        second.run(use_second)
-        total = wo[x, k].astype(f32)
-        for copy, (_, i) in zip(over_wo, of_exp):
-            copy.wait_recv()
-            total = total + wo_came[i - 1].astype(f32)
-        wo_out[...] = total
+        number = bulk[0].shape[0]
+        waiting = [(i, j) for j in range(number) for i in (0, 1, 2)]
+        over = [{"z": z ^ 2}, {"z": z ^ 1}, {"y": 1 - y}]
+        over_bulk = []
+
+        def send_bulk(most):
+            for i, j in waiting[:most]:
+                over_bulk.append(
+                    send(
+                        ins[9 + i].at[j],
+                        outs[5 + i].at[j],
+                        sems[3],
+                        i * number + j,
+                        over[i],
+                    )
+                )
+            del waiting[:most]
+
+        for step in range(second.length()):
+            second.advance(step, use_second)
+            if step < first.length():
+                first.advance(step, use_first)
+            if step < third.length():
+                third.advance(step, use_third)
+            if step == 1:
+                total = qkv[x, k].astype(f32)
+                for copy, (_, i) in zip(over_qkv, of_exp):
+                    copy.wait_recv()
+                    total = total + qkv_came[i - 1].astype(f32)
+                qkv_sum[...] = total.astype(bf16)
+                qkv_out[z, y] = qkv_sum[z, y]
+                over_ctx = [
+                    send(qkv_sum.at[p[0], p[1]], qkv_out.at[z, y], sems[1], i - 1, place(p))
+                    for p, i in of_ctx
+                ]
+                over_small = [
+                    send(small.at[p], small_came.at[i - 1], sems[2], i - 1, place(p))
+                    for p, i in everyone
+                ]
+            if step >= 2:
+                send_bulk(3)
+        send_bulk(len(waiting))
         total = small[z, y, x, k].astype(f32)
         for copy, (_, i) in zip(over_small, everyone):
             copy.wait_recv()
             total = total + small_came[i - 1].astype(f32)
         small_out[...] = total
-        for copy in over_ctx:
+        for copy in over_ctx + over_bulk:
             copy.wait_recv()
         first.finish()
         second.finish()
-        for copy in over_qkv + over_wo + over_ctx + over_small:
+        third.finish()
+        for copy in over_qkv + over_ctx + over_small + over_bulk:
             copy.wait_send()
 
     return exchange(
         kernel,
         "last_step",
         4,
-        (part, mixed, tokens, middle, grad_middle, gain, qkv_part, wo_part, small_part),
-        [ANY_SPEC] * 2 + [VMEM_SPEC] * 7,
+        (part, mixed, tokens, middle, grad_middle, gain, qkv_part, wo_part, small_part, *bulk),
+        [ANY_SPEC] * 2 + [VMEM_SPEC] * 5 + [ANY_SPEC, VMEM_SPEC] + [ANY_SPEC] * len(bulk),
         [
             jax.ShapeDtypeStruct((count, D), bf16),
             jax.ShapeDtypeStruct((count, D), f32),
             jax.ShapeDtypeStruct((4, 2, own, columns), bf16),
             jax.ShapeDtypeStruct((own, D), f32),
             jax.ShapeDtypeStruct((own, 128), f32),
-        ],
-        [VMEM_SPEC] * 5,
+        ]
+        + [jax.ShapeDtypeStruct(a.shape, a.dtype) for a in bulk],
+        [VMEM_SPEC] * 5 + [ANY_SPEC] * len(bulk),
         [
             Scatter.scratch(part, ("y",), chunks),
             Scatter.scratch(mixed, ("x", "k"), chunks),
+            Scatter.scratch(wo_part, ("y", "x", "k"), 1),
             [
                 pltpu.VMEM((3, 4, 2, own, columns), bf16),
                 pltpu.VMEM((4, 2, own, columns), bf16),
-                pltpu.VMEM((3, own, D), bf16),
                 pltpu.VMEM((31, own, 128), bf16),
             ]
             + dma_pair(3)
-            + dma_pair(3)
             + dma_pair(7)
-            + dma_pair(31),
+            + dma_pair(31)
+            + dma_pair(len(bulk) * bulk[0].shape[0]),
         ],
     )
 
@@ -1262,7 +1430,8 @@
     wout = expert_out.transpose(1, 0, 2)
     swap_z = [[(i, i ^ s) for i in range(n_z)] for s in range(n_z)]
     swap_y = [(i, i ^ 1) for i in range(n_y)]
-    near = [take_units(units * (z_index ^ s), units, win, wout) for s in range(4)]
+    swap_z = [[(i, i ^ s) for i in range(n_z)] for s in range(n_z)]
+    swap_y = [(i, i ^ 1) for i in range(n_y)]
 
     wq, wk, wv = (a.astype(bf16) for a in (attn_q, attn_k, attn_v))
     own_qkv = jnp.concatenate(
@@ -1285,19 +1454,19 @@
     slices = jnp.concatenate(
         [own_qkv.transpose(1, 0, 2), jnp.broadcast_to(small, (n_ctx, own, 64))], axis=-1
     )
-    token_all, slices, wo, near_parts, far_parts = share_inputs(
-        tokens[0], slices.reshape(n_z, n_y, own, -1), attn_o.astype(bf16), near
+    marked = jnp.concatenate(
+        [cotangent[0], routes[0].astype(bf16), jnp.zeros((count, 128 - TOP), bf16)], axis=1
+    )
+    token_all, slices, wo, marked_blocks, parts = share_inputs(
+        tokens[0], slices.reshape(n_z, n_y, own, -1), attn_o.astype(bf16), marked, win, wout
     )
     token_all = token_all.reshape(group, D)
     slices = slices.reshape(D, -1)
-    wo = wo.reshape(width, D)
+    wo = wo.reshape(HEADS * HEAD, D)
     wqkv, small = slices[:, : width + 2 * HEAD], slices[:, width + 2 * HEAD :]
     weight_r = jnp.concatenate([small[:, :experts], jnp.zeros((D, 128 - experts), bf16)], axis=1)
     gain_one_f = small[:, experts].astype(f32)[None, :]
     gain_two_f = small[:, experts + 1].astype(f32)[None, :]
-    marked = jnp.concatenate(
-        [cotangent[0], routes[0].astype(bf16), jnp.zeros((count, 128 - TOP), bf16)], axis=1
-    )
 
     perm_row = span_perm[0]
     first_len = lengths[0, 0]
@@ -1331,9 +1500,8 @@
     )
     log_total = highest + jnp.log(total)
     attended_b = attended.transpose(1, 0, 2).reshape(group, width).astype(bf16)
-    branch = jnp.dot(attended_b, wo, preferred_element_type=f32).astype(bf16)
-    middle, hidden_blocks, marked_blocks = middle_step(
-        branch.reshape(n_z, n_y, count, D), tokens[0], marked, gain_two_f
+    own_attended, middle, hidden_blocks = middle_step(
+        attended_b.reshape(n_z, n_y, count, width), tokens[0], wo, gain_two_f
     )
     hidden_blocks = hidden_blocks.reshape(-1, count, D)
     marked_blocks = marked_blocks.reshape(-1, count, D + 128)
@@ -1359,30 +1527,25 @@
 
     meta = jnp.stack([shift, z_index, y_index, base]).astype(jnp.int32)
     made, back, *grads = run_experts(
-        meta, row_in, row_up, slot_gate, near[0], near_parts, far_parts
-    )
-    logit_grad, grad_gain_two, grad_middle, branch_all = router_step(
+        meta, row_in, row_up, slot_gate, parts
+    )
+    logit_grad, grad_gain_two, grad_middle, grad_heads, *others = router_step(
         to_tokens(back).reshape(n_z, 2, 2, count, D + 128),
         middle,
         cotangent[0],
         gates,
         weight_r,
         gain_two_f,
-    )
-    branch_all = branch_all.reshape(group, D)
-
-    swap_z = [[(i, i ^ s) for i in range(n_z)] for s in range(n_z)]
-    swap_y = [(i, i ^ 1) for i in range(n_y)]
-    sums = [None] * 4
-    for s in (3, 2, 1, 0):
-        other = lax.ppermute(grads[4 + s], "y", swap_y)
-        sums[s] = (grads[s].astype(f32) + other.astype(f32)).astype(bf16)
-    sums, branch_all = lax.optimization_barrier((sums, branch_all))
-    for s in (3, 2, 1):
-        sums[s] = lax.ppermute(sums[s], "z", swap_z[s])
-    grad_expert_in, grad_expert_out = place_units(z_index, jnp.concatenate(sums), units)
-    grad_expert_in = grad_expert_in.transpose(1, 0, 2)
-    grad_expert_out = grad_expert_out.transpose(1, 0, 2)
+        wo,
+        grads[6:8],
+    )
+
+    grads[5], grad_heads = lax.optimization_barrier((grads[5], grad_heads))
+    others = [grads[4], lax.ppermute(grads[5], "y", swap_y)] + others
+    add = lambda a, b: (a.astype(f32) + b.astype(f32)).astype(bf16)
+    sums = [None, None, add(grads[2], others[2]), add(grads[3], others[3])]
+    sums[3], sums[2], grad_heads = lax.optimization_barrier((sums[3], sums[2], grad_heads))
+    sums[3] = lax.ppermute(sums[3], "z", swap_z[3])
 
     hidden_two = lax.dynamic_index_in_dim(
         hidden_blocks, z_index * n_exp + exp_index, 0, keepdims=False
@@ -1396,8 +1559,13 @@
     )
     small_grads = small_grads.astype(bf16).reshape(n_z, n_y, 2, 2, own, 128)
 
-    grad_wo = contract_rows(attended_b, branch_all).astype(bf16)
-    grad_heads = contract_cols(branch_all, wo).astype(bf16).reshape(group, repeat, HEAD)
+    grad_wo = jnp.einsum(
+        "cth,td->chd",
+        own_attended.reshape(n_ctx, count, width),
+        grad_middle.astype(bf16),
+        preferred_element_type=f32,
+    ).astype(bf16)
+    grad_heads = grad_heads.reshape(group, repeat, HEAD)
     grad_heads = grad_heads.transpose(1, 0, 2)
     drift = jnp.sum(grad_heads.astype(f32) * attended, axis=-1)
     scores = (
@@ -1426,7 +1594,9 @@
     grad_hidden = contract_cols(grad_qkv, wqkv).astype(bf16).reshape(n_z, n_y, count, D)
     grad_wqkv = contract_rows(hidden_all, grad_qkv).astype(bf16)
     grad_wqkv = grad_wqkv.reshape(n_ctx, n_exp, own, width + 2 * HEAD).transpose(1, 0, 2, 3)
-    output, grad_tokens, grad_wqkv, grad_wo, small_grads = last_step(
+    sums[1] = add(grads[1], others[1])
+    grad_hidden, sums[1:] = lax.optimization_barrier((grad_hidden, sums[1:]))
+    output, grad_tokens, grad_wqkv, grad_wo, small_grads, *bulk = last_step(
         grad_hidden,
         to_tokens(made).reshape(n_z, 2, 2, count, D),
         tokens[0],
@@ -1434,9 +1604,14 @@
         grad_middle,
         gain_one_f,
         grad_wqkv.reshape(2, 2, n_z, n_y, own, width + 2 * HEAD),
-        grad_wo.reshape(2, 2, own, D),
+        grad_wo.reshape(n_z, n_y, 2, 2, own, D),
         small_grads,
-    )
+        [sums[2], sums[1], others[0]],
+    )
+    sums[2], sums[1], sums[0] = bulk[0], bulk[1], add(grads[0], bulk[2])
+    grad_expert_in, grad_expert_out = place_units(z_index, jnp.concatenate(sums), units)
+    grad_expert_in = grad_expert_in.transpose(1, 0, 2)
+    grad_expert_out = grad_expert_out.transpose(1, 0, 2)
     grad_wqkv = grad_wqkv.reshape(n_ctx, own, width + 2 * HEAD).astype(f32)
     grad_q = grad_wqkv[:, :, :width].transpose(1, 0, 2).reshape(own, HEADS * HEAD)
     grad_k = grad_wqkv[:, :, width : width + HEAD].transpose(1, 0, 2).reshape(own, KV_HEADS * HEAD)

time: 973 us -> 756 us (0.78)
  Pallas kernels: 825 us -> 618 us
    pallas_call x4, Pallas kernels: 727 us -> 539 us  [exchange(): pl.pallas_call(run, out_shape=outs, in_specs=specs, out_specs=out_specs,...]
    pallas_call x4 -> x0, Pallas kernels: 18.1 us -> none  [take_units(): pl.pallas_call(unit_kernel, grid_spec=pltpu.PrefetchScalarGridSpec(num_sc...]
  transfers between devices with their start and end apart: 7 -> 2, of which waited for: 0 -> 0; matrix products, arithmetic and copies ran while one was open for 4% -> 7% of each run, Pallas kernels for 37% -> 0%
where the time goes in v3:
time: 756 us; the launch traced here: 746 us
  Pallas kernels  618 us (82%)
  matrix products  61.2 us (8%)
  other arithmetic  39.2 us (5%)
  local copies, waits for them, and re-layouts  22.5 us (3%)
    pallas_call x4, Pallas kernels, exchange(): pl.pallas_call(run, out_shape=outs, in_specs=specs, out_specs=out_specs,...  539 us
    pallas_call x1, Pallas kernels, run_experts(): pl.pallas_call(lambda *refs: expert_kernel(depth, *refs), grid_spec=pltpu...  54.4 us
    pallas_call x1, Pallas kernels, dispatch(): pl.pallas_call(dispatch_kernel, grid_spec=pltpu.PrefetchScalarGridSpec(nu...  15.4 us
    dot_general x2, matrix products, to_tokens(): jnp.einsum('prt,prd->ptd', spread, rows.reshape(pairs, held * 2 * slots,...  15.1 us
  transfers between devices with their start and end apart: 2, of which 0 were waited for; matrix products, arithmetic and copies ran while one was open for 7% of the time, Pallas kernels for 0%

profile of v3, /device:TPU:0, one launch (start us, length us, event | category | flops | bytes accessed | tf_op | source)
XLA Modules:
  0.0 745.7 jit_solution(14171680821049558848)
XLA Ops:
  0.7 0.8 select_reduce_fusion
  1.5 0.7 broadcast_compare_fusion
  2.2 0.7 fusion.60
  2.8 0.7 convert_element_type.173
  3.6 0.7 convert_bitcast_fusion.1
  4.5 0.9 convert_element_type.171
  5.6 0.9 convert_element_type.172
  6.6 0.8 copy.67
  7.5 1.0 convert_element_type.170
  8.7 1.1 convert_element_type.176.refs_2_
  10.2 204.5 %share_inputs.1 = (bf16[4,2,128,1536]{3,2,1,0:T(8,128)(2,1)}, bf16[4,2,2,2,48,384]{5,4,3,2,1,0:T(8,128)(2,1)S(1)}, bf16[4,2,2,2,48,1536]{5,4,3,2,1,0:T(8,128)(2,...) custom-call(bf16[128,1536]{1,0:T(8,128)(2,1)S(1)} %bitcast.149, ...), custom_call_target="tpu_custom_call" | custom-call | tf_op jit(solution)/shard_map/share_inputs/pallas_call | solution.py:940
  214.8 1.2 copy-done.11
  215.9 1.2 copy-done.12
  217.8 2.7 multiply_reduce_fusion
  220.7 0.8 fusion.7
  222.0 1.2 fusion.23
  223.7 1.2 compare_and_fusion
  225.0 1.2 fusion.39
  226.3 5.9 fusion.2
  232.3 7.3 fusion.4
  239.7 7.7 %fusion.25 = (bf16[1024,3,64]{0,2,1:T(8,128)(2,1)S(1)}, f32[3,1024,64]{1,2,0:T(8,128)}) fusion(f32[1024,3]{0,1:T(4,128)S(1)} %bitcast.181, f32[1024,1024,3]{1,0,2:T(8,128)} %get-tuple-element.174, f32[3,1024]{1,0:T(4,128)S(1)} %get-tuple-element.173, pred[1024,1024]{0,1:T(8,128)(4,1)S(1)} %compare_and_fusion, f32[1024,320]{0,1:T(8,128)S(1)} %fusion.23), kind=kOutput, calls=%fused_computation.40 | convolution fusion | flops 415629312 | bytes 14974976 | tf_op jit(solution)/shard_map/rqk,kd->rqd/dot_general | solution.py:1498
  248.2 62.9 %middle_step.1 = (bf16[4,2,128,192]{3,2,1,0:T(8,128)(2,1)S(1)}, f32[128,1536]{1,0:T(8,128)S(1)}, bf16[4,2,2,128,1536]{4,3,2,1,0:T(8,128)(2,1)}) custom-call(bf16[4,2,128,192]{3,2,1,0:T(8,128)(2,1)S(1)} %copy.69.refs_0_, bf16[128,1536]{1,0:T(8,128)(2,1)S(1)} %bitcast.150, bf16[1536,1536]{1,0:T(8,128)(2,1)} %bitcast.166, f32[1,1536]{1,0:T(1,128)S(1)} %reshape.371.refs_3_.refs_5_), custom_call_target="tpu_custom_call" | custom-call | tf_op jit(solution)/shard_map/middle_step/pallas_call | solution.py:940
  311.0 0.8 copy-done.6
  311.8 15.4 %dispatch.1 = (bf16[8,3,80,1536]{3,2,1,0:T(8,128)(2,1)}, bf16[8,3,80,1536]{3,2,1,0:T(8,128)(2,1)}, f32[8,3,80,1]{3,2,1,0:T(8,128)S(1)}, bf16[8,240,256]{2,1,0:T(8,128)(2,1)S(1)}, f32[16,128,128]{2,1,0:T(8,128)S(1)}) custom-call(s32[1]{0:T(128)} %bitcast.20.base, bf16[16,128,1536]{2,1,0:T(8,128)(2,1)} %bitcast.170, bf16[16,128,1664]{2,1,0:T(8,128)(2,1)} %bitcast.172, ...), custom_call_target="tpu_custom_call" | custom-call | tf_op jit(solution)/shard_map/dispatch/pallas_call | solution.py:445
  327.2 1.0 copy-done.13
  328.2 0.6 pad_add_fusion.refs_0_
  328.8 54.4 %experts.1 = (bf16[8,3,80,1536]{3,2,1,0:T(8,128)(2,1)}, bf16[8,3,80,1664]{3,2,1,0:T(8,128)(2,1)}, bf16[5,192,768]{2,1,0:T(8,128)(2,1)}, bf16[5,192,768]{2,1,0:T(...) custom-call(s32[4]{0:T(128)} %pad_add_fusion.refs_0_, ...), custom_call_target="tpu_custom_call" | custom-call | flops 22649241600 | bytes 62914560 | tf_op jit(solution)/shard_map/experts/pallas_call | solution.py:553
  383.2 7.8 %convolution_convert_fusion = bf16[8,256,1664]{2,1,0:T(8,128)(2,1)} fusion(bf16[8,240,256]{2,1,0:T(8,128)(2,1)S(1)} %get-tuple-element.83, bf16[8,240,1664]{2,1,0:T(8,128)(2,1)} %bitcast.165), kind=kOutput, calls=%fused_computation.19 | convolution fusion | flops 1639186432 | bytes 14188544 | tf_op jit(solution)/shard_map/prt,prd->ptd/dot_general | solution.py:1520
  391.0 77.9 %router_step.1 = (bf16[128,128]{1,0:T(8,128)(2,1)S(1)}, f32[1,1536]{1,0:T(1,128)S(1)}, f32[128,1536]{1,0:T(8,128)S(1)}, bf16[4,2,128,192]{3,2,1,0:T(8,128)(2,1)S...) custom-call(bf16[4,2,2,128,1664]{4,3,2,1,0:T(8,128)(2,1)} %bitcast.163, ...), custom_call_target="tpu_custom_call" | custom-call | tf_op jit(solution)/shard_map/router_step/pallas_call | solution.py:940
  468.9 1.5 add_convert_fusion.3
  470.4 0.7 copy-done.27
  471.1 1.5 add_convert_fusion.2.refs_9_
  472.6 1.6 collective-permute-start.1
  474.2 1.4 collective-permute-start
  475.7 0.6 log_add_fusion
  477.1 0.7 copy-done.21
  477.8 1.3 multiply_reduce_fusion.1
  479.1 7.8 %fusion.19 = bf16[1024,64]{0,1:T(8,128)(2,1)S(1)} fusion(f32[1024,1024,3]{1,0,2:T(8,128)} %get-tuple-element.174, f32[3,1024]{1,0:T(4,128)} %log_add_fusion, pred[1024,1024]{0,1:T(8,128)(4,1)} %copy-done.15, bf16[1024,3,64]{0,2,1:T(8,128)(2,1)} %copy-done.21), kind=kOutput, calls=%fused_computation.34 | convolution fusion | flops 415301632 | bytes 14168064 | tf_op jit(solution)/shard_map/rqk,rqd->kd/dot_general | solution.py:1580
  487.0 7.0 multiply_convert_fusion
  494.0 2.0 fusion.15
  496.0 1.2 fusion.14
  497.3 2.2 fusion.27
  499.5 0.6 fusion.47
  501.0 1.2 convolution_convert_fusion.4
  502.2 1.6 copy.75
  503.8 1.4 copy.76
  505.2 5.0 convolution_convert_fusion.3
  510.2 1.5 concatenate.56
  511.7 1.3 pad_maximum_fusion.4.refs_8_
  513.0 4.9 convolution_convert_fusion.2
  517.9 7.3 convolution_convert_fusion.1
  525.3 2.9 add_convert_fusion.1.refs_10_
  528.2 193.3 %last_step.1 = (bf16[128,1536]{1,0:T(8,128)(2,1)S(1)}, f32[128,1536]{1,0:T(8,128)S(1)}, bf16[4,2,48,320]{3,2,1,0:T(8,128)(2,1)S(1)}, f32[48,1536]{1,0:T(8,128)S(...) custom-call(bf16[4,2,128,1536]{3,2,1,0:T(8,128)(2,1)} %bitcast.176, ...), custom_call_target="tpu_custom_call" | custom-call | tf_op jit(solution)/shard_map/last_step/pallas_call | solution.py:940
  723.1 0.7 slice_reduce_fusion
  723.8 0.7 copy.82
  724.5 0.7 reshape.368
  725.5 0.9 reshape.366
  726.4 0.7 reshape.367
  727.2 1.9 add_convert_fusion
  729.4 4.2 pad_maximum_fusion.low_ref.high_ref
  733.6 9.3 %place_units.1 = (f32[10,192,1024]{2,1,0:T(8,128)}, f32[10,192,512]{2,1,0:T(8,128)}) custom-call(s32[1]{0:T(128)} %bitcast.18.z_ref, bf16[20,192,768]{2,1,0:T(8,128)(2,1)} %pad_maximum_fusion.low_ref.high_ref, bf16[20,192,768]{2,1,0:T(8,128)(2,1)} %pad_maximum_fusion.low_ref.high_ref), custom_call_target="tpu_custom_call" | custom-call | tf_op jit(solution)/shard_map/place_units/pallas_call | solution.py:603
  742.9 0.7 copy.92
  743.7 0.9 copy.93
  744.5 0.7 copy.94
  (148 shorter events, 7.7 us)
Async XLA Ops:
  0.6 9.4 %copy-start.3 = (bf16[1,128,1536]{2,1,0:T(8,128)(2,1)S(1)}, bf16[1,128,1536]{2,1,0:T(8,128)(2,1)}, u32[]{:S(2)}) copy-start(bf16[1,128,1536]{2,1,0:T(8,128)(2,1)} %param.15) | copy-start | bytes 1179652
  0.7 9.5 %copy-start = (bf16[1,128,1536]{2,1,0:T(8,128)(2,1)S(1)}, bf16[1,128,1536]{2,1,0:T(8,128)(2,1)}, u32[]{:S(2)}) copy-start(bf16[1,128,1536]{2,1,0:T(8,128)(2,1)} %param.14) | copy-start | bytes 1179652
  5.5 209.2 %copy-start.31 = (bf16[48,8,64]{2,0,1:T(8,128)(2,1)}, bf16[48,8,64]{2,0,1:T(8,128)(2,1)S(1)}, u32[]{:S(2)}) copy-start(bf16[48,8,64]{2,0,1:T(8,128)(2,1)S(1)} %copy.64) | copy-start | bytes 147460
  6.6 3.4 copy-start.33
  8.7 1.3 copy-start.19
  214.7 1.2 copy-start.11
  215.9 1.2 copy-start.12
  217.1 3.5 copy-start.4
  217.8 2.9 copy-start.14
  220.7 1.3 copy-start.5
  222.0 1.7 copy-start.17
  223.6 16.0 %copy-start.35 = (f32[1024,320]{0,1:T(8,128)}, f32[1024,320]{0,1:T(8,128)S(1)}, u32[]{:S(2)}) copy-start(f32[1024,320]{0,1:T(8,128)S(1)} %fusion.23) | copy-start | bytes 3932164
  224.9 14.7 %copy-start.15 = (pred[1024,1024]{0,1:T(8,128)(4,1)}, pred[1024,1024]{0,1:T(8,128)(4,1)S(1)}, u32[]{:S(2)}) copy-start(pred[1024,1024]{0,1:T(8,128)(4,1)S(1)} %compare_and_fusion) | copy-start | bytes 3145732
  226.2 6.1 copy-start.29
  226.2 6.1 copy-start.42
  226.2 6.1 copy-start.44
  226.3 6.0 copy-start.36
  226.3 6.0 copy-start.38
  232.3 7.3 copy-start.46
  311.0 0.8 copy-start.6
  327.2 1.0 copy-start.13
  391.0 77.9 %copy-start.28 = (bf16[5,192,768]{2,1,0:T(8,128)(2,1)S(1)}, bf16[5,192,768]{2,1,0:T(8,128)(2,1)}, u32[]{:S(2)}) copy-start(bf16[5,192,768]{2,1,0:T(8,128)(2,1)} %get-tuple-element.82) | copy-start | bytes 4423684
  468.9 3.7 copy-start.1
  468.9 2.2 copy-start.27
  470.4 5.2 copy-start.47
  472.6 55.5 %collective-permute-start.1 = (bf16[5,192,768]{2,1,0:T(8,128)(2,1)}, bf16[5,192,768]{2,1,0:T(8,128)(2,1)}, u32[]{:S(2)}, u32[]{:S(2)}) collective-permute-start(bf16[5,192,768]{2,1,0:T(8,128)(2,1)} %add_convert_fusion.3), channel_id=1, source_target_pairs={{0,24},{8,16},{16,8},{24,0},{1,25},{9,17},{17,9},{25,1},{2,26},{10... | collective-permute-start | bytes 4423688 | tf_op jit(solution)/shard_map/ppermute | solution.py:1548
  474.2 51.0 %collective-permute-start = (bf16[5,192,768]{2,1,0:T(8,128)(2,1)}, bf16[5,192,768]{2,1,0:T(8,128)(2,1)}, u32[]{:S(2)}, u32[]{:S(2)}) collective-permute-start(bf16[5,192,768]{2,1,0:T(8,128)(2,1)} %get-tuple-element.97), channel_id=1, source_target_pairs={{0,4},{4,0},{1,5},{5,1},{2,6},{6,2},{3,7},{7,3},{8,12},{12,8},{9,1... | collective-permute-start | bytes 4423688 | tf_op jit(solution)/shard_map/ppermute | solution.py:1544
  477.1 0.7 copy-start.21
  479.1 7.8 %copy-start.16 = (pred[1024,1024]{0,1:T(8,128)(4,1)S(1)}, pred[1024,1024]{0,1:T(8,128)(4,1)}, u32[]{:S(2)}) copy-start(pred[1024,1024]{0,1:T(8,128)(4,1)} %copy-done.15) | copy-start | bytes 3145732
  479.1 7.8 %copy-start.22 = (bf16[1024,3,64]{0,2,1:T(8,128)(2,1)S(1)}, bf16[1024,3,64]{0,2,1:T(8,128)(2,1)}, u32[]{:S(2)}) copy-start(bf16[1024,3,64]{0,2,1:T(8,128)(2,1)} %copy-done.21) | copy-start | bytes 1179652
  479.1 7.8 %copy-start.52 = (f32[3,1024]{1,0:T(4,128)S(1)}, f32[3,1024]{1,0:T(4,128)}, u32[]{:S(2)}) copy-start(f32[3,1024]{1,0:T(4,128)} %log_add_fusion) | copy-start | bytes 36868
  486.9 13.3 %copy-start.54 = (bf16[1024,64]{0,1:T(8,128)(2,1)}, bf16[1024,64]{0,1:T(8,128)(2,1)S(1)}, u32[]{:S(2)}) copy-start(bf16[1024,64]{0,1:T(8,128)(2,1)S(1)} %fusion.19) | copy-start | bytes 393220
  486.9 7.0 copy-start.37
  487.0 7.0 copy-start.39
  493.9 2.1 copy-start.43
  494.0 2.0 copy-start.45
  496.0 4.0 copy-start.30
  496.0 4.0 copy-start.40
  497.2 3.7 copy-start.18
  500.0 0.6 copy-start.48
  500.0 0.6 copy-start.50
  500.2 0.7 copy-start.41
  502.1 3.0 copy-start.49
  502.2 3.0 copy-start.51
  517.9 7.3 copy-start.24
  525.3 2.9 copy-start.2
  528.2 193.4 %copy-start.20 = (bf16[48,8,192]{2,0,1:T(8,128)(2,1)S(1)}, bf16[48,8,192]{2,0,1:T(8,128)(2,1)}, u32[]{:S(2)}) copy-start(bf16[48,8,192]{2,0,1:T(8,128)(2,1)} %copy-done.19) | copy-start | bytes 442372
  528.2 193.4 %copy-start.32 = (bf16[48,8,64]{2,0,1:T(8,128)(2,1)S(1)}, bf16[48,8,64]{2,0,1:T(8,128)(2,1)}, u32[]{:S(2)}) copy-start(bf16[48,8,64]{2,0,1:T(8,128)(2,1)} %copy-done.31) | copy-start | bytes 147460
  528.2 193.4 %copy-start.34 = (bf16[48,8,64]{2,0,1:T(8,128)(2,1)S(1)}, bf16[48,8,64]{2,0,1:T(8,128)(2,1)}, u32[]{:S(2)}) copy-start(bf16[48,8,64]{2,0,1:T(8,128)(2,1)} %copy-done.33) | copy-start | bytes 147460
  721.6 0.7 copy-start.7
  721.6 0.8 copy-start.9
  721.6 0.9 copy-start.53
  721.6 5.5 copy-start.23
  727.2 1.9 copy-start.25
  727.2 2.3 copy-start.26
  733.6 9.3 %copy-start.8 = (bf16[128,1536]{1,0:T(8,128)(2,1)S(1)}, bf16[128,1536]{1,0:T(8,128)(2,1)}, u32[]{:S(2)}) copy-start(bf16[128,1536]{1,0:T(8,128)(2,1)} %copy-done.7) | copy-start | bytes 1179652
  733.6 11.0 %copy-start.10 = (f32[48,1536]{1,0:T(8,128)S(1)}, f32[48,1536]{1,0:T(8,128)}, u32[]{:S(2)}) copy-start(f32[48,1536]{1,0:T(8,128)} %copy-done.9) | copy-start | bytes 884740

commit v4 on v3

--- a/solution.py
+++ b/solution.py
@@ -484,7 +484,7 @@
     first = jnp.logical_or(j == 0, lax.rem(j + shift, 2) == 0)
     keep = jnp.where(first, 0.0, 1.0)
     pairs, _, rows, _ = x_ref.shape
-    step = 2
+    step = 4
 
     def forward(i, carry):
         at = pl.ds(i * step, step)
@@ -528,15 +528,17 @@
 
     lax.fori_loop(0, pairs // step, forward, 0)
 
+    wide = D // 2
+
     def gradient(i, carry):
-        at = pl.ds(pl.multiple_of(i * 256, 256), 256)
-        x = x_ref[:, 0, :, at].reshape(pairs * rows, 256)
-        g = g_ref[:, 0, :, at].reshape(pairs * rows, 256)
+        at = pl.ds(pl.multiple_of(i * wide, wide), wide)
+        x = x_ref[:, 0, :, at].reshape(pairs * rows, wide)
+        g = g_ref[:, 0, :, at].reshape(pairs * rows, wide)
         weight[at, : 2 * half] = contract_rows(x, du_ref[...]).astype(bf16)
         weight[at, 2 * half :] = contract_rows(g, act_ref[...]).astype(bf16)
         return carry
 
-    lax.fori_loop(0, D // 256, gradient, 0)
+    lax.fori_loop(0, D // wide, gradient, 0)
     for out, offset in zip(outs, offsets):
         out[0] = weight[pl.ds(offset, depth), :]
 
@@ -581,34 +583,43 @@
     )(meta, row_in, row_up, slot_gate, *parts)
 
 
-def spread_kernel(z_ref, low_ref, high_ref, in_ref, out_ref):
-    half = low_ref.shape[-1] // 3
-    for h, ref in enumerate((low_ref, high_ref)):
-        for p in range(2):
-            at = p * 2 * half + h * half
-            in_ref[0, :, at : at + half] = ref[0, :, p * half : (p + 1) * half].astype(in_ref.dtype)
-        out_ref[0, :, h * half : (h + 1) * half] = ref[0, :, 2 * half :].astype(out_ref.dtype)
-
-
-def place_units(z_index, units, number):
-    depth, columns = units.shape[1:]
-
-    def pick(h):
-        def index(i, z):
-            unit = 2 * i + h
-            return ((unit // number) ^ z[0]) * number + lax.rem(unit, number), 0, 0
+def place_kernel(number, z_ref, *refs):
+    in_ref, out_ref = refs[10:]
+    half = refs[0].shape[-1] // 3
+    for h in range(2):
+        source = ((2 * pl.program_id(0) + h) // number) ^ z_ref[0]
+        first, other, *rest = refs[5 * h : 5 * h + 5]
+        for i, group in enumerate([(first, other)] + [(ref,) for ref in rest]):
+
+            @pl.when(source == i)
+            def _(h=h, group=group):
+                total = group[0][0].astype(jnp.float32)
+                for ref in group[1:]:
+                    total = total + ref[0].astype(jnp.float32)
+                in_ref[0, :, h * half : (h + 1) * half] = total[:, :half]
+                in_ref[0, :, HID + h * half : HID + (h + 1) * half] = total[:, half : 2 * half]
+                out_ref[0, :, h * half : (h + 1) * half] = total[:, 2 * half :]
+
+
+def place_units(z_index, first, other, near, mid, far):
+    number, depth, columns = first.shape
+
+    def block(i, h):
+        def index(e, z):
+            unit = 2 * e + h
+            return jnp.where((unit // number) ^ z[0] == i, lax.rem(unit, number), 0), 0, 0
 
         return pl.BlockSpec((1, depth, columns), index)
 
     return pl.pallas_call(
-        spread_kernel,
+        lambda *refs: place_kernel(number, *refs),
         grid_spec=pltpu.PrefetchScalarGridSpec(
             num_scalar_prefetch=1,
             grid=(EXP_DEV,),
-            in_specs=[pick(0), pick(1)],
+            in_specs=[block(i, h) for h in range(2) for i in (0, 0, 1, 2, 3)],
             out_specs=[
-                pl.BlockSpec((1, depth, 2 * HID), lambda i, z: (i, 0, 0)),
-                pl.BlockSpec((1, depth, HID), lambda i, z: (i, 0, 0)),
+                pl.BlockSpec((1, depth, 2 * HID), lambda e, z: (e, 0, 0)),
+                pl.BlockSpec((1, depth, HID), lambda e, z: (e, 0, 0)),
             ],
         ),
         out_shape=[
@@ -616,7 +627,7 @@
             jax.ShapeDtypeStruct((EXP_DEV, depth, HID), jnp.float32),
         ],
         name="place_units",
-    )(z_index.reshape(1), units, units)
+    )(z_index.reshape(1), *[first, other, near, mid, far] * 2)
 
 
 MESH = pl.DeviceIdType.MESH
@@ -656,8 +667,8 @@
 
 
 class Scatter:
-    def __init__(self, part, axes, chunks, refs):
-        self.part, self.axes, self.chunks = part, axes, chunks
+    def __init__(self, part, axes, chunks, refs, direct=False):
+        self.part, self.axes, self.chunks, self.direct = part, axes, chunks, direct
         depth = len(axes)
         self.own, self.came = refs[0], refs[1 : 1 + depth]
         self.sums = refs[1 + depth : 1 + 2 * depth]
@@ -740,8 +751,22 @@
     def steps(self):
         return [(3, True), (0, False), (2, True), (1, False), (1, True), (2, False)]
 
+    def over_z(self, c, s):
+        return pltpu.make_async_remote_copy(
+            src_ref=self.sums[0].at[c, self.z ^ s],
+            dst_ref=self.line.at[c, s],
+            send_sem=self.sems[-1][0].at[s * self.chunks + c],
+            recv_sem=self.sems[-1][1].at[s * self.chunks + c],
+            device_id={"z": self.z ^ s},
+            device_id_type=MESH,
+        )
+
     def relay(self, c):
         z = self.z
+        if self.direct:
+            for s in (3, 2, 1):
+                self.over_z(c, s).start()
+            return
         for w, up in self.steps():
             slot = w + 1 if up else w
 
@@ -765,6 +790,12 @@
 
     def total(self, c):
         z = self.z
+        if self.direct:
+            total = self.sums[0][c, z].astype(jnp.float32)
+            for s in (1, 2, 3):
+                self.over_z(c, s).wait_recv()
+                total = total + self.line[c, s].astype(jnp.float32)
+            return total
         self.result[...] = self.sums[0][c, z].astype(jnp.float32)
         for up in (True, False):
 
@@ -775,7 +806,7 @@
 
         return self.result[...]
 
-    lag = 2
+    lag = 1
 
     def length(self):
         return self.chunks + len(self.axes) + self.lag
@@ -801,6 +832,10 @@
         for copy in sum(self.flying, []):
             copy.wait_send()
         for c in range(self.chunks):
+            if self.direct:
+                for s in (1, 2, 3):
+                    self.over_z(c, s).wait_send()
+                continue
             for w, up in self.steps():
 
                 @pl.when((self.z < w) if up else (self.z > w))
@@ -809,8 +844,8 @@
 
 
 class Gather:
-    def __init__(self, own, out, axes, chunks, refs):
-        self.own, self.out, self.axes, self.chunks = own, out, axes, chunks
+    def __init__(self, own, out, axes, chunks, refs, direct=False):
+        self.own, self.out, self.axes, self.chunks, self.direct = own, out, axes, chunks, direct
         self.keep_sem = refs[0]
         self.sems = [refs[1 + 2 * i : 3 + 2 * i] for i in range(len(axes) + 1)]
         self.z = lax.axis_index("z")
@@ -857,9 +892,22 @@
             device_id_type=MESH,
         )
 
+    def over_z(self, c, s):
+        where = self.block(c, self.z, ())
+        return pltpu.make_async_remote_copy(
+            src_ref=self.own.at[pl.ds(c * self.rows, self.rows)],
+            dst_ref=where,
+            send_sem=self.sems[0][0].at[s * self.chunks + c],
+            recv_sem=self.sems[0][1].at[s * self.chunks + c],
+            device_id={"z": self.z ^ s},
+            device_id_type=MESH,
+        )
+
     def start(self, c):
         z = self.z
-        for up in (True, False):
+        for s in (3, 2, 1) if self.direct else ():
+            self.over_z(c, s).start()
+        for up in () if self.direct else (True, False):
 
             @pl.when((z < 3) if up else (z > 0))
             def _(up=up):
@@ -875,7 +923,11 @@
 
     def forward(self, c, hops=(1, 2, 3)):
         z = self.z
-        for t in hops:
+        for s in hops if self.direct else ():
+            self.over_z(c, s).wait_recv()
+            for level in range(len(self.axes)):
+                self.across(level, c, z ^ s, (0,) * level).start()
+        for t in () if self.direct else hops:
             for up in (True, False):
 
                 @pl.when((z >= t) if up else (z + t <= 3))
@@ -914,7 +966,9 @@
                 for level in range(last + 1):
                     for flips in self.flips(level):
                         self.across(level, c, z ^ s, flips).wait_send()
-            for t in (0, 1, 2, 3):
+            for s in (1, 2, 3) if self.direct else ():
+                self.over_z(c, s).wait_send()
+            for t in () if self.direct else (0, 1, 2, 3):
                 for up in (True, False):
                     here = ((z >= t) & (z < 3)) if up else ((z + t <= 3) & (z > 0))
 
@@ -1118,7 +1172,7 @@
 
 
 def middle_step(heads, tokens, wo, gain):
-    count, chunks = tokens.shape[0], 4
+    count, chunks = tokens.shape[0], 2
     width = heads.shape[-1]
     bf16, f32 = jnp.bfloat16, jnp.float32
 
@@ -1139,16 +1193,17 @@
         for copy in copies:
             copy.wait_recv()
         step = count // chunks
+        middle = tok[...].astype(f32)
+        for i in range(8):
+            middle = middle + jnp.dot(
+                attended_ref[i // 2, i % 2],
+                wo_ref[i * width : (i + 1) * width, :],
+                preferred_element_type=f32,
+            )
+        middle_ref[...] = middle
         for c in range(chunks):
             at = pl.ds(c * step, step)
-            middle = tok[at, :].astype(f32)
-            for i in range(8):
-                middle = middle + jnp.dot(
-                    attended_ref[i // 2, i % 2, at, :],
-                    wo_ref[i * width : (i + 1) * width, :],
-                    preferred_element_type=f32,
-                )
-            middle_ref[at, :] = middle
+            middle = middle_ref[at, :]
             scale = lax.rsqrt(jnp.mean(middle * middle, axis=-1, keepdims=True) + EPSILON)
             own[at, :] = (middle * scale * gain_ref[...]).astype(bf16)
             hidden.start(c)
@@ -1178,24 +1233,46 @@
     )
 
 
-def router_step(part, middle, cotangent, gates, router, gain, wo, bulk):
+def router_step(part, mixed, middle, cotangent, gates, router, gain, wo, bulk, added):
     count, chunks = middle.shape[0], 4
-    width = wo.shape[0] // 8
+    width, (number, depth, _) = wo.shape[0] // 8, added.shape
     bf16, f32 = jnp.bfloat16, jnp.float32
 
-    def kernel(ins, outs, scatter_refs, other):
-        part_ref, middle_ref, up_ref, gates_ref, router_ref, gain_ref, wo_ref = ins[:7]
-        logit_ref, gain_out, grad_ref, heads_out = outs[:4]
-        turned, sems, bulk_sems = other[0], other[1:3], other[3:5]
+    def kernel(ins, outs, scatter_refs, mixed_refs, other):
+        part_ref, mixed_ref, middle_ref, up_ref, gates_ref, router_ref, gain_ref, wo_ref = ins[:8]
+        logit_ref, gain_out, grad_ref, heads_out, out_ref = outs[:5]
+        turned, sems, bulk_sems, first_sems, far_sems = other[0], *(
+            other[i : i + 2] for i in (1, 3, 5, 7)
+        )
+        own_unit, came_unit, load_sem = other[9:12]
+        bulk_in, bulk_out, added_ref = ins[8:-1], outs[6:], ins[-1]
+        far_out = outs[5]
         z, y = lax.axis_index("z"), lax.axis_index("y")
+        load = pltpu.make_async_copy(added_ref, own_unit, load_sem.at[0])
+        load.start()
         greet([{"z": p, "y": q} for p, q, _ in ctx_peers()] + siblings(("x", "k")))
         scatter = Scatter(part_ref, ("x", "k"), chunks, scatter_refs)
+        mixture = Scatter(mixed_ref, ("x", "k"), chunks, mixed_refs)
         copies = []
         scatter.start()
-        bulk_copies = [
-            send(a, b, bulk_sems, i, {"y": 1 - y})
-            for i, (a, b) in enumerate(zip(ins[7:], outs[4:]))
+        mixture.start()
+        pieces = 2 * number
+        piece = lambda ref, j: ref.at[j // 2, pl.ds(j % 2 * (depth // 2), depth // 2)]
+        over_first = [
+            send(piece(bulk_in[0], j), piece(came_unit, j), first_sems, j, {"y": 1 - y})
+            for j in range(pieces)
         ]
+        over_far = []
+        bulk_copies = [send(bulk_in[1], bulk_out[0], bulk_sems, 0, {"y": 1 - y})]
+        load.wait()
+
+        def send_far(j):
+            over_first[j].wait_recv()
+            mine = piece(own_unit, j)
+            total = mine[...].astype(f32) + piece(came_unit, j)[...].astype(f32)
+            mine[...] = total.astype(bf16)
+            over_far.append(send(mine, piece(far_out, j), far_sems, j, {"z": z ^ 3}))
+
         gain_out[...] = jnp.zeros_like(gain_out)
 
         def use(c, at, total):
@@ -1213,61 +1290,76 @@
                 scaled - normed * jnp.mean(scaled * normed, axis=-1, keepdims=True)
             )
             grad_ref[at, :] = result
-            down = result.astype(bf16)
+
+        def to_heads():
+            down = grad_ref[...].astype(bf16)
             for i in range(8):
-                turned[i // 2, i % 2, at, :] = contract_cols(
+                turned[i // 2, i % 2] = contract_cols(
                     down, wo_ref[i * width : (i + 1) * width, :]
                 ).astype(bf16)
             for p, q, i in ctx_peers():
                 copies.append(
                     send(
-                        turned.at[p, q, at],
-                        heads_out.at[z, y, at],
-                        sems,
-                        (i - 1) * chunks + c,
-                        {"z": p, "y": q},
+                        turned.at[p, q], heads_out.at[z, y], sems, i - 1, {"z": p, "y": q}
                     )
                 )
-            heads_out[z, y, at, :] = turned[z, y, at, :]
-
-        scatter.run(use)
-        for copy in copies + bulk_copies:
+            heads_out[z, y] = turned[z, y]
+
+        def use_mixture(c, at, total):
+            out_ref[at, :] = (middle_ref[at, :] + total).astype(bf16)
+
+        behind = 3
+        plan = [[0], [1, 2], [3], [4], [5], [6], [7], [8], [9], []]
+        for step in range(scatter.length() + behind):
+            if step < scatter.length():
+                scatter.advance(step, use)
+            if step == scatter.length() - 1:
+                to_heads()
+            if step >= behind:
+                mixture.advance(step - behind, use_mixture)
+            for j in plan[step]:
+                send_far(j)
+        for copy in copies + bulk_copies + over_far:
             copy.wait_recv()
-        for copy in copies + bulk_copies:
+        for copy in copies + bulk_copies + over_first + over_far:
             copy.wait_send()
         scatter.finish()
+        mixture.finish()
 
     return exchange(
         kernel,
         "router_step",
         3,
-        (part, middle, cotangent, gates, router, gain, wo, *bulk),
-        [ANY_SPEC] + [VMEM_SPEC] * 6 + [ANY_SPEC] * len(bulk),
+        (part, mixed, middle, cotangent, gates, router, gain, wo, *bulk, added),
+        [ANY_SPEC] * 2 + [VMEM_SPEC] * 6 + [ANY_SPEC] * 3,
         [
             jax.ShapeDtypeStruct((count, 128), bf16),
             jax.ShapeDtypeStruct((1, D), f32),
             jax.ShapeDtypeStruct((count, D), f32),
             jax.ShapeDtypeStruct((4, 2, count, width), bf16),
+            jax.ShapeDtypeStruct((count, D), bf16),
         ]
-        + [jax.ShapeDtypeStruct(a.shape, a.dtype) for a in bulk],
-        [VMEM_SPEC] * 4 + [ANY_SPEC] * len(bulk),
+        + [jax.ShapeDtypeStruct(added.shape, bf16)] * 2,
+        [VMEM_SPEC] * 5 + [ANY_SPEC] * 2,
         [
             Scatter.scratch(part, ("x", "k"), chunks),
-            [pltpu.VMEM((4, 2, count, width), bf16)] + dma_pair(7 * chunks) + dma_pair(len(bulk)),
+            Scatter.scratch(mixed, ("x", "k"), chunks),
+            [pltpu.VMEM((4, 2, count, width), bf16)] + dma_pair(7) + dma_pair(1) + dma_pair(2 * number) * 2
+            + [pltpu.VMEM(added.shape, bf16)] * 2 + [pltpu.SemaphoreType.DMA((1,))],
         ],
     )
 
 
 def last_step(
-    part, mixed, tokens, middle, grad_middle, gain, qkv_part, wo_part, small_part, bulk
+    part, tokens, grad_middle, gain, qkv_part, wo_part, small_part, bulk
 ):
     count, chunks = tokens.shape[0], 4
     own, columns = qkv_part.shape[-2:]
     bf16, f32 = jnp.bfloat16, jnp.float32
 
-    def kernel(ins, outs, part_refs, mixed_refs, wo_refs, other):
-        part_ref, mixed_ref, tok, middle_ref, grad_ref, gain_ref, qkv, wo, small = ins[:9]
-        out_ref, tokens_ref, qkv_out, wo_out, small_out = outs[:5]
+    def kernel(ins, outs, part_refs, wo_refs, other):
+        part_ref, tok, grad_ref, gain_ref, qkv, wo, small = ins[:7]
+        tokens_ref, qkv_out, wo_out, small_out = outs[:4]
         qkv_came, qkv_sum, small_came = other[:3]
         sems = [other[3 + 2 * i : 5 + 2 * i] for i in range(4)]
         names = ("z", "y", "x", "k")
@@ -1281,10 +1373,8 @@
         place = lambda p: dict(zip(names, p))
         greet([place(p) for p, _ in everyone])
         first = Scatter(part_ref, ("y",), chunks, part_refs)
-        second = Scatter(mixed_ref, ("x", "k"), chunks, mixed_refs)
-        third = Scatter(wo, ("y", "x", "k"), 1, wo_refs)
+        third = Scatter(wo, ("y", "x", "k"), 3, wo_refs, True)
         first.start()
-        second.start()
         third.start()
         over_qkv = [
             send(qkv.at[p[2], p[3]], qkv_came.at[i - 1], sems[0], i - 1, place(p))
@@ -1302,20 +1392,17 @@
         def use_third(c, at, total):
             wo_out[at, :] = total
 
-        def use_second(c, at, total):
-            out_ref[at, :] = (middle_ref[at, :] + total).astype(bf16)
-
         number = bulk[0].shape[0]
-        waiting = [(i, j) for j in range(number) for i in (0, 1, 2)]
-        over = [{"z": z ^ 2}, {"z": z ^ 1}, {"y": 1 - y}]
+        waiting = [(i, j) for j in range(number) for i in range(len(bulk))]
+        over = [{"z": z ^ 1}, {"y": 1 - y}]
         over_bulk = []
 
         def send_bulk(most):
             for i, j in waiting[:most]:
                 over_bulk.append(
                     send(
-                        ins[9 + i].at[j],
-                        outs[5 + i].at[j],
+                        ins[7 + i].at[j],
+                        outs[4 + i].at[j],
                         sems[3],
                         i * number + j,
                         over[i],
@@ -1323,8 +1410,7 @@
                 )
             del waiting[:most]
 
-        for step in range(second.length()):
-            second.advance(step, use_second)
+        for step in range(third.length()):
             if step < first.length():
                 first.advance(step, use_first)
             if step < third.length():
@@ -1345,7 +1431,7 @@
                     for p, i in everyone
                 ]
             if step >= 2:
-                send_bulk(3)
+                send_bulk(2)
         send_bulk(len(waiting))
         total = small[z, y, x, k].astype(f32)
         for copy, (_, i) in zip(over_small, everyone):
@@ -1355,7 +1441,6 @@
         for copy in over_ctx + over_bulk:
             copy.wait_recv()
         first.finish()
-        second.finish()
         third.finish()
         for copy in over_qkv + over_ctx + over_small + over_bulk:
             copy.wait_send()
@@ -1364,21 +1449,19 @@
         kernel,
         "last_step",
         4,
-        (part, mixed, tokens, middle, grad_middle, gain, qkv_part, wo_part, small_part, *bulk),
-        [ANY_SPEC] * 2 + [VMEM_SPEC] * 5 + [ANY_SPEC, VMEM_SPEC] + [ANY_SPEC] * len(bulk),
+        (part, tokens, grad_middle, gain, qkv_part, wo_part, small_part, *bulk),
+        [ANY_SPEC] + [VMEM_SPEC] * 4 + [ANY_SPEC, VMEM_SPEC] + [ANY_SPEC] * len(bulk),
         [
-            jax.ShapeDtypeStruct((count, D), bf16),
             jax.ShapeDtypeStruct((count, D), f32),
             jax.ShapeDtypeStruct((4, 2, own, columns), bf16),
             jax.ShapeDtypeStruct((own, D), f32),
             jax.ShapeDtypeStruct((own, 128), f32),
         ]
         + [jax.ShapeDtypeStruct(a.shape, a.dtype) for a in bulk],
-        [VMEM_SPEC] * 5 + [ANY_SPEC] * len(bulk),
+        [VMEM_SPEC] * 4 + [ANY_SPEC] * len(bulk),
         [
             Scatter.scratch(part, ("y",), chunks),
-            Scatter.scratch(mixed, ("x", "k"), chunks),
-            Scatter.scratch(wo_part, ("y", "x", "k"), 1),
+            Scatter.scratch(wo_part, ("y", "x", "k"), 3),
             [
                 pltpu.VMEM((3, 4, 2, own, columns), bf16),
                 pltpu.VMEM((4, 2, own, columns), bf16),
@@ -1389,6 +1472,189 @@
             + dma_pair(31)
             + dma_pair(len(bulk) * bulk[0].shape[0]),
         ],
+    )
+
+
+def pick(rows, columns, kind, test):
+    row = lax.broadcasted_iota(jnp.int32, (rows, columns), 0)
+    column = lax.broadcasted_iota(jnp.int32, (rows, columns), 1)
+    return jnp.where(test(row, column), 1.0, 0.0).astype(kind)
+
+
+def half_swap():
+    to_first = pick(256, 256, jnp.float32, lambda r, c: (c % HEAD < HEAD // 2) & (r == c + HEAD // 2))
+    to_second = pick(
+        256, 256, jnp.float32, lambda r, c: (c % HEAD >= HEAD // 2) & (r + HEAD // 2 == c)
+    )
+    return to_second - to_first
+
+
+def twice(a):
+    return jnp.concatenate([a, a], axis=-1)
+
+
+def exact_dot(left, right):
+    return jnp.dot(
+        left, right, preferred_element_type=jnp.float32, precision=lax.Precision.HIGHEST
+    )
+
+
+def attention_forward_kernel(
+    tok, weight, gain, cosine, sine, rows, starts, key_rows, hidden, qk, keys, values, out, lse
+):
+    bf16, f32 = jnp.bfloat16, jnp.float32
+    swap = half_swap()
+    width = out.shape[-1]
+    to_keys = pick(256, 256, bf16, lambda r, c: (c < width) & (r - width == c % HEAD))
+    to_values = pick(128, 256, bf16, lambda r, c: (c < width) & (r == c % HEAD))
+    block = 256
+    steps = tok.shape[0] // block
+
+    def project(b, carry):
+        at = pl.ds(pl.multiple_of(b * block, block), block)
+        x = tok[at, :].astype(f32)
+        normed = x * lax.rsqrt(jnp.mean(x * x, axis=-1, keepdims=True) + EPSILON)
+        h = (normed * gain[...]).astype(bf16)
+        hidden[at, :] = h
+        t = jnp.dot(h, weight[...], preferred_element_type=f32)
+        u = t[:, :256]
+        turned = (u * twice(cosine[at, :]) + exact_dot(u, swap) * twice(sine[at, :])).astype(bf16)
+        qk[at, :] = turned
+        keys[at, :] = jnp.dot(turned, to_keys, preferred_element_type=f32).astype(bf16)
+        values[at, :] = jnp.dot(
+            t[:, 256:].astype(bf16), to_values, preferred_element_type=f32
+        ).astype(bf16)
+        return carry
+
+    lax.fori_loop(0, steps, project, 0)
+    head = lax.broadcasted_iota(jnp.int32, (block, 256), 1) // HEAD
+    lane = lax.broadcasted_iota(jnp.int32, (block, 128), 1)
+
+    def attend(b, carry):
+        at = pl.ds(pl.multiple_of(b * block, block), block)
+        mask = (key_rows[...] <= rows[at, :]) & (key_rows[...] >= starts[at, :])
+        result = jnp.zeros((block, 256), f32)
+        logs = jnp.zeros((block, 128), f32)
+        for h in range(HEADS // KV_HEADS):
+            query = jnp.where(head == h, qk[at, :], jnp.zeros((), bf16))
+            scores = contract_cols(query, keys[...]) * HEAD ** (-0.5)
+            scores = jnp.where(mask, scores, NEGATIVE)
+            top = jnp.max(scores, axis=-1, keepdims=True)
+            weights = jnp.exp(scores - top)
+            total = jnp.sum(weights, axis=-1, keepdims=True)
+            mixed = jnp.dot(weights.astype(bf16), values[...], preferred_element_type=f32)
+            result = jnp.where(head == h, mixed / total, result)
+            logs = jnp.where(lane == h, top + jnp.log(total), logs)
+        out[at, :] = result[:, :width].astype(bf16)
+        lse[at, :] = logs
+        return carry
+
+    lax.fori_loop(0, steps, attend, 0)
+
+
+def attention_forward(tokens, weight, gain, cosine, sine, rows, starts):
+    count, width = tokens.shape[0], HEADS // KV_HEADS * HEAD
+    bf16, f32 = jnp.bfloat16, jnp.float32
+    shape = jax.ShapeDtypeStruct
+    return pl.pallas_call(
+        attention_forward_kernel,
+        in_specs=[VMEM_SPEC] * 8,
+        out_specs=[VMEM_SPEC] * 6,
+        out_shape=[shape((count, D), bf16)]
+        + [shape((count, 256), bf16)] * 3
+        + [shape((count, width), bf16), shape((count, 128), f32)],
+        compiler_params=pltpu.CompilerParams(vmem_limit_bytes=48 * 2**20),
+        name="attention_forward",
+    )(tokens, weight, gain, cosine, sine, rows[:, None], starts[:, None], rows[None, :])
+
+
+def attention_backward_kernel(
+    hidden, qk, keys, values, lse, upstream, weight, cosine, sine, rows, starts, key_rows,
+    weight_grad, hidden_grad, grads, query_grad, key_grad, value_grad, up
+):
+    bf16, f32 = jnp.bfloat16, jnp.float32
+    width = upstream.shape[-1]
+    scale = HEAD ** (-0.5)
+    block = 256
+    steps = hidden.shape[0] // block
+    head = lax.broadcasted_iota(jnp.int32, (block, 256), 1) // HEAD
+    lane = lax.broadcasted_iota(jnp.int32, (block, 128), 1)
+    up[...] = jnp.zeros_like(up)
+    up[:, :width] = upstream[...]
+    key_grad[...] = jnp.zeros_like(key_grad)
+    value_grad[...] = jnp.zeros_like(value_grad)
+
+    def attend(b, carry):
+        at = pl.ds(pl.multiple_of(b * block, block), block)
+        mask = (key_rows[...] <= rows[at, :]) & (key_rows[...] >= starts[at, :])
+        logs = lse[at, :]
+        result = jnp.zeros((block, 256), f32)
+        for h in range(HEADS // KV_HEADS):
+            zero = jnp.zeros((), bf16)
+            query = jnp.where(head == h, qk[at, :], zero)
+            grad = jnp.where(head == h, up[at, :], zero)
+            log = jnp.sum(jnp.where(lane == h, logs, 0.0), axis=-1, keepdims=True)
+            scores = contract_cols(query, keys[...]) * scale
+            weights = jnp.where(mask, jnp.exp(scores - log), 0.0)
+            prob_grad = contract_cols(grad, values[...])
+            drift = jnp.sum(weights * prob_grad, axis=-1, keepdims=True)
+            score_grad = (weights * (prob_grad - drift)).astype(bf16)
+            part = jnp.dot(score_grad, keys[...], preferred_element_type=f32)
+            result = jnp.where(head == h, part, result)
+            key_grad[...] += contract_rows(score_grad, query)
+            value_grad[...] += contract_rows(weights.astype(bf16), grad)
+        query_grad[at, :] = result
+        return carry
+
+    lax.fori_loop(0, steps, attend, 0)
+    swap = half_swap()
+    from_keys = pick(256, 256, f32, lambda r, c: (r < width) & (c - width == r % HEAD))
+    from_values = pick(256, 128, f32, lambda r, c: (r < width) & (c == r % HEAD))
+
+    def turn(b, carry):
+        at = pl.ds(pl.multiple_of(b * block, block), block)
+        t = jnp.where(head < HEADS // KV_HEADS, query_grad[at, :], 0.0)
+        t = (t + exact_dot(key_grad[at, :], from_keys)) * scale
+        grads[at, :256] = (
+            t * twice(cosine[at, :]) - exact_dot(t, swap) * twice(sine[at, :])
+        ).astype(bf16)
+        grads[at, 256:] = exact_dot(value_grad[at, :], from_values).astype(bf16)
+        hidden_grad[at, :] = contract_cols(grads[at, :], weight[...]).astype(bf16)
+        return carry
+
+    lax.fori_loop(0, steps, turn, 0)
+    parts, places, own, columns = weight_grad.shape
+    for i in range(places // 2):
+        deep = 2 * parts * own
+        part = contract_rows(hidden[:, i * deep : (i + 1) * deep], grads[...]).astype(bf16)
+        for j in range(2 * parts):
+            weight_grad[j % parts, 2 * i + j // parts] = part[j * own : (j + 1) * own, :columns]
+
+
+def attention_backward(hidden, qk, keys, values, lse, upstream, weight, cosine, sine, rows, starts, own):
+    count = hidden.shape[0]
+    bf16, f32 = jnp.bfloat16, jnp.float32
+    shape = jax.ShapeDtypeStruct
+    return pl.pallas_call(
+        attention_backward_kernel,
+        in_specs=[VMEM_SPEC] * 12,
+        out_specs=[VMEM_SPEC] * 2,
+        out_shape=[
+            shape((4, D // own // 4, own, upstream.shape[-1] + 2 * HEAD), bf16),
+            shape((count, D), bf16),
+        ],
+        scratch_shapes=[
+            pltpu.VMEM((count, 384), bf16),
+            pltpu.VMEM((count, 256), f32),
+            pltpu.VMEM((count, 256), f32),
+            pltpu.VMEM((count, 256), f32),
+            pltpu.VMEM((count, 256), bf16),
+        ],
+        compiler_params=pltpu.CompilerParams(vmem_limit_bytes=48 * 2**20),
+        name="attention_backward",
+    )(
+        hidden, qk, keys, values, lse, upstream, weight, cosine, sine,
+        rows[:, None], starts[:, None], rows[None, :],
     )
 
 
@@ -1463,7 +1729,7 @@
     token_all = token_all.reshape(group, D)
     slices = slices.reshape(D, -1)
     wo = wo.reshape(HEADS * HEAD, D)
-    wqkv, small = slices[:, : width + 2 * HEAD], slices[:, width + 2 * HEAD :]
+    small = slices[:, width + 2 * HEAD :]
     weight_r = jnp.concatenate([small[:, :experts], jnp.zeros((D, 128 - experts), bf16)], axis=1)
     gain_one_f = small[:, experts].astype(f32)[None, :]
     gain_two_f = small[:, experts + 1].astype(f32)[None, :]
@@ -1471,35 +1737,15 @@
     perm_row = span_perm[0]
     first_len = lengths[0, 0]
     rows = global_rows(perm_row, jnp.arange(group, dtype=jnp.int32))
-    position = rows - jnp.where(rows >= first_len, first_len, 0)
-    freqs = jnp.exp(jnp.arange(HEAD // 2, dtype=f32) * (-2.0 * math.log(10000.0) / HEAD))
-    angle = position.astype(f32)[:, None] * freqs[None, :]
-    cosine, sine = (jnp.cos(angle), jnp.sin(angle))
-    resid_all = token_all.astype(f32)
-    normed_all = resid_all * lax.rsqrt(
-        jnp.mean(resid_all * resid_all, axis=-1, keepdims=True) + EPSILON
-    )
-    hidden_all = (normed_all * gain_one_f).astype(bf16)
-    qkv = jnp.dot(hidden_all, wqkv, preferred_element_type=f32)
-    queries = rotate(
-        qkv[:, :width].reshape(group, repeat, HEAD), cosine[:, None], sine[:, None]
-    ).astype(bf16)
-    keys = rotate(qkv[:, width : width + HEAD], cosine, sine).astype(bf16)
-    values = qkv[:, width + HEAD :].astype(bf16)
-    mask = allowed(rows, rows, first_len)[None]
-    scores = (
-        jnp.einsum("qrd,kd->rqk", queries, keys, preferred_element_type=f32) * softmax_scale
-    )
-    scores = jnp.where(mask, scores, NEGATIVE)
-    highest = jnp.max(scores, axis=-1)
-    weights = jnp.exp(scores - highest[..., None])
-    total = jnp.sum(weights, axis=-1)
-    attended = (
-        jnp.einsum("rqk,kd->rqd", weights.astype(bf16), values, preferred_element_type=f32)
-        / total[..., None]
-    )
-    log_total = highest + jnp.log(total)
-    attended_b = attended.transpose(1, 0, 2).reshape(group, width).astype(bf16)
+    starts = jnp.where(rows >= first_len, first_len, 0)
+    freqs = jnp.exp(
+        (jnp.arange(128) % (HEAD // 2)).astype(f32) * (-2.0 * math.log(10000.0) / HEAD)
+    )
+    angle = (rows - starts).astype(f32)[:, None] * freqs[None, :]
+    cosine, sine = jnp.cos(angle), jnp.sin(angle)
+    hidden_all, queries, keys, values, attended_b, log_total = attention_forward(
+        token_all, slices, gain_one_f, cosine, sine, rows, starts
+    )
     own_attended, middle, hidden_blocks = middle_step(
         attended_b.reshape(n_z, n_y, count, width), tokens[0], wo, gain_two_f
     )
@@ -1529,23 +1775,24 @@
     made, back, *grads = run_experts(
         meta, row_in, row_up, slot_gate, parts
     )
-    logit_grad, grad_gain_two, grad_middle, grad_heads, *others = router_step(
+    logit_grad, grad_gain_two, grad_middle, grad_heads, output, far_sum, other = router_step(
         to_tokens(back).reshape(n_z, 2, 2, count, D + 128),
+        to_tokens(made).reshape(n_z, 2, 2, count, D),
         middle,
         cotangent[0],
         gates,
         weight_r,
         gain_two_f,
         wo,
-        grads[6:8],
-    )
-
-    grads[5], grad_heads = lax.optimization_barrier((grads[5], grad_heads))
-    others = [grads[4], lax.ppermute(grads[5], "y", swap_y)] + others
+        [grads[7], grads[6]],
+        grads[3],
+    )
+
     add = lambda a, b: (a.astype(f32) + b.astype(f32)).astype(bf16)
-    sums = [None, None, add(grads[2], others[2]), add(grads[3], others[3])]
-    sums[3], sums[2], grad_heads = lax.optimization_barrier((sums[3], sums[2], grad_heads))
-    sums[3] = lax.ppermute(sums[3], "z", swap_z[3])
+    sums = [None, None, add(grads[2], other), far_sum]
+    sums[2], grads[5], grad_heads = lax.optimization_barrier((sums[2], grads[5], grad_heads))
+    sums[2] = lax.ppermute(sums[2], "z", swap_z[2])
+    other = lax.ppermute(grads[5], "y", swap_y)
 
     hidden_two = lax.dynamic_index_in_dim(
         hidden_blocks, z_index * n_exp + exp_index, 0, keepdims=False
@@ -1565,51 +1812,36 @@
         grad_middle.astype(bf16),
         preferred_element_type=f32,
     ).astype(bf16)
-    grad_heads = grad_heads.reshape(group, repeat, HEAD)
-    grad_heads = grad_heads.transpose(1, 0, 2)
-    drift = jnp.sum(grad_heads.astype(f32) * attended, axis=-1)
-    scores = (
-        jnp.einsum("qrd,kd->rqk", queries, keys, preferred_element_type=f32) * softmax_scale
-    )
-    weights = jnp.where(mask, jnp.exp(scores - log_total[..., None]), 0.0)
-    prob_grad = jnp.einsum("rqd,kd->rqk", grad_heads, values, preferred_element_type=f32)
-    score_grad = (weights * (prob_grad - drift[..., None])).astype(bf16)
-    query_grad = (
-        jnp.einsum("rqk,kd->qrd", score_grad, keys, preferred_element_type=f32) * softmax_scale
-    )
-    value_grad = jnp.einsum(
-        "rqk,rqd->kd", weights.astype(bf16), grad_heads, preferred_element_type=f32
-    )
-    key_grad = (
-        jnp.einsum("rqk,qrd->kd", score_grad, queries, preferred_element_type=f32) * softmax_scale
-    )
-    grad_qkv = jnp.concatenate(
-        [
-            rotate(query_grad, cosine[:, None], -sine[:, None]).reshape(group, width),
-            rotate(key_grad, cosine, -sine),
-            value_grad,
-        ],
-        axis=-1,
-    ).astype(bf16)
-    grad_hidden = contract_cols(grad_qkv, wqkv).astype(bf16).reshape(n_z, n_y, count, D)
-    grad_wqkv = contract_rows(hidden_all, grad_qkv).astype(bf16)
-    grad_wqkv = grad_wqkv.reshape(n_ctx, n_exp, own, width + 2 * HEAD).transpose(1, 0, 2, 3)
-    sums[1] = add(grads[1], others[1])
-    grad_hidden, sums[1:] = lax.optimization_barrier((grad_hidden, sums[1:]))
-    output, grad_tokens, grad_wqkv, grad_wo, small_grads, *bulk = last_step(
+    grad_wqkv, grad_hidden = attention_backward(
+        hidden_all,
+        queries,
+        keys,
+        values,
+        log_total,
+        grad_heads.reshape(group, width),
+        slices,
+        cosine,
+        sine,
+        rows,
+        starts,
+        own,
+    )
+    grad_hidden = grad_hidden.reshape(n_z, n_y, count, D)
+    sums[1] = add(grads[1], other)
+    sums[1], grad_hidden = lax.optimization_barrier((sums[1], grad_hidden))
+    grad_tokens, grad_wqkv, grad_wo, small_grads, *bulk = last_step(
         grad_hidden,
-        to_tokens(made).reshape(n_z, 2, 2, count, D),
         tokens[0],
-        middle,
         grad_middle,
         gain_one_f,
         grad_wqkv.reshape(2, 2, n_z, n_y, own, width + 2 * HEAD),
         grad_wo.reshape(n_z, n_y, 2, 2, own, D),
         small_grads,
-        [sums[2], sums[1], others[0]],
-    )
-    sums[2], sums[1], sums[0] = bulk[0], bulk[1], add(grads[0], bulk[2])
-    grad_expert_in, grad_expert_out = place_units(z_index, jnp.concatenate(sums), units)
+        [sums[1], grads[4]],
+    )
+    grad_expert_in, grad_expert_out = place_units(
+        z_index, grads[0], bulk[1], bulk[0], sums[2], sums[3]
+    )
     grad_expert_in = grad_expert_in.transpose(1, 0, 2)
     grad_expert_out = grad_expert_out.transpose(1, 0, 2)
     grad_wqkv = grad_wqkv.reshape(n_ctx, own, width + 2 * HEAD).astype(f32)

time: 756 us -> 694 us (0.918)
  matrix products: 61.2 us -> 17.2 us
  other arithmetic: 39.2 us -> 15.9 us
    pallas_call x1 -> x3, Pallas kernels: 9.32 us -> 52.8 us  [the longest x1 24.7 us: attention_backward(): pl.pallas_call(attention_backward_kernel, in_specs=[VMEM_SPEC] * 12, out_...]
    dot_general x8 -> x0, matrix products: 37.8 us -> none  [the longest x1 7.75 us: body_heads(): jnp.einsum('rqk,rqd->kd', weights.astype(bf16), grad_heads, preferred_ele...]
    pallas_call x4, Pallas kernels: 539 us -> 512 us  [exchange(): pl.pallas_call(run, out_shape=outs, in_specs=specs, out_specs=out_specs,...]
    pallas_call x1, Pallas kernels: 54.4 us -> 40.8 us  [run_experts(): pl.pallas_call(lambda *refs: expert_kernel(depth, *refs), grid_spec=pltpu...]
    reduce_sum x3 -> x0, other arithmetic: 11.3 us -> none  [the longest x1 7.31 us: body_heads(): total = jnp.sum(weights, axis=-1)]
    unnamed x115 -> x87, local copies, waits for them, and re-layouts: 11.9 us -> 20.1 us
  transfers between devices with their start and end apart: 2 -> 2, of which waited for: 0 -> 0; matrix products, arithmetic and copies ran while one was open for 7% -> 2% of each run, Pallas kernels for 0% -> 19%
where the time goes in v4:
time: 694 us; the launch traced here: 686 us
  Pallas kernels  621 us (89%)
  local copies, waits for them, and re-layouts  27.2 us (4%)
  matrix products  17.2 us (2%)
  other arithmetic  15.9 us (2%)
    pallas_call x4, Pallas kernels, exchange(): pl.pallas_call(run, out_shape=outs, in_specs=specs, out_specs=out_specs,...  512 us
    pallas_call x1, Pallas kernels, run_experts(): pl.pallas_call(lambda *refs: expert_kernel(depth, *refs), grid_spec=pltpu...  40.8 us
    pallas_call x1, Pallas kernels, attention_backward(): pl.pallas_call(attention_backward_kernel, in_specs=[VMEM_SPEC] * 12, out_...  24.7 us
    unnamed x87, local copies, waits for them, and re-layouts  20.1 us
    pallas_call x1, Pallas kernels, attention_forward(): pl.pallas_call(attention_forward_kernel, in_specs=[VMEM_SPEC] * 8, out_sp...  16.5 us
    pallas_call x1, Pallas kernels, dispatch(): pl.pallas_call(dispatch_kernel, grid_spec=pltpu.PrefetchScalarGridSpec(nu...  15.4 us
  transfers between devices with their start and end apart: 2, of which 0 were waited for; matrix products, arithmetic and copies ran while one was open for 2% of the time, Pallas kernels for 19%

profile of v4, /device:TPU:0, one launch (start us, length us, event | category | flops | bytes accessed | tf_op | source)
XLA Modules:
  0.0 685.8 jit_solution(14614116759285132411)
XLA Ops:
  0.7 0.8 convert_element_type.115
  1.6 0.7 convert_bitcast_fusion.1
  2.4 0.9 convert_element_type.113
  3.3 0.1 reshape.233
  3.5 0.9 convert_element_type.114
  4.6 0.8 copy.51
  5.4 1.0 convert_element_type.112
  6.4 0.2 reshape.232
  6.6 1.0 convert_element_type.118.refs_2_
  7.6 0.1 fusion.10
  8.1 204.5 %share_inputs.1 = (bf16[4,2,128,1536]{3,2,1,0:T(8,128)(2,1)}, bf16[4,2,2,2,48,384]{5,4,3,2,1,0:T(8,128)(2,1)S(1)}, bf16[4,2,2,2,48,1536]{5,4,3,2,1,0:T(8,128)(2,...) custom-call(bf16[128,1536]{1,0:T(8,128)(2,1)S(1)} %bitcast.77, ...), custom_call_target="tpu_custom_call" | custom-call | tf_op jit(solution)/shard_map/share_inputs/pallas_call | solution.py:994
  212.6 1.1 copy-done.27
  213.7 1.1 copy-done.28
  214.9 0.5 convert_reduce_fusion
  215.4 0.2 slice.47
  215.8 0.2 copy.52
  216.0 0.1 compare_select_fusion
  216.2 0.8 concatenate.28.router_ref.refs_5_
  217.0 1.9 multiply_sine_fusion
  218.9 16.5 %attention_forward.1 = (bf16[1024,1536]{1,0:T(8,128)(2,1)}, bf16[1024,256]{1,0:T(8,128)(2,1)S(1)}, bf16[1024,256]{1,0:T(8,128)(2,1)S(1)}, bf16[1024,256]{1,0:T(8...) custom-call(bf16[1024,1536]{1,0:T(8,128)(2,1)} %bitcast.104, bf16[1536,384]{1,0:T(8,128)(2,1)S(1)} %bitcast.75, ...), custom_call_target="tpu_custom_call" | custom-call | tf_op jit(solution)/shard_map/attention_forward/pallas_call | solution.py:1559
  235.4 0.8 copy-done.20
  236.2 56.6 %middle_step.1 = (bf16[4,2,128,192]{3,2,1,0:T(8,128)(2,1)S(1)}, f32[128,1536]{1,0:T(8,128)S(1)}, bf16[4,2,2,128,1536]{4,3,2,1,0:T(8,128)(2,1)}) custom-call(bf16[4,2,128,192]{3,2,1,0:T(8,128)(2,1)S(1)} %bitcast.87, bf16[128,1536]{1,0:T(8,128)(2,1)S(1)} %bitcast.78, bf16[1536,1536]{1,0:T(8,128)(2,1)} %bitcast.95, f32[1,1536]{1,0:T(1,128)S(1)} %reshape.253.refs_3_.refs_6_), custom_call_target="tpu_custom_call" | custom-call | tf_op jit(solution)/shard_map/middle_step/pallas_call | solution.py:994
  292.8 0.7 pad_add_fusion.refs_0_
  293.5 15.4 %dispatch.1 = (bf16[8,3,80,1536]{3,2,1,0:T(8,128)(2,1)}, bf16[8,3,80,1536]{3,2,1,0:T(8,128)(2,1)}, f32[8,3,80,1]{3,2,1,0:T(8,128)S(1)}, bf16[8,240,256]{2,1,0:T(8,128)(2,1)S(1)}, f32[16,128,128]{2,1,0:T(8,128)S(1)}) custom-call(s32[1]{0:T(128)} %bitcast.base, bf16[16,128,1536]{2,1,0:T(8,128)(2,1)} %bitcast.99, bf16[16,128,1664]{2,1,0:T(8,128)(2,1)} %bitcast.101, ...), custom_call_target="tpu_custom_call" | custom-call | tf_op jit(solution)/shard_map/dispatch/pallas_call | solution.py:445
  309.0 0.9 copy-done.26
  309.9 1.0 copy-done.29
  310.9 40.8 %experts.1 = (bf16[8,3,80,1536]{3,2,1,0:T(8,128)(2,1)}, bf16[8,3,80,1664]{3,2,1,0:T(8,128)(2,1)}, bf16[5,192,768]{2,1,0:T(8,128)(2,1)}, bf16[5,192,768]{2,1,0:T(...) custom-call(s32[4]{0:T(128)} %pad_add_fusion.refs_0_, ...), custom_call_target="tpu_custom_call" | custom-call | flops 22649241600 | bytes 62914560 | tf_op jit(solution)/shard_map/experts/pallas_call | solution.py:555
  351.7 7.3 %convolution_convert_fusion.1 = bf16[8,256,1536]{2,1,0:T(8,128)(2,1)} fusion(bf16[8,240,256]{2,1,0:T(8,128)(2,1)S(1)} %get-tuple-element.75, bf16[8,240,1536]{2,1,0:T(8,128)(2,1)} %bitcast.102), kind=kOutput, calls=%fused_computation.1 | convolution fusion | flops 1513095168 | bytes 13172736 | tf_op jit(solution)/shard_map/prt,prd->ptd/dot_general | solution.py:1766
  359.1 5.0 convolution_convert_fusion
  364.1 0.8 dynamic-slice_bitcast_fusion.refs_4_
  364.9 1.0 copy-done.9
  365.9 1.1 copy-done.11
  367.1 146.3 %router_step.1 = (bf16[128,128]{1,0:T(8,128)(2,1)S(1)}, f32[1,1536]{1,0:T(1,128)S(1)}, f32[128,1536]{1,0:T(8,128)S(1)}, bf16[4,2,128,192]{3,2,1,0:T(8,128)(2,1)S...) custom-call(bf16[4,2,2,128,1664]{4,3,2,1,0:T(8,128)(2,1)} %bitcast.90, ...), custom_call_target="tpu_custom_call" | custom-call | tf_op jit(solution)/shard_map/router_step/pallas_call | solution.py:994
  513.4 1.2 copy-done.1
  514.6 0.8 copy-done.22
  515.4 0.7 copy-done.24
  516.1 2.9 add_convert_fusion.1
  519.0 1.3 collective-permute-start
  520.4 1.3 collective-permute-start.1
  521.7 0.7 concatenate.32
  522.4 1.0 copy-done.15
  523.5 1.0 copy-done.17
  524.5 1.0 copy-done.19
  525.5 1.0 copy-done.21
  526.6 1.0 copy-done.23
  527.6 24.7 %attention_backward.1 = (bf16[4,8,48,320]{3,2,1,0:T(8,128)(2,1)S(1)}, bf16[1024,1536]{1,0:T(8,128)(2,1)}) custom-call(bf16[1024,1536]{1,0:T(8,128)(2,1)} %get-tuple-element.101.hidden, bf16[1024,256]{1,0:T(8,128)(2,1)S(1)} %copy-done.15, bf16[1024,256]{1,0:T(8,128)(2,1)S(1)} %copy-done.17, bf16[1024,256]{1,0:T(8,128)(2,1)S(1)} %copy-done.19, ...), custom_call_target="tpu_custom_call" | custom-call | tf_op jit(solution)/shard_map/attention_backward/pallas_call | solution.py:1638
  552.4 1.3 fusion.5
  553.7 0.2 pad_maximum_fusion.refs_6_
  553.9 3.6 convolution_convert_fusion.2
  557.5 2.9 add_convert_fusion.refs_7_
  560.4 104.9 %last_step.1 = (f32[128,1536]{1,0:T(8,128)S(1)}, bf16[4,2,48,320]{3,2,1,0:T(8,128)(2,1)S(1)}, f32[48,1536]{1,0:T(8,128)S(1)}, f32[48,128]{1,0:T(8,128)S(1)}, bf1...) custom-call(bf16[4,2,128,1536]{3,2,1,0:T(8,128)(2,1)} %bitcast.105, bf16[128,1536]{1,0:T(8,128)(2,1)S(1)} %bitcast.79, ...), custom_call_target="tpu_custom_call" | custom-call | tf_op jit(solution)/shard_map/last_step/pallas_call | solution.py:994
  665.4 1.1 copy-done.2
  666.5 0.7 copy.58
  667.4 0.7 reshape.251
  668.2 0.2 copy.55
  668.5 0.9 reshape.249
  669.4 0.7 reshape.250
  670.1 0.7 slice_reduce_fusion
  670.8 0.3 fusion
  671.1 0.5 convert_divide_fusion
  671.6 11.6 %place_units.1 = (f32[10,192,1024]{2,1,0:T(8,128)}, f32[10,192,512]{2,1,0:T(8,128)}) custom-call(s32[1]{0:T(128)} %bitcast.21.refs_0_, bf16[5,192,768]{2,1,0:T(8,128)(2,1)} %get-tuple-element.120.refs_1_.refs_6_, bf16[5,192,768]{2,1,0:T(8,128)(2,1)} %get-tuple-element.121.refs_2_.refs_7_, bf16[5,192,768]{2,1,0:T(8,128)(2,1)} %copy-done.2, ...), custom_call_target="tpu_custom_call" | custom-call | tf_op jit(solution)/shard_map/place_units/pallas_call | solution.py:614
  683.2 0.7 copy.63
  684.0 0.9 copy.64
  684.9 0.7 copy.65
  (95 shorter events, 1.3 us)
Async XLA Ops:
  0.6 7.3 %copy-start.8 = (bf16[1,128,1536]{2,1,0:T(8,128)(2,1)S(1)}, bf16[1,128,1536]{2,1,0:T(8,128)(2,1)}, u32[]{:S(2)}) copy-start(bf16[1,128,1536]{2,1,0:T(8,128)(2,1)} %param.15) | copy-start | bytes 1179652
  0.7 7.4 %copy-start.3 = (bf16[1,128,1536]{2,1,0:T(8,128)(2,1)S(1)}, bf16[1,128,1536]{2,1,0:T(8,128)(2,1)}, u32[]{:S(2)}) copy-start(bf16[1,128,1536]{2,1,0:T(8,128)(2,1)} %param.14) | copy-start | bytes 1179652
  3.5 4.3 copy-start.32
  4.6 3.2 copy-start.34
  8.0 207.6 %copy-start.37 = (s32[1,16]{1,0:T(1,128)S(1)}, s32[1,16]{1,0:T(1,128)}, u32[]{:S(2)}) copy-start(s32[1,16]{1,0:T(1,128)} %param.17) | copy-start | bytes 196
  8.0 207.7 %copy-start.36 = (s32[1,2]{1,0:T(1,128)S(1)}, s32[1,2]{1,0:T(1,128)}, u32[]{:S(2)}) copy-start(s32[1,2]{1,0:T(1,128)} %param.16) | copy-start | bytes 28
  212.6 1.1 copy-start.27
  213.7 1.1 copy-start.28
  214.9 20.5 %copy-start = (bf16[4,2,2,2,48,384]{5,4,3,2,1,0:T(8,128)(2,1)}, bf16[4,2,2,2,48,384]{5,4,3,2,1,0:T(8,128)(2,1)S(1)}, u32[]{:S(2)}) copy-start(bf16[4,2,2,2,48,384]{5,4,3,2,1,0:T(8,128)(2,1)S(1)} %get-tuple-element.70) | copy-start | bytes 3538948
  218.9 17.3 %copy-start.4 = (bf16[1,128,1536]{2,1,0:T(8,128)(2,1)S(1)}, bf16[1,128,1536]{2,1,0:T(8,128)(2,1)}, u32[]{:S(2)}) copy-start(bf16[1,128,1536]{2,1,0:T(8,128)(2,1)} %param.14) | copy-start | bytes 1179652
  235.4 0.8 copy-start.20
  236.2 57.3 %copy-start.14 = (bf16[1024,256]{1,0:T(8,128)(2,1)}, bf16[1024,256]{1,0:T(8,128)(2,1)S(1)}, u32[]{:S(2)}) copy-start(bf16[1024,256]{1,0:T(8,128)(2,1)S(1)} %get-tuple-element.102.qk) | copy-start | bytes 1572868
  236.2 72.7 %copy-start.16 = (bf16[1024,256]{1,0:T(8,128)(2,1)}, bf16[1024,256]{1,0:T(8,128)(2,1)S(1)}, u32[]{:S(2)}) copy-start(bf16[1024,256]{1,0:T(8,128)(2,1)S(1)} %get-tuple-element.103.keys) | copy-start | bytes 1572868
  236.2 72.7 %copy-start.18 = (bf16[1024,256]{1,0:T(8,128)(2,1)}, bf16[1024,256]{1,0:T(8,128)(2,1)S(1)}, u32[]{:S(2)}) copy-start(bf16[1024,256]{1,0:T(8,128)(2,1)S(1)} %get-tuple-element.104.values) | copy-start | bytes 1572868
  236.2 57.3 %copy-start.6 = (bf16[1536,128]{1,0:T(8,128)(2,1)S(1)}, bf16[1536,128]{1,0:T(8,128)(2,1)}, u32[]{:S(2)}) copy-start(bf16[1536,128]{1,0:T(8,128)(2,1)} %concatenate.28.router_ref.refs_5_) | copy-start | bytes 1179652
  292.8 16.2 %copy-start.10 = (f32[128,1536]{1,0:T(8,128)}, f32[128,1536]{1,0:T(8,128)S(1)}, u32[]{:S(2)}) copy-start(f32[128,1536]{1,0:T(8,128)S(1)} %get-tuple-element.89.refs_2_) | copy-start | bytes 2359300
  292.8 16.2 %copy-start.12 = (bf16[4,2,128,192]{3,2,1,0:T(8,128)(2,1)}, bf16[4,2,128,192]{3,2,1,0:T(8,128)(2,1)S(1)}, u32[]{:S(2)}) copy-start(bf16[4,2,128,192]{3,2,1,0:T(8,128)(2,1)S(1)} %get-tuple-element.111) | copy-start | bytes 1179652
  309.0 1.0 copy-start.26
  309.9 1.0 copy-start.29
  351.7 7.4 %slice-start = ((s8[6389760]{0:T(1024)(128)(4,1)}), s8[4194304]{0:T(1024)(128)(4,1)S(1)}, s32[]{:S(2)}) async-start(s8[6389760]{0:T(1024)(128)(4,1)} %bitcast.92), calls=%async_computation | async-start | bytes 8388608
  351.7 7.3 %slice-start.1 = ((s8[6389760]{0:T(1024)(128)(4,1)}), s8[2195456]{0:T(1024)(128)(4,1)S(1)}, s32[]{:S(2)}) async-start(s8[6389760]{0:T(1024)(128)(4,1)} %bitcast.92), calls=%async_computation.1 | async-start | bytes 4390912
  359.1 5.9 copy-start.7
  364.9 1.0 copy-start.9
  365.9 1.1 copy-start.11
  367.1 149.0 %copy-start.31 = (bf16[5,192,768]{2,1,0:T(8,128)(2,1)S(1)}, bf16[5,192,768]{2,1,0:T(8,128)(2,1)}, u32[]{:S(2)}) copy-start(bf16[5,192,768]{2,1,0:T(8,128)(2,1)} %get-tuple-element.96) | copy-start | bytes 4423684
  513.4 1.2 copy-start.1
  514.6 0.8 copy-start.22
  515.4 0.7 copy-start.24
  519.0 38.5 %collective-permute-start = (bf16[5,192,768]{2,1,0:T(8,128)(2,1)}, bf16[5,192,768]{2,1,0:T(8,128)(2,1)}, u32[]{:S(2)}, u32[]{:S(2)}) collective-permute-start(bf16[5,192,768]{2,1,0:T(8,128)(2,1)} %get-tuple-element.100), channel_id=1, source_target_pairs={{0,4},{4,0},{1,5},{5,1},{2,6},{6,2},{3,7},{7,3},{8,12},{12,8},{9,1... | collective-permute-start | bytes 4423688 | tf_op jit(solution)/shard_map/ppermute | solution.py:1795
  520.4 151.3 %collective-permute-start.1 = (bf16[5,192,768]{2,1,0:T(8,128)(2,1)}, bf16[5,192,768]{2,1,0:T(8,128)(2,1)}, u32[]{:S(2)}, u32[]{:S(2)}) collective-permute-start(bf16[5,192,768]{2,1,0:T(8,128)(2,1)} %add_convert_fusion.1), channel_id=1, source_target_pairs={{0,16},{8,24},{16,0},{24,8},{1,17},{9,25},{17,1},{25,9},{2,18},{10... | collective-permute-start | bytes 4423688 | tf_op jit(solution)/shard_map/ppermute | solution.py:1794
  522.4 1.0 copy-start.15
  523.5 1.0 copy-start.17
  524.5 1.0 copy-start.19
  525.5 1.0 copy-start.21
  526.6 1.0 copy-start.23
  527.6 26.3 %copy-start.13 = (bf16[4,2,128,192]{3,2,1,0:T(8,128)(2,1)S(1)}, bf16[4,2,128,192]{3,2,1,0:T(8,128)(2,1)}, u32[]{:S(2)}) copy-start(bf16[4,2,128,192]{3,2,1,0:T(8,128)(2,1)} %copy-done.12) | copy-start | bytes 1179652
  553.9 3.6 copy-start.30
  557.5 2.9 copy-start.5
  665.3 1.1 copy-start.2
  666.5 4.3 copy-start.33
  666.5 4.3 copy-start.35
  667.2 3.9 copy-start.38
  671.6 11.6 %copy-start.25 = (bf16[128,1536]{1,0:T(8,128)(2,1)S(1)}, bf16[128,1536]{1,0:T(8,128)(2,1)}, u32[]{:S(2)}) copy-start(bf16[128,1536]{1,0:T(8,128)(2,1)} %copy-done.24) | copy-start | bytes 1179652

commit v5 on v4

--- a/solution.py
+++ b/solution.py
@@ -18,6 +18,7 @@
 
 
 EPSILON = 1e-06
+LATE = 2
 NEGATIVE = -1e30
 
 
@@ -469,8 +470,8 @@
 
 
 def expert_kernel(depth, meta, x_ref, g_ref, gate_ref, *refs):
-    parts, (y_ref, d_ref), outs = refs[:8], refs[8:10], refs[10:18]
-    weight, du_ref, act_ref = refs[18:]
+    parts, (y_ref, d_ref), outs = refs[:10], refs[10:12], refs[12:20]
+    weight, du_ref, act_ref = refs[20:]
     bf16, f32 = jnp.bfloat16, jnp.float32
     j = pl.program_id(0)
     shift, z, y, base = meta[0], meta[1], meta[2], meta[3]
@@ -478,8 +479,15 @@
     offsets = [
         pl.multiple_of(((z ^ (i % 4)) * 2 + (y ^ (i // 4))) * depth, 64) for i in range(8)
     ]
-    for part, offset in zip(parts, offsets):
-        weight[pl.ds(offset, depth), :] = part[0]
+    cut = pl.num_programs(0) - LATE
+    for i, offset in enumerate(offsets):
+        group = parts[i // 4 * 5 + i % 4 : i // 4 * 5 + i % 4 + (2 if i % 4 == 3 else 1)]
+        for part, here in zip(group, (j < cut, j >= cut) if len(group) > 1 else (j >= 0,)):
+
+            @pl.when(here)
+            def _(part=part, offset=offset):
+                weight[pl.ds(offset, depth), :] = part[0]
+
     expert = base + (j + shift) // 2
     first = jnp.logical_or(j == 0, lax.rem(j + shift, 2) == 0)
     keep = jnp.where(first, 0.0, 1.0)
@@ -550,6 +558,9 @@
         (pairs, 1, rows, width), lambda j, m: (0, (j + m[0]) // 2, 0, 0)
     )
     unit_block = pl.BlockSpec((1, depth, columns), lambda j, m: (j, 0, 0))
+    cut = units - LATE
+    early_block = pl.BlockSpec((1, depth, columns), lambda j, m: (jnp.minimum(j, cut - 1), 0, 0))
+    late_block = pl.BlockSpec((1, depth, columns), lambda j, m: (jnp.maximum(j - cut, 0), 0, 0))
     bf16 = jnp.bfloat16
     total = units * pairs * rows * D * columns * 6
     return pl.pallas_call(
@@ -562,7 +573,7 @@
                 held_block(D),
                 held_block(1),
             ]
-            + [unit_block] * 8,
+            + [unit_block, unit_block, unit_block, early_block, late_block] * 2,
             out_specs=[held_block(D), held_block(D + 128)] + [unit_block] * 8,
             scratch_shapes=[
                 pltpu.VMEM((D, columns), bf16),
@@ -584,11 +595,14 @@
 
 
 def place_kernel(number, z_ref, *refs):
-    in_ref, out_ref = refs[10:]
+    in_ref, out_ref = refs[12:]
     half = refs[0].shape[-1] // 3
     for h in range(2):
-        source = ((2 * pl.program_id(0) + h) // number) ^ z_ref[0]
-        first, other, *rest = refs[5 * h : 5 * h + 5]
+        unit = 2 * pl.program_id(0) + h
+        source = (unit // number) ^ z_ref[0]
+        late = (source == 3) & (lax.rem(unit, number) >= number - LATE)
+        source = jnp.where(late, 4, source)
+        first, other, *rest = refs[6 * h : 6 * h + 6]
         for i, group in enumerate([(first, other)] + [(ref,) for ref in rest]):
 
             @pl.when(source == i)
@@ -601,13 +615,16 @@
                 out_ref[0, :, h * half : (h + 1) * half] = total[:, 2 * half :]
 
 
-def place_units(z_index, first, other, near, mid, far):
+def place_units(z_index, first, other, near, mid, far, late):
     number, depth, columns = first.shape
 
     def block(i, h):
+        low, most = {3: (0, number - LATE - 1), 4: (number - LATE, LATE - 1)}.get(i, (0, number - 1))
+
         def index(e, z):
             unit = 2 * e + h
-            return jnp.where((unit // number) ^ z[0] == i, lax.rem(unit, number), 0), 0, 0
+            at = jnp.clip(lax.rem(unit, number) - low, 0, most)
+            return jnp.where((unit // number) ^ z[0] == min(i, 3), at, 0), 0, 0
 
         return pl.BlockSpec((1, depth, columns), index)
 
@@ -616,7 +633,7 @@
         grid_spec=pltpu.PrefetchScalarGridSpec(
             num_scalar_prefetch=1,
             grid=(EXP_DEV,),
-            in_specs=[block(i, h) for h in range(2) for i in (0, 0, 1, 2, 3)],
+            in_specs=[block(i, h) for h in range(2) for i in (0, 0, 1, 2, 3, 4)],
             out_specs=[
                 pl.BlockSpec((1, depth, 2 * HID), lambda e, z: (e, 0, 0)),
                 pl.BlockSpec((1, depth, HID), lambda e, z: (e, 0, 0)),
@@ -627,7 +644,7 @@
             jax.ShapeDtypeStruct((EXP_DEV, depth, HID), jnp.float32),
         ],
         name="place_units",
-    )(z_index.reshape(1), *[first, other, near, mid, far] * 2)
+    )(z_index.reshape(1), *[first, other, near, mid, far, late] * 2)
 
 
 MESH = pl.DeviceIdType.MESH
@@ -1009,13 +1026,14 @@
     columns, wide = slices.shape[-1], marked.shape[-1]
     depth, half = win.shape[1], HID // 2
     number = 2 * win.shape[0] // 4
+    early = number - LATE
     chunks = 2
     bf16 = jnp.bfloat16
 
     def kernel(ins, outs, token_refs, wo_refs, marked_refs, other):
         tok, cut, wo_ref, marked_ref, win_ref, wout_ref = ins
         tok_out, cut_out, wo_out, marked_out = outs[:4]
-        near, far = outs[4:8], outs[8:12]
+        near, far, late = outs[4:8], (outs[8], None, *outs[9:11]), outs[11]
         keep, ctx_sems, exp_sems = other[0], other[1:3], other[3:5]
         near_sems, far_sems, win_in, wout_in, unit = other[5:7], other[7:9], *other[9:12]
         z, y, x, k = (lax.axis_index(a) for a in ("z", "y", "x", "k"))
@@ -1067,6 +1085,9 @@
         def own_unit(j):
             return pltpu.make_async_copy(unit.at[0, j], near[0].at[j], keep.at[3 + j])
 
+        def late_unit(j):
+            return pltpu.make_async_copy(unit.at[3, j], late.at[j - early], keep.at[3 + number + j])
+
         def convert(j):
             for i in range(4):
                 index = number * (z ^ i) + j
@@ -1078,11 +1099,11 @@
                 unit[i, j, :, 2 * half :] = wout_in[e, :, first].astype(bf16)
 
         def send_units(j):
-            for i in (3, 2, 1):
+            for i in (3, 2, 1) if j < early else (2, 1):
                 over_z(i, j).start()
 
         def pass_units(j):
-            for i in (1, 2, 3):
+            for i in (2, 3) if j < early else (2,):
                 over_z(i, j).wait_recv()
                 over_y(i, j).start()
 
@@ -1094,6 +1115,8 @@
             if j:
                 convert(j)
             own_unit(j).start()
+            if j >= early:
+                late_unit(j).start()
             over_y(0, j).start()
         for t in (1, 2, 3):
             whole.forward(0, (t,))
@@ -1126,13 +1149,22 @@
             copy.wait_send()
         for j in range(number):
             own_unit(j).wait()
+            if j >= early:
+                late_unit(j).wait()
             for i in range(4):
-                over_y(i, j).wait_recv()
-                over_y(i, j).wait_send()
+                if i == 3 and j >= early:
+                    continue
+                if i == 1:
+                    over_z(i, j).wait_recv()
+                else:
+                    over_y(i, j).wait_recv()
+                    over_y(i, j).wait_send()
                 if i:
                     over_z(i, j).wait_send()
 
-    units = jax.ShapeDtypeStruct((number, depth, 3 * half), bf16)
+    units, most, few = (
+        jax.ShapeDtypeStruct((n, depth, 3 * half), bf16) for n in (number, early, LATE)
+    )
     outs = exchange(
         kernel,
         "share_inputs",
@@ -1145,13 +1177,14 @@
             jax.ShapeDtypeStruct((4, 2, 2, 2, own, D), bf16),
             jax.ShapeDtypeStruct((4, 2, 2, count, wide), bf16),
         ]
-        + [units] * 8,
+        + [units] * 3
+        + [most, units, units, most, few],
         [ANY_SPEC] * 12,
         [
             Gather.scratch(("y",), chunks),
             Gather.scratch(("y", "x", "k"), 1),
             Gather.scratch(("x", "k"), 1),
-            [pltpu.SemaphoreType.DMA((3 + number,))]
+            [pltpu.SemaphoreType.DMA((3 + 2 * number,))]
             + dma_pair(7)
             + dma_pair(3)
             + dma_pair(4 * number)
@@ -1163,7 +1196,7 @@
             ],
         ],
     )
-    return (*outs[:4], list(outs[4:]))
+    return (*outs[:4], outs[4:8], outs[8:11], outs[11])
 
 
 def ctx_peers():
@@ -1171,15 +1204,15 @@
     return [(z ^ (i // 2), y ^ (i % 2), i) for i in range(7, 0, -1)]
 
 
-def middle_step(heads, tokens, wo, gain):
+def middle_step(heads, tokens, wo, gain, bulk):
     count, chunks = tokens.shape[0], 2
     width = heads.shape[-1]
     bf16, f32 = jnp.bfloat16, jnp.float32
 
     def kernel(ins, outs, hidden_refs, other):
-        heads_ref, tok, wo_ref, gain_ref = ins
-        attended_ref, middle_ref, hidden_out = outs
-        own, sems = other[0], other[1:3]
+        heads_ref, tok, wo_ref, gain_ref = ins[:4]
+        attended_ref, middle_ref, hidden_out = outs[:3]
+        own, sems, bulk_sems = other[0], other[1:3], other[3:5]
         z, y = lax.axis_index("z"), lax.axis_index("y")
         greet(
             [{"z": p, "y": q} for p, q, _ in ctx_peers()] + siblings(("x", "k"))
@@ -1190,6 +1223,9 @@
             for p, q, i in ctx_peers()
         ]
         attended_ref[z, y] = heads_ref[z, y]
+        bulk_copies = [
+            send(a, b, bulk_sems, i, {"y": 1 - y}) for i, (a, b) in enumerate(zip(ins[4:], outs[3:]))
+        ]
         for copy in copies:
             copy.wait_recv()
         step = count // chunks
@@ -1211,24 +1247,27 @@
             hidden.forward(c)
             hidden.spread(c)
         hidden.finish()
-        for copy in copies:
+        for copy in bulk_copies:
+            copy.wait_recv()
+        for copy in copies + bulk_copies:
             copy.wait_send()
 
     return exchange(
         kernel,
         "middle_step",
         2,
-        (heads, tokens, wo, gain),
-        [VMEM_SPEC] * 4,
+        (heads, tokens, wo, gain, *bulk),
+        [VMEM_SPEC] * 4 + [ANY_SPEC] * len(bulk),
         [
             jax.ShapeDtypeStruct((4, 2, count, width), bf16),
             jax.ShapeDtypeStruct((count, D), f32),
             jax.ShapeDtypeStruct((4, 2, 2, count, D), bf16),
-        ],
-        [VMEM_SPEC, VMEM_SPEC, ANY_SPEC],
+        ]
+        + [jax.ShapeDtypeStruct(a.shape, a.dtype) for a in bulk],
+        [VMEM_SPEC, VMEM_SPEC, ANY_SPEC] + [ANY_SPEC] * len(bulk),
         [
             Gather.scratch(("x", "k"), chunks),
-            [pltpu.VMEM((count, D), bf16)] + dma_pair(7),
+            [pltpu.VMEM((count, D), bf16)] + dma_pair(7) + dma_pair(len(bulk)),
         ],
     )
 
@@ -1236,6 +1275,7 @@
 def router_step(part, mixed, middle, cotangent, gates, router, gain, wo, bulk, added):
     count, chunks = middle.shape[0], 4
     width, (number, depth, _) = wo.shape[0] // 8, added.shape
+    early = number - LATE
     bf16, f32 = jnp.bfloat16, jnp.float32
 
     def kernel(ins, outs, scatter_refs, mixed_refs, other):
@@ -1248,7 +1288,7 @@
         bulk_in, bulk_out, added_ref = ins[8:-1], outs[6:], ins[-1]
         far_out = outs[5]
         z, y = lax.axis_index("z"), lax.axis_index("y")
-        load = pltpu.make_async_copy(added_ref, own_unit, load_sem.at[0])
+        load = pltpu.make_async_copy(added_ref.at[pl.ds(0, early)], own_unit, load_sem.at[0])
         load.start()
         greet([{"z": p, "y": q} for p, q, _ in ctx_peers()] + siblings(("x", "k")))
         scatter = Scatter(part_ref, ("x", "k"), chunks, scatter_refs)
@@ -1256,14 +1296,19 @@
         copies = []
         scatter.start()
         mixture.start()
-        pieces = 2 * number
+        pieces = 2 * early
         piece = lambda ref, j: ref.at[j // 2, pl.ds(j % 2 * (depth // 2), depth // 2)]
         over_first = [
             send(piece(bulk_in[0], j), piece(came_unit, j), first_sems, j, {"y": 1 - y})
             for j in range(pieces)
         ]
         over_far = []
-        bulk_copies = [send(bulk_in[1], bulk_out[0], bulk_sems, 0, {"y": 1 - y})]
+        bulk_copies = [
+            send(
+                bulk_in[0].at[pl.ds(early, number - early)], bulk_out[0], bulk_sems, 0, {"y": 1 - y}
+            ),
+            send(bulk_in[1], bulk_out[1], bulk_sems, 1, {"y": 1 - y}),
+        ]
         load.wait()
 
         def send_far(j):
@@ -1304,12 +1349,13 @@
                     )
                 )
             heads_out[z, y] = turned[z, y]
+            bulk_copies.append(send(bulk_in[2], bulk_out[2], bulk_sems, 2, {"y": 1 - y}))
 
         def use_mixture(c, at, total):
             out_ref[at, :] = (middle_ref[at, :] + total).astype(bf16)
 
         behind = 3
-        plan = [[0], [1, 2], [3], [4], [5], [6], [7], [8], [9], []]
+        plan = [[0, 1], [2], [3], [4], [5]] + [[]] * 5
         for step in range(scatter.length() + behind):
             if step < scatter.length():
                 scatter.advance(step, use)
@@ -1331,7 +1377,7 @@
         "router_step",
         3,
         (part, mixed, middle, cotangent, gates, router, gain, wo, *bulk, added),
-        [ANY_SPEC] * 2 + [VMEM_SPEC] * 6 + [ANY_SPEC] * 3,
+        [ANY_SPEC] * 2 + [VMEM_SPEC] * 6 + [ANY_SPEC] * 4,
         [
             jax.ShapeDtypeStruct((count, 128), bf16),
             jax.ShapeDtypeStruct((1, D), f32),
@@ -1339,29 +1385,32 @@
             jax.ShapeDtypeStruct((4, 2, count, width), bf16),
             jax.ShapeDtypeStruct((count, D), bf16),
         ]
-        + [jax.ShapeDtypeStruct(added.shape, bf16)] * 2,
-        [VMEM_SPEC] * 5 + [ANY_SPEC] * 2,
+        + [
+            jax.ShapeDtypeStruct((n, *added.shape[1:]), bf16)
+            for n in (early, number - early, number, number)
+        ],
+        [VMEM_SPEC] * 5 + [ANY_SPEC] * 4,
         [
             Scatter.scratch(part, ("x", "k"), chunks),
             Scatter.scratch(mixed, ("x", "k"), chunks),
-            [pltpu.VMEM((4, 2, count, width), bf16)] + dma_pair(7) + dma_pair(1) + dma_pair(2 * number) * 2
-            + [pltpu.VMEM(added.shape, bf16)] * 2 + [pltpu.SemaphoreType.DMA((1,))],
+            [pltpu.VMEM((4, 2, count, width), bf16)] + dma_pair(7) + dma_pair(3) + dma_pair(2 * early) * 2
+            + [pltpu.VMEM((early, *added.shape[1:]), bf16)] * 2 + [pltpu.SemaphoreType.DMA((1,))],
         ],
     )
 
 
 def last_step(
-    part, tokens, grad_middle, gain, qkv_part, wo_part, small_part, bulk
+    part, tokens, grad_middle, gain, qkv_part, wo_part, small_part
 ):
     count, chunks = tokens.shape[0], 4
     own, columns = qkv_part.shape[-2:]
     bf16, f32 = jnp.bfloat16, jnp.float32
 
     def kernel(ins, outs, part_refs, wo_refs, other):
-        part_ref, tok, grad_ref, gain_ref, qkv, wo, small = ins[:7]
-        tokens_ref, qkv_out, wo_out, small_out = outs[:4]
+        part_ref, tok, grad_ref, gain_ref, qkv, wo, small = ins
+        tokens_ref, qkv_out, wo_out, small_out = outs
         qkv_came, qkv_sum, small_came = other[:3]
-        sems = [other[3 + 2 * i : 5 + 2 * i] for i in range(4)]
+        sems = [other[3 + 2 * i : 5 + 2 * i] for i in range(3)]
         names = ("z", "y", "x", "k")
         z, y, x, k = (lax.axis_index(a) for a in names)
         everyone = [
@@ -1392,24 +1441,6 @@
         def use_third(c, at, total):
             wo_out[at, :] = total
 
-        number = bulk[0].shape[0]
-        waiting = [(i, j) for j in range(number) for i in range(len(bulk))]
-        over = [{"z": z ^ 1}, {"y": 1 - y}]
-        over_bulk = []
-
-        def send_bulk(most):
-            for i, j in waiting[:most]:
-                over_bulk.append(
-                    send(
-                        ins[7 + i].at[j],
-                        outs[4 + i].at[j],
-                        sems[3],
-                        i * number + j,
-                        over[i],
-                    )
-                )
-            del waiting[:most]
-
         for step in range(third.length()):
             if step < first.length():
                 first.advance(step, use_first)
@@ -1430,35 +1461,31 @@
                     send(small.at[p], small_came.at[i - 1], sems[2], i - 1, place(p))
                     for p, i in everyone
                 ]
-            if step >= 2:
-                send_bulk(2)
-        send_bulk(len(waiting))
         total = small[z, y, x, k].astype(f32)
         for copy, (_, i) in zip(over_small, everyone):
             copy.wait_recv()
             total = total + small_came[i - 1].astype(f32)
         small_out[...] = total
-        for copy in over_ctx + over_bulk:
+        for copy in over_ctx:
             copy.wait_recv()
         first.finish()
         third.finish()
-        for copy in over_qkv + over_ctx + over_small + over_bulk:
+        for copy in over_qkv + over_ctx + over_small:
             copy.wait_send()
 
     return exchange(
         kernel,
         "last_step",
         4,
-        (part, tokens, grad_middle, gain, qkv_part, wo_part, small_part, *bulk),
-        [ANY_SPEC] + [VMEM_SPEC] * 4 + [ANY_SPEC, VMEM_SPEC] + [ANY_SPEC] * len(bulk),
+        (part, tokens, grad_middle, gain, qkv_part, wo_part, small_part),
+        [ANY_SPEC] + [VMEM_SPEC] * 4 + [ANY_SPEC, VMEM_SPEC],
         [
             jax.ShapeDtypeStruct((count, D), f32),
             jax.ShapeDtypeStruct((4, 2, own, columns), bf16),
             jax.ShapeDtypeStruct((own, D), f32),
             jax.ShapeDtypeStruct((own, 128), f32),
-        ]
-        + [jax.ShapeDtypeStruct(a.shape, a.dtype) for a in bulk],
-        [VMEM_SPEC] * 4 + [ANY_SPEC] * len(bulk),
+        ],
+        [VMEM_SPEC] * 4,
         [
             Scatter.scratch(part, ("y",), chunks),
             Scatter.scratch(wo_part, ("y", "x", "k"), 3),
@@ -1469,8 +1496,7 @@
             ]
             + dma_pair(3)
             + dma_pair(7)
-            + dma_pair(31)
-            + dma_pair(len(bulk) * bulk[0].shape[0]),
+            + dma_pair(31),
         ],
     )
 
@@ -1723,9 +1749,10 @@
     marked = jnp.concatenate(
         [cotangent[0], routes[0].astype(bf16), jnp.zeros((count, 128 - TOP), bf16)], axis=1
     )
-    token_all, slices, wo, marked_blocks, parts = share_inputs(
+    token_all, slices, wo, marked_blocks, near, far, late = share_inputs(
         tokens[0], slices.reshape(n_z, n_y, own, -1), attn_o.astype(bf16), marked, win, wout
     )
+    late = lax.ppermute(late, "z", swap_z[3])
     token_all = token_all.reshape(group, D)
     slices = slices.reshape(D, -1)
     wo = wo.reshape(HEADS * HEAD, D)
@@ -1746,9 +1773,10 @@
     hidden_all, queries, keys, values, attended_b, log_total = attention_forward(
         token_all, slices, gain_one_f, cosine, sine, rows, starts
     )
-    own_attended, middle, hidden_blocks = middle_step(
-        attended_b.reshape(n_z, n_y, count, width), tokens[0], wo, gain_two_f
-    )
+    own_attended, middle, hidden_blocks, *passed = middle_step(
+        attended_b.reshape(n_z, n_y, count, width), tokens[0], wo, gain_two_f, [near[1], late]
+    )
+    parts = [*near, late, far[0], passed[0], far[1], far[2], passed[1]]
     hidden_blocks = hidden_blocks.reshape(-1, count, D)
     marked_blocks = marked_blocks.reshape(-1, count, D + 128)
 
@@ -1775,7 +1803,7 @@
     made, back, *grads = run_experts(
         meta, row_in, row_up, slot_gate, parts
     )
-    logit_grad, grad_gain_two, grad_middle, grad_heads, output, far_sum, other = router_step(
+    logit_grad, grad_gain_two, grad_middle, grad_heads, output, far_sum, *others = router_step(
         to_tokens(back).reshape(n_z, 2, 2, count, D + 128),
         to_tokens(made).reshape(n_z, 2, 2, count, D),
         middle,
@@ -1784,15 +1812,19 @@
         weight_r,
         gain_two_f,
         wo,
-        [grads[7], grads[6]],
+        [grads[7], grads[6], grads[5]],
         grads[3],
     )
 
     add = lambda a, b: (a.astype(f32) + b.astype(f32)).astype(bf16)
-    sums = [None, None, add(grads[2], other), far_sum]
-    sums[2], grads[5], grad_heads = lax.optimization_barrier((sums[2], grads[5], grad_heads))
-    sums[2] = lax.ppermute(sums[2], "z", swap_z[2])
-    other = lax.ppermute(grads[5], "y", swap_y)
+    late_sum, mid_sum = add(grads[3][-LATE:], others[0]), add(grads[2], others[1])
+    late_sum, mid_sum, grads[4], grad_heads = lax.optimization_barrier(
+        (late_sum, mid_sum, grads[4], grad_heads)
+    )
+    late_sum = lax.ppermute(late_sum, "z", swap_z[3])
+    mid_sum = lax.ppermute(mid_sum, "z", swap_z[2])
+    other = lax.ppermute(grads[4], "y", swap_y)
+    near_sum = lax.ppermute(add(grads[1], others[2]), "z", swap_z[1])
 
     hidden_two = lax.dynamic_index_in_dim(
         hidden_blocks, z_index * n_exp + exp_index, 0, keepdims=False
@@ -1827,9 +1859,7 @@
         own,
     )
     grad_hidden = grad_hidden.reshape(n_z, n_y, count, D)
-    sums[1] = add(grads[1], other)
-    sums[1], grad_hidden = lax.optimization_barrier((sums[1], grad_hidden))
-    grad_tokens, grad_wqkv, grad_wo, small_grads, *bulk = last_step(
+    grad_tokens, grad_wqkv, grad_wo, small_grads = last_step(
         grad_hidden,
         tokens[0],
         grad_middle,
@@ -1837,10 +1867,9 @@
         grad_wqkv.reshape(2, 2, n_z, n_y, own, width + 2 * HEAD),
         grad_wo.reshape(n_z, n_y, 2, 2, own, D),
         small_grads,
-        [sums[1], grads[4]],
     )
     grad_expert_in, grad_expert_out = place_units(
-        z_index, grads[0], bulk[1], bulk[0], sums[2], sums[3]
+        z_index, grads[0], other, near_sum, mid_sum, far_sum, late_sum
     )
     grad_expert_in = grad_expert_in.transpose(1, 0, 2)
     grad_expert_out = grad_expert_out.transpose(1, 0, 2)

time: 694 us -> 651 us (0.938)
  Pallas kernels: 621 us -> 572 us
  starting transfers between devices: 2.65 us -> 12.8 us
    pallas_call x4, Pallas kernels: 512 us -> 461 us  [exchange(): pl.pallas_call(run, out_shape=outs, in_specs=specs, out_specs=out_specs,...]
    ppermute x2 -> x5, starting transfers between devices: 2.65 us -> 12.8 us  [the longest x1 6.95 us: body_heads(): other = lax.ppermute(grads[4], 'y', swap_y)]
    unnamed x87, local copies, waits for them, and re-layouts: 20.1 us -> 11.6 us
  transfers between devices with their start and end apart: 2 -> 5, of which waited for: 0 -> 0; matrix products, arithmetic and copies ran while one was open for 2% -> 3% of each run, Pallas kernels for 19% -> 22%
where the time goes in v5:
time: 651 us; the launch traced here: 646 us
  Pallas kernels  572 us (88%)
  local copies, waits for them, and re-layouts  21 us (3%)
  other arithmetic  20.3 us (3%)
  matrix products  18.4 us (3%)
  starting transfers between devices  12.8 us (2%)
    pallas_call x4, Pallas kernels, exchange(): pl.pallas_call(run, out_shape=outs, in_specs=specs, out_specs=out_specs,...  461 us
    pallas_call x1, Pallas kernels, run_experts(): pl.pallas_call(lambda *refs: expert_kernel(depth, *refs), grid_spec=pltpu...  41.3 us
    pallas_call x1, Pallas kernels, attention_backward(): pl.pallas_call(attention_backward_kernel, in_specs=[VMEM_SPEC] * 12, out_...  24.8 us
    pallas_call x1, Pallas kernels, attention_forward(): pl.pallas_call(attention_forward_kernel, in_specs=[VMEM_SPEC] * 8, out_sp...  16.5 us
    pallas_call x1, Pallas kernels, dispatch(): pl.pallas_call(dispatch_kernel, grid_spec=pltpu.PrefetchScalarGridSpec(nu...  16.2 us
  transfers between devices with their start and end apart: 5, of which 0 were waited for; matrix products, arithmetic and copies ran while one was open for 3% of the time, Pallas kernels for 22%

profile of v5, /device:TPU:0, one launch (start us, length us, event | category | flops | bytes accessed | tf_op | source)
XLA Modules:
  0.0 645.9 jit_solution(7920856767505294057)
XLA Ops:
  0.7 0.8 convert_element_type.124
  1.6 0.7 convert_bitcast_fusion.1
  2.4 0.9 convert_element_type.122
  3.3 0.1 reshape.233
  3.5 0.9 convert_element_type.123
  4.4 0.1 reshape.234
  4.6 0.8 copy.51
  5.4 1.0 convert_element_type.121
  6.4 0.2 reshape.232
  6.6 1.1 convert_element_type.127.refs_2_
  7.7 0.1 fusion.10
  7.8 0.1 pad_maximum_fusion.2
  8.0 0.1 concatenate.27.refs_3_
  8.1 171.9 %share_inputs.1 = (bf16[4,2,128,1536]{3,2,1,0:T(8,128)(2,1)}, bf16[4,2,2,2,48,384]{5,4,3,2,1,0:T(8,128)(2,1)S(1)}, bf16[4,2,2,2,48,1536]{5,4,3,2,1,0:T(8,128)(2,...) custom-call(bf16[128,1536]{1,0:T(8,128)(2,1)S(1)} %bitcast.77, ...), custom_call_target="tpu_custom_call" | custom-call | tf_op jit(solution)/shard_map/share_inputs/pallas_call | solution.py:1011
  180.0 0.9 copy-done.24
  181.0 0.9 copy-done.25
  181.9 1.5 collective-permute-start
  183.4 0.5 convert_reduce_fusion
  183.9 0.2 slice.51
  184.3 1.0 copy.52
  185.3 0.8 concatenate.28.router_ref.refs_5_
  186.2 1.9 multiply_sine_fusion
  188.1 1.2 compare_select_fusion
  189.2 16.5 %attention_forward.1 = (bf16[1024,1536]{1,0:T(8,128)(2,1)}, bf16[1024,256]{1,0:T(8,128)(2,1)S(1)}, bf16[1024,256]{1,0:T(8,128)(2,1)S(1)}, bf16[1024,256]{1,0:T(8...) custom-call(bf16[1024,1536]{1,0:T(8,128)(2,1)} %bitcast.104, bf16[1536,384]{1,0:T(8,128)(2,1)S(1)} %bitcast.75, ...), custom_call_target="tpu_custom_call" | custom-call | tf_op jit(solution)/shard_map/attention_forward/pallas_call | solution.py:1585
  205.7 0.8 copy-done.8
  206.5 0.8 copy-done.10
  207.3 0.8 copy-done.12
  208.1 0.8 copy-done.14
  208.9 0.6 pad_add_fusion.refs_0_
  209.5 56.7 %middle_step.1 = (bf16[4,2,128,192]{3,2,1,0:T(8,128)(2,1)S(1)}, f32[128,1536]{1,0:T(8,128)S(1)}, bf16[4,2,2,128,1536]{4,3,2,1,0:T(8,128)(2,1)}, bf16[5,192,768]{2,1,0:T(8,128)(2,1)S(1)}, bf16[2,192,768]{2,1,0:T(8,128)(2,1)S(1)}) custom-call(bf16[4,2,128,192]{3,2,1,0:T(8,128)(2,1)S(1)} %bitcast.87, bf16[128,1536]{1,0:T(8,128)(2,1)S(1)} %bitcast.78, ...), custom_call_target="tpu_custom_call" | custom-call | tf_op jit(solution)/shard_map/middle_step/pallas_call | solution.py:1011
  266.2 0.8 copy-done.26
  267.0 16.2 %dispatch.1 = (bf16[8,3,80,1536]{3,2,1,0:T(8,128)(2,1)}, bf16[8,3,80,1536]{3,2,1,0:T(8,128)(2,1)}, f32[8,3,80,1]{3,2,1,0:T(8,128)S(1)}, bf16[8,240,256]{2,1,0:T(8,128)(2,1)S(1)}, f32[16,128,128]{2,1,0:T(8,128)S(1)}) custom-call(s32[1]{0:T(128)} %bitcast.base, bf16[16,128,1536]{2,1,0:T(8,128)(2,1)} %bitcast.99, bf16[16,128,1664]{2,1,0:T(8,128)(2,1)} %bitcast.101, ...), custom_call_target="tpu_custom_call" | custom-call | tf_op jit(solution)/shard_map/dispatch/pallas_call | solution.py:446
  283.2 1.0 copy-done.23
  284.2 41.3 %experts.1 = (bf16[8,3,80,1536]{3,2,1,0:T(8,128)(2,1)}, bf16[8,3,80,1664]{3,2,1,0:T(8,128)(2,1)}, bf16[5,192,768]{2,1,0:T(8,128)(2,1)}, bf16[5,192,768]{2,1,0:T(...) custom-call(s32[4]{0:T(128)} %pad_add_fusion.refs_0_, ...), custom_call_target="tpu_custom_call" | custom-call | flops 22649241600 | bytes 62914560 | tf_op jit(solution)/shard_map/experts/pallas_call | solution.py:566
  325.5 7.3 %convolution_convert_fusion.1 = bf16[8,256,1536]{2,1,0:T(8,128)(2,1)} fusion(bf16[8,240,256]{2,1,0:T(8,128)(2,1)S(1)} %get-tuple-element.78, bf16[8,240,1536]{2,1,0:T(8,128)(2,1)} %bitcast.102), kind=kOutput, calls=%fused_computation.1 | convolution fusion | flops 1513095168 | bytes 13172736 | tf_op jit(solution)/shard_map/prt,prd->ptd/dot_general | solution.py:1794
  332.8 5.0 convolution_convert_fusion
  337.8 129.7 %router_step.1 = (bf16[128,128]{1,0:T(8,128)(2,1)S(1)}, f32[1,1536]{1,0:T(1,128)S(1)}, f32[128,1536]{1,0:T(8,128)S(1)}, bf16[4,2,128,192]{3,2,1,0:T(8,128)(2,1)S...) custom-call(bf16[4,2,2,128,1664]{4,3,2,1,0:T(8,128)(2,1)} %bitcast.9, ...), custom_call_target="tpu_custom_call" | custom-call | tf_op jit(solution)/shard_map/router_step/pallas_call | solution.py:1011
  467.6 2.5 fusion.5
  470.1 2.0 add_convert_fusion.2
  472.1 2.9 add_convert_fusion.1
  475.0 1.5 concatenate.32
  476.6 6.9 %collective-permute-start.1 = (bf16[5,192,768]{2,1,0:T(8,128)(2,1)}, bf16[5,192,768]{2,1,0:T(8,128)(2,1)}, u32[]{:S(2)}, u32[]{:S(2)}) collective-permute-start(bf16[5,192,768]{2,1,0:T(8,128)(2,1)} %get-tuple-element.121), channel_id=1, source_target_pairs={{0,4},{4,0},{1,5},{5,1},{2,6},{6,2},{3,7},{7,3},{8,12},{12,8},{9,1... | collective-permute-start | bytes 4423688 | tf_op jit(solution)/shard_map/ppermute | solution.py:1826
  483.6 2.0 collective-permute-start.3
  485.6 3.3 add_convert_fusion
  488.9 2.3 collective-permute-start.2
  491.2 1.2 pad_maximum_fusion.refs_6_
  492.4 24.8 %attention_backward.1 = (bf16[4,8,48,320]{3,2,1,0:T(8,128)(2,1)S(1)}, bf16[1024,1536]{1,0:T(8,128)(2,1)}) custom-call(bf16[1024,1536]{1,0:T(8,128)(2,1)} %get-tuple-element.99.hidden, bf16[1024,256]{1,0:T(8,128)(2,1)S(1)} %copy-done.9, bf16[1024,256]{1,0:T(8,128)(2,1)S(1)} %copy-done.11, bf16[1024,256]{1,0:T(8,128)(2,1)S(1)} %copy-done.13, ...), custom_call_target="tpu_custom_call" | custom-call | tf_op jit(solution)/shard_map/attention_backward/pallas_call | solution.py:1664
  517.2 3.6 convolution_convert_fusion.2
  520.8 103.0 %last_step.1 = (f32[128,1536]{1,0:T(8,128)S(1)}, bf16[4,2,48,320]{3,2,1,0:T(8,128)(2,1)S(1)}, f32[48,1536]{1,0:T(8,128)S(1)}, f32[48,128]{1,0:T(8,128)S(1)}) custom-call(bf16[4,2,128,1536]{3,2,1,0:T(8,128)(2,1)} %bitcast.105, bf16[128,1536]{1,0:T(8,128)(2,1)S(1)} %bitcast.79, f32[128,1536]{1,0:T(8,128)S(1)} %get-tuple-element.111.refs_2_, ...), custom_call_target="tpu_custom_call" | custom-call | tf_op jit(solution)/shard_map/last_step/pallas_call | solution.py:1011
  624.0 0.8 slice_bitcast_fusion.1
  624.8 0.7 copy.58
  625.5 0.7 reshape.251
  626.3 0.2 copy.55
  626.5 0.9 reshape.249
  627.4 1.0 copy.56
  628.3 0.7 reshape.250
  629.1 0.7 slice_reduce_fusion
  629.8 0.3 fusion
  630.1 0.5 convert_divide_fusion
  630.6 0.8 copy-done.27
  631.4 11.9 %place_units.1 = (f32[10,192,1024]{2,1,0:T(8,128)}, f32[10,192,512]{2,1,0:T(8,128)}) custom-call(s32[1]{0:T(128)} %bitcast.21.refs_0_, bf16[5,192,768]{2,1,0:T(8,128)(2,1)} %get-tuple-element.120.refs_1_.refs_7_, bf16[5,192,768]{2,1,0:T(8,128)(2,1)} %collective-permute-done.1.refs_2_.refs_8_, bf16[5,192,768]{2,1,0:T(8,128)(2,1)} %collective-permute-done.2.refs_3_.refs_9_, ...), custom_call_target="tpu_custom_call" | custom-call | tf_op jit(solution)/shard_map/place_units/pallas_call | solution.py:631
  643.3 0.7 copy.63
  644.0 0.9 copy.64
  644.9 0.7 copy.65
  (102 shorter events, 1.0 us)
Async XLA Ops:
  0.6 7.3 %copy-start.6 = (bf16[1,128,1536]{2,1,0:T(8,128)(2,1)S(1)}, bf16[1,128,1536]{2,1,0:T(8,128)(2,1)}, u32[]{:S(2)}) copy-start(bf16[1,128,1536]{2,1,0:T(8,128)(2,1)} %param.15) | copy-start | bytes 1179652
  0.7 7.4 %copy-start.1 = (bf16[1,128,1536]{2,1,0:T(8,128)(2,1)S(1)}, bf16[1,128,1536]{2,1,0:T(8,128)(2,1)}, u32[]{:S(2)}) copy-start(bf16[1,128,1536]{2,1,0:T(8,128)(2,1)} %param.14) | copy-start | bytes 1179652
  3.5 4.3 copy-start.32
  4.5 3.3 copy-start.34
  6.6 1.4 copy-start.28
  8.1 176.0 %copy-start.37 = (s32[1,16]{1,0:T(1,128)S(1)}, s32[1,16]{1,0:T(1,128)}, u32[]{:S(2)}) copy-start(s32[1,16]{1,0:T(1,128)} %param.17) | copy-start | bytes 196
  8.1 176.1 %copy-start.36 = (s32[1,2]{1,0:T(1,128)S(1)}, s32[1,2]{1,0:T(1,128)}, u32[]{:S(2)}) copy-start(s32[1,2]{1,0:T(1,128)} %param.16) | copy-start | bytes 28
  180.0 0.9 copy-start.24
  180.9 0.9 copy-start.25
  181.9 23.9 %copy-start = (bf16[4,2,2,2,48,384]{5,4,3,2,1,0:T(8,128)(2,1)}, bf16[4,2,2,2,48,384]{5,4,3,2,1,0:T(8,128)(2,1)S(1)}, u32[]{:S(2)}) copy-start(bf16[4,2,2,2,48,384]{5,4,3,2,1,0:T(8,128)(2,1)S(1)} %get-tuple-element.71) | copy-start | bytes 3538948
  181.9 27.6 %collective-permute-start = (bf16[2,192,768]{2,1,0:T(8,128)(2,1)}, bf16[2,192,768]{2,1,0:T(8,128)(2,1)}, u32[]{:S(2)}, u32[]{:S(2)}) collective-permute-start(bf16[2,192,768]{2,1,0:T(8,128)(2,1)} %get-tuple-element.75), channel_id=1, source_target_pairs={{0,24},{8,16},{16,8},{24,0},{1,25},{9,17},{17,9},{25,1},{2,26},{10... | collective-permute-start | bytes 1769480 | tf_op jit(solution)/shard_map/ppermute | solution.py:1755
  189.2 20.3 %copy-start.2 = (bf16[1,128,1536]{2,1,0:T(8,128)(2,1)S(1)}, bf16[1,128,1536]{2,1,0:T(8,128)(2,1)}, u32[]{:S(2)}) copy-start(bf16[1,128,1536]{2,1,0:T(8,128)(2,1)} %param.14) | copy-start | bytes 1179652
  205.7 0.8 copy-start.8
  206.5 0.8 copy-start.10
  207.3 0.8 copy-start.12
  208.1 0.8 copy-start.14
  209.5 57.5 %copy-start.5 = (bf16[1536,128]{1,0:T(8,128)(2,1)S(1)}, bf16[1536,128]{1,0:T(8,128)(2,1)}, u32[]{:S(2)}) copy-start(bf16[1536,128]{1,0:T(8,128)(2,1)} %concatenate.28.router_ref.refs_5_) | copy-start | bytes 1179652
  266.2 0.8 copy-start.26
  267.0 16.2 %copy-start.16 = (bf16[4,2,128,192]{3,2,1,0:T(8,128)(2,1)}, bf16[4,2,128,192]{3,2,1,0:T(8,128)(2,1)S(1)}, u32[]{:S(2)}) copy-start(bf16[4,2,128,192]{3,2,1,0:T(8,128)(2,1)S(1)} %get-tuple-element.113) | copy-start | bytes 1179652
  267.0 16.2 %copy-start.22 = (bf16[5,192,768]{2,1,0:T(8,128)(2,1)}, bf16[5,192,768]{2,1,0:T(8,128)(2,1)S(1)}, u32[]{:S(2)}) copy-start(bf16[5,192,768]{2,1,0:T(8,128)(2,1)S(1)} %get-tuple-element.86.refs_10_) | copy-start | bytes 4423684
  283.2 1.0 copy-start.23
  325.5 7.3 %slice-start = ((s8[6389760]{0:T(1024)(128)(4,1)}), s8[4194304]{0:T(1024)(128)(4,1)S(1)}, s32[]{:S(2)}) async-start(s8[6389760]{0:T(1024)(128)(4,1)} %bitcast.92), calls=%async_computation | async-start | bytes 8388608
  325.5 7.3 %slice-start.1 = ((s8[6389760]{0:T(1024)(128)(4,1)}), s8[2195456]{0:T(1024)(128)(4,1)S(1)}, s32[]{:S(2)}) async-start(s8[6389760]{0:T(1024)(128)(4,1)} %bitcast.92), calls=%async_computation.1 | async-start | bytes 4390912
  332.8 5.0 copy-start.7
  467.5 7.5 %copy-start.4 = (bf16[3,192,768]{2,1,0:T(8,128)(2,1)}, bf16[3,192,768]{2,1,0:T(8,128)(2,1)S(1)}, u32[]{:S(2)}) copy-start(bf16[3,192,768]{2,1,0:T(8,128)(2,1)S(1)} %get-tuple-element.125.refs_5_.refs_11_) | copy-start | bytes 2654212
  467.5 7.5 %copy-start.18 = (bf16[4,2,128,192]{3,2,1,0:T(8,128)(2,1)}, bf16[4,2,128,192]{3,2,1,0:T(8,128)(2,1)S(1)}, u32[]{:S(2)}) copy-start(bf16[4,2,128,192]{3,2,1,0:T(8,128)(2,1)S(1)} %get-tuple-element.109) | copy-start | bytes 1179652
  467.5 7.5 %copy-start.20 = (bf16[128,1536]{1,0:T(8,128)(2,1)}, bf16[128,1536]{1,0:T(8,128)(2,1)S(1)}, u32[]{:S(2)}) copy-start(bf16[128,1536]{1,0:T(8,128)(2,1)S(1)} %get-tuple-element.98) | copy-start | bytes 1179652
  467.6 4.5 copy-start.31
  476.5 14.6 %copy-start.30 = (bf16[4,2,2,2,48,1]{5,4,3,2,1,0:T(8,128)(2,1)S(1)}, bf16[4,2,2,2,48,1]{5,4,3,2,1,0:T(8,128)(2,1)}, u32[]{:S(2)}) copy-start(bf16[4,2,2,2,48,1]{5,4,3,2,1,0:T(8,128)(2,1)} %concatenate.32) | copy-start | bytes 9220
  476.5 15.9 %copy-start.9 = (bf16[1024,256]{1,0:T(8,128)(2,1)S(1)}, bf16[1024,256]{1,0:T(8,128)(2,1)}, u32[]{:S(2)}) copy-start(bf16[1024,256]{1,0:T(8,128)(2,1)} %copy-done.8) | copy-start | bytes 1572868
  476.5 15.9 %copy-start.11 = (bf16[1024,256]{1,0:T(8,128)(2,1)S(1)}, bf16[1024,256]{1,0:T(8,128)(2,1)}, u32[]{:S(2)}) copy-start(bf16[1024,256]{1,0:T(8,128)(2,1)} %copy-done.10) | copy-start | bytes 1572868
  476.5 15.9 %copy-start.13 = (bf16[1024,256]{1,0:T(8,128)(2,1)S(1)}, bf16[1024,256]{1,0:T(8,128)(2,1)}, u32[]{:S(2)}) copy-start(bf16[1024,256]{1,0:T(8,128)(2,1)} %copy-done.12) | copy-start | bytes 1572868
  476.5 15.9 %copy-start.15 = (f32[1024,128]{1,0:T(8,128)S(1)}, f32[1024,128]{1,0:T(8,128)}, u32[]{:S(2)}) copy-start(f32[1024,128]{1,0:T(8,128)} %copy-done.14) | copy-start | bytes 1572868
  476.5 15.9 %copy-start.19 = (bf16[4,2,128,192]{3,2,1,0:T(8,128)(2,1)S(1)}, bf16[4,2,128,192]{3,2,1,0:T(8,128)(2,1)}, u32[]{:S(2)}) copy-start(bf16[4,2,128,192]{3,2,1,0:T(8,128)(2,1)} %copy-done.18) | copy-start | bytes 1179652
  476.6 154.0 %collective-permute-start.4 = (bf16[2,192,768]{2,1,0:T(8,128)(2,1)}, bf16[2,192,768]{2,1,0:T(8,128)(2,1)S(1)}, u32[]{:S(2)}, u32[]{:S(2)}) collective-permute-start(bf16[2,192,768]{2,1,0:T(8,128)(2,1)} %add_convert_fusion.2), channel_id=1, source_target_pairs={{0,24},{8,16},{16,8},{24,0},{1,25},{9,17},{17,9},{25,1},{2,26},{10... | collective-permute-start | bytes 1769480 | tf_op jit(solution)/shard_map/ppermute | solution.py:1824
  476.6 154.0 %collective-permute-start.1 = (bf16[5,192,768]{2,1,0:T(8,128)(2,1)}, bf16[5,192,768]{2,1,0:T(8,128)(2,1)}, u32[]{:S(2)}, u32[]{:S(2)}) collective-permute-start(bf16[5,192,768]{2,1,0:T(8,128)(2,1)} %get-tuple-element.121), channel_id=1, source_target_pairs={{0,4},{4,0},{1,5},{5,1},{2,6},{6,2},{3,7},{7,3},{8,12},{12,8},{9,1... | collective-permute-start | bytes 4423688 | tf_op jit(solution)/shard_map/ppermute | solution.py:1826
  483.6 147.0 %collective-permute-start.3 = (bf16[5,192,768]{2,1,0:T(8,128)(2,1)}, bf16[5,192,768]{2,1,0:T(8,128)(2,1)}, u32[]{:S(2)}, u32[]{:S(2)}) collective-permute-start(bf16[5,192,768]{2,1,0:T(8,128)(2,1)} %add_convert_fusion.1), channel_id=1, source_target_pairs={{0,16},{8,24},{16,0},{24,8},{1,17},{9,25},{17,1},{25,9},{2,18},{10... | collective-permute-start | bytes 4423688 | tf_op jit(solution)/shard_map/ppermute | solution.py:1825
  488.9 141.7 %collective-permute-start.2 = (bf16[5,192,768]{2,1,0:T(8,128)(2,1)}, bf16[5,192,768]{2,1,0:T(8,128)(2,1)}, u32[]{:S(2)}, u32[]{:S(2)}) collective-permute-start(bf16[5,192,768]{2,1,0:T(8,128)(2,1)} %add_convert_fusion), channel_id=1, source_target_pairs={{0,8},{8,0},{16,24},{24,16},{1,9},{9,1},{17,25},{25,17},{2,10},{10... | collective-permute-start | bytes 4423688 | tf_op jit(solution)/shard_map/ppermute | solution.py:1827
  492.4 24.8 %copy-start.17 = (bf16[4,2,128,192]{3,2,1,0:T(8,128)(2,1)S(1)}, bf16[4,2,128,192]{3,2,1,0:T(8,128)(2,1)}, u32[]{:S(2)}) copy-start(bf16[4,2,128,192]{3,2,1,0:T(8,128)(2,1)} %copy-done.16) | copy-start | bytes 1179652
  517.2 3.6 copy-start.3
  623.8 6.0 copy-start.29
  623.8 6.0 copy-start.33
  623.8 6.0 copy-start.35
  623.8 6.2 copy-start.38
  630.6 0.8 copy-start.27
  631.4 11.9 %copy-start.21 = (bf16[128,1536]{1,0:T(8,128)(2,1)S(1)}, bf16[128,1536]{1,0:T(8,128)(2,1)}, u32[]{:S(2)}) copy-start(bf16[128,1536]{1,0:T(8,128)(2,1)} %copy-done.20) | copy-start | bytes 1179652

commit v6 on v5

--- a/solution.py
+++ b/solution.py
@@ -469,6 +469,33 @@
     )(base.reshape(1).astype(jnp.int32), hidden, marked, router)
 
 
+def combine_kernel(spread, made, back, made_out, back_out):
+    for rows, out in ((made, made_out), (back, back_out)):
+        width = rows.shape[-1]
+        total = contract_rows(spread[0], rows[0].reshape(-1, width))
+        out[...] = total.astype(out.dtype).reshape(out.shape)
+
+
+def combine(spread, made, back):
+    pairs, slots, both = spread.shape
+    count = both // 2
+    rows = lambda a: pl.BlockSpec((1, *a.shape[1:]), lambda p: (p,) + (0,) * (a.ndim - 1))
+    return pl.pallas_call(
+        combine_kernel,
+        grid=(pairs,),
+        in_specs=[rows(spread), rows(made), rows(back)],
+        out_specs=[
+            pl.BlockSpec((2, count, a.shape[-1]), lambda p: (p, 0, 0)) for a in (made, back)
+        ],
+        out_shape=[
+            jax.ShapeDtypeStruct((2 * pairs, count, a.shape[-1]), jnp.bfloat16)
+            for a in (made, back)
+        ],
+        compiler_params=pltpu.CompilerParams(vmem_limit_bytes=48 * 2**20),
+        name="combine",
+    )(spread, made, back)
+
+
 def expert_kernel(depth, meta, x_ref, g_ref, gate_ref, *refs):
     parts, (y_ref, d_ref), outs = refs[:10], refs[10:12], refs[12:20]
     weight, du_ref, act_ref = refs[20:]
@@ -996,6 +1023,10 @@
 
 VMEM_SPEC = pl.BlockSpec(memory_space=pltpu.VMEM)
 ANY_SPEC = pl.BlockSpec(memory_space=pl.ANY)
+
+
+def whole(shape):
+    return pl.BlockSpec(tuple(shape), lambda i: (0,) * len(shape))
 
 
 def exchange(kernel, name, number, inputs, specs, outs, out_specs, scratch):
@@ -1582,16 +1613,21 @@
     count, width = tokens.shape[0], HEADS // KV_HEADS * HEAD
     bf16, f32 = jnp.bfloat16, jnp.float32
     shape = jax.ShapeDtypeStruct
+    inputs = (tokens, weight, gain, cosine, sine, rows[:, None], starts[:, None], rows[None, :])
+    outs = (
+        [shape((count, D), bf16)]
+        + [shape((count, 256), bf16)] * 3
+        + [shape((count, width), bf16), shape((count, 128), f32)]
+    )
     return pl.pallas_call(
         attention_forward_kernel,
-        in_specs=[VMEM_SPEC] * 8,
-        out_specs=[VMEM_SPEC] * 6,
-        out_shape=[shape((count, D), bf16)]
-        + [shape((count, 256), bf16)] * 3
-        + [shape((count, width), bf16), shape((count, 128), f32)],
-        compiler_params=pltpu.CompilerParams(vmem_limit_bytes=48 * 2**20),
+        grid=(1,),
+        in_specs=[whole(a.shape) for a in inputs],
+        out_specs=[whole(a.shape) for a in outs],
+        out_shape=outs,
+        compiler_params=pltpu.CompilerParams(vmem_limit_bytes=56 * 2**20),
         name="attention_forward",
-    )(tokens, weight, gain, cosine, sine, rows[:, None], starts[:, None], rows[None, :])
+    )(*inputs)
 
 
 def attention_backward_kernel(
@@ -1661,14 +1697,20 @@
     count = hidden.shape[0]
     bf16, f32 = jnp.bfloat16, jnp.float32
     shape = jax.ShapeDtypeStruct
+    inputs = (
+        hidden, qk, keys, values, lse, upstream, weight, cosine, sine,
+        rows[:, None], starts[:, None], rows[None, :],
+    )
+    outs = [
+        shape((4, D // own // 4, own, upstream.shape[-1] + 2 * HEAD), bf16),
+        shape((count, D), bf16),
+    ]
     return pl.pallas_call(
         attention_backward_kernel,
-        in_specs=[VMEM_SPEC] * 12,
-        out_specs=[VMEM_SPEC] * 2,
-        out_shape=[
-            shape((4, D // own // 4, own, upstream.shape[-1] + 2 * HEAD), bf16),
-            shape((count, D), bf16),
-        ],
+        grid=(1,),
+        in_specs=[whole(a.shape) for a in inputs],
+        out_specs=[whole(a.shape) for a in outs],
+        out_shape=outs,
         scratch_shapes=[
             pltpu.VMEM((count, 384), bf16),
             pltpu.VMEM((count, 256), f32),
@@ -1676,12 +1718,9 @@
             pltpu.VMEM((count, 256), f32),
             pltpu.VMEM((count, 256), bf16),
         ],
-        compiler_params=pltpu.CompilerParams(vmem_limit_bytes=48 * 2**20),
+        compiler_params=pltpu.CompilerParams(vmem_limit_bytes=56 * 2**20),
         name="attention_backward",
-    )(
-        hidden, qk, keys, values, lse, upstream, weight, cosine, sine,
-        rows[:, None], starts[:, None], rows[None, :],
-    )
+    )(*inputs)
 
 
 def body_heads(
@@ -1790,22 +1829,14 @@
     )
     gates = lax.dynamic_index_in_dim(gates_blocks, z_index * n_exp + exp_index, 0, keepdims=False)
 
-    def to_tokens(rows):
-        a = jnp.einsum(
-            "prt,prd->ptd",
-            spread,
-            rows.reshape(pairs, held * 2 * slots, -1),
-            preferred_element_type=f32,
-        )
-        return a.astype(bf16).reshape(blocks, count, -1)
-
     meta = jnp.stack([shift, z_index, y_index, base]).astype(jnp.int32)
     made, back, *grads = run_experts(
         meta, row_in, row_up, slot_gate, parts
     )
+    made, back = combine(spread, made, back)
     logit_grad, grad_gain_two, grad_middle, grad_heads, output, far_sum, *others = router_step(
-        to_tokens(back).reshape(n_z, 2, 2, count, D + 128),
-        to_tokens(made).reshape(n_z, 2, 2, count, D),
+        back.reshape(n_z, 2, 2, count, D + 128),
+        made.reshape(n_z, 2, 2, count, D),
         middle,
         cotangent[0],
         gates,

time: 651 us -> 642 us (0.986)
  matrix products: 18.4 us -> 5.31 us
    pallas_call x2 -> x3, Pallas kernels: 41.2 us -> 56.2 us  [the longest x1 27 us: attention_backward(): pl.pallas_call(attention_backward_kernel, grid=(1,), in_specs=[whole(a.sh...]
    dot_general x2 -> x0, matrix products: 12.3 us -> none  [to_tokens(): jnp.einsum('prt,prd->ptd', spread, rows.reshape(pairs, held * 2 * slots,...]
    pallas_call x4, Pallas kernels: 461 us -> 451 us  [exchange(): pl.pallas_call(run, out_shape=outs, in_specs=specs, out_specs=out_specs,...]
  transfers between devices with their start and end apart: 5 -> 5, of which waited for: 0 -> 0; matrix products, arithmetic and copies ran while one was open for 3% -> 3% of each run, Pallas kernels for 22% -> 23%
where the time goes in v6:
time: 642 us; the launch traced here: 635 us
  Pallas kernels  576 us (90%)
  other arithmetic  20 us (3%)
  local copies, waits for them, and re-layouts  18.5 us (3%)
  starting transfers between devices  14.4 us (2%)
    pallas_call x4, Pallas kernels, exchange(): pl.pallas_call(run, out_shape=outs, in_specs=specs, out_specs=out_specs,...  451 us
    pallas_call x1, Pallas kernels, run_experts(): pl.pallas_call(lambda *refs: expert_kernel(depth, *refs), grid_spec=pltpu...  41.2 us
    pallas_call x1, Pallas kernels, attention_backward(): pl.pallas_call(attention_backward_kernel, grid=(1,), in_specs=[whole(a.sh...  27 us
    pallas_call x1, Pallas kernels, attention_forward(): pl.pallas_call(attention_forward_kernel, grid=(1,), in_specs=[whole(a.sha...  16.6 us
    pallas_call x1, Pallas kernels, dispatch(): pl.pallas_call(dispatch_kernel, grid_spec=pltpu.PrefetchScalarGridSpec(nu...  15.4 us
  transfers between devices with their start and end apart: 5, of which 0 were waited for; matrix products, arithmetic and copies ran while one was open for 3% of the time, Pallas kernels for 23%

profile of v6, /device:TPU:0, one launch (start us, length us, event | category | flops | bytes accessed | tf_op | source)
XLA Modules:
  0.0 635.3 jit_solution(3728610471784839892)
XLA Ops:
  0.7 0.8 convert_element_type.118
  1.5 0.7 convert_bitcast_fusion.1
  2.3 0.1 copy.50
  2.4 0.9 convert_element_type.116
  3.3 0.1 reshape.233
  3.4 0.9 convert_element_type.117
  4.4 0.1 reshape.234
  4.5 0.8 copy.51
  5.3 1.0 convert_element_type.115
  6.4 0.2 reshape.232
  6.7 0.1 fusion.10
  6.8 0.1 pad_maximum_fusion.2
  7.0 0.3 copy-done.16
  7.3 0.1 concatenate.27.refs_3_
  7.4 0.3 copy-done.1
  7.7 171.8 %share_inputs.1 = (bf16[4,2,128,1536]{3,2,1,0:T(8,128)(2,1)}, bf16[4,2,2,2,48,384]{5,4,3,2,1,0:T(8,128)(2,1)S(1)}, bf16[4,2,2,2,48,1536]{5,4,3,2,1,0:T(8,128)(2,...) custom-call(bf16[128,1536]{1,0:T(8,128)(2,1)S(1)} %bitcast.71, ...), custom_call_target="tpu_custom_call" | custom-call | tf_op jit(solution)/shard_map/share_inputs/pallas_call | solution.py:1042
  179.5 0.9 copy-done.13
  180.5 0.9 copy-done.14
  181.4 1.5 collective-permute-start
  182.9 0.5 convert_reduce_fusion
  183.5 0.9 slice.51
  184.4 0.1 select_reduce_fusion
  184.6 0.2 copy.52
  184.8 0.6 reshape.252.gain.refs_3_
  185.4 1.1 concatenate.28.router_ref.refs_5_
  186.5 3.1 multiply_sine_fusion
  189.6 0.6 fusion.17.key_rows
  190.2 1.1 compare_select_fusion
  191.3 16.6 %attention_forward.1 = (bf16[1024,1536]{1,0:T(8,128)(2,1)}, bf16[1024,256]{1,0:T(8,128)(2,1)}, bf16[1024,256]{1,0:T(8,128)(2,1)}, bf16[1024,256]{1,0:T(8,128)(2,...) custom-call(bf16[1024,1536]{1,0:T(8,128)(2,1)} %bitcast.94, bf16[1536,384]{1,0:T(8,128)(2,1)} %bitcast.69, ...), custom_call_target="tpu_custom_call" | custom-call | tf_op jit(solution)/shard_map/attention_forward/pallas_call | solution.py:1622
  207.9 0.6 pad_add_fusion.refs_0_
  208.5 1.3 copy-done.7
  209.8 56.6 %middle_step.1 = (bf16[4,2,128,192]{3,2,1,0:T(8,128)(2,1)S(1)}, f32[128,1536]{1,0:T(8,128)S(1)}, bf16[4,2,2,128,1536]{4,3,2,1,0:T(8,128)(2,1)}, bf16[5,192,768]{2,1,0:T(8,128)(2,1)S(1)}, bf16[2,192,768]{2,1,0:T(8,128)(2,1)S(1)}) custom-call(bf16[4,2,128,192]{3,2,1,0:T(8,128)(2,1)S(1)} %bitcast.81, bf16[128,1536]{1,0:T(8,128)(2,1)S(1)} %bitcast.72, ...), custom_call_target="tpu_custom_call" | custom-call | tf_op jit(solution)/shard_map/middle_step/pallas_call | solution.py:1042
  266.4 1.2 copy-done.11
  267.6 0.8 copy-done.15
  268.4 15.4 %dispatch.1 = (bf16[8,3,80,1536]{3,2,1,0:T(8,128)(2,1)}, bf16[8,3,80,1536]{3,2,1,0:T(8,128)(2,1)}, f32[8,3,80,1]{3,2,1,0:T(8,128)S(1)}, bf16[8,240,256]{2,1,0:T(8,128)(2,1)S(1)}, f32[16,128,128]{2,1,0:T(8,128)S(1)}) custom-call(s32[1]{0:T(128)} %bitcast.base, bf16[16,128,1536]{2,1,0:T(8,128)(2,1)} %bitcast.88, bf16[16,128,1664]{2,1,0:T(8,128)(2,1)} %bitcast.90, ...), custom_call_target="tpu_custom_call" | custom-call | tf_op jit(solution)/shard_map/dispatch/pallas_call | solution.py:446
  283.8 1.0 copy-done.12
  284.8 41.2 %experts.1 = (bf16[8,3,80,1536]{3,2,1,0:T(8,128)(2,1)}, bf16[8,3,80,1664]{3,2,1,0:T(8,128)(2,1)}, bf16[5,192,768]{2,1,0:T(8,128)(2,1)}, bf16[5,192,768]{2,1,0:T(...) custom-call(s32[4]{0:T(128)} %pad_add_fusion.refs_0_, ...), custom_call_target="tpu_custom_call" | custom-call | flops 22649241600 | bytes 62914560 | tf_op jit(solution)/shard_map/experts/pallas_call | solution.py:593
  326.0 12.6 %combine.1 = (bf16[16,128,1536]{2,1,0:T(8,128)(2,1)}, bf16[16,128,1664]{2,1,0:T(8,128)(2,1)}) custom-call(bf16[8,240,256]{2,1,0:T(8,128)(2,1)S(1)} %get-tuple-element.80.spread, bf16[8,3,80,1536]{3,2,1,0:T(8,128)(2,1)} %get-tuple-element.92.made, bf16[8,3,80,1664]{3,2,1,0:T(8,128)(2,1)} %get-tuple-element.93.back), custom_call_target="tpu_custom_call" | custom-call | tf_op jit(solution)/shard_map/combine/pallas_call | solution.py:483
  338.6 120.1 %router_step.1 = (bf16[128,128]{1,0:T(8,128)(2,1)S(1)}, f32[1,1536]{1,0:T(1,128)S(1)}, f32[128,1536]{1,0:T(8,128)S(1)}, bf16[4,2,128,192]{3,2,1,0:T(8,128)(2,1)S...) custom-call(bf16[4,2,2,128,1664]{4,3,2,1,0:T(8,128)(2,1)} %bitcast.9, ...), custom_call_target="tpu_custom_call" | custom-call | tf_op jit(solution)/shard_map/router_step/pallas_call | solution.py:1042
  458.7 1.7 fusion.5
  460.4 2.0 add_convert_fusion.2
  462.4 2.9 add_convert_fusion.1
  465.3 0.7 concatenate.32
  466.1 8.5 %collective-permute-start.1 = (bf16[5,192,768]{2,1,0:T(8,128)(2,1)}, bf16[5,192,768]{2,1,0:T(8,128)(2,1)}, u32[]{:S(2)}, u32[]{:S(2)}) collective-permute-start(bf16[5,192,768]{2,1,0:T(8,128)(2,1)} %get-tuple-element.125), channel_id=1, source_target_pairs={{0,4},{4,0},{1,5},{5,1},{2,6},{6,2},{3,7},{7,3},{8,12},{12,8},{9,1... | collective-permute-start | bytes 4423688 | tf_op jit(solution)/shard_map/ppermute | solution.py:1857
  474.6 1.5 collective-permute-start.3
  476.1 3.3 add_convert_fusion
  479.4 2.8 collective-permute-start.2
  482.2 0.2 pad_maximum_fusion.refs_6_
  482.4 27.0 %attention_backward.1 = (bf16[4,8,48,320]{3,2,1,0:T(8,128)(2,1)}, bf16[1024,1536]{1,0:T(8,128)(2,1)}) custom-call(bf16[1024,1536]{1,0:T(8,128)(2,1)} %get-tuple-element.103.hidden, bf16[1024,256]{1,0:T(8,128)(2,1)} %get-tuple-element.104.qk, bf16[1024,256]{1,0:T(8,128)(2,1)} %get-tuple-element.105.keys, bf16[1024,256]{1,0:T(8,128)(2,1)} %get-tuple-element.106.values, ...), custom_call_target="tpu_custom_call" | custom-call | tf_op jit(solution)/shard_map/attention_backward/pallas_call | solution.py:1708
  509.5 3.6 convolution_convert_fusion
  513.1 102.2 %last_step.1 = (f32[128,1536]{1,0:T(8,128)S(1)}, bf16[4,2,48,320]{3,2,1,0:T(8,128)(2,1)S(1)}, f32[48,1536]{1,0:T(8,128)S(1)}, f32[48,128]{1,0:T(8,128)S(1)}) custom-call(bf16[4,2,128,1536]{3,2,1,0:T(8,128)(2,1)} %bitcast.95, bf16[128,1536]{1,0:T(8,128)(2,1)S(1)} %bitcast.73, f32[128,1536]{1,0:T(8,128)S(1)} %get-tuple-element.115.refs_2_, ...), custom_call_target="tpu_custom_call" | custom-call | tf_op jit(solution)/shard_map/last_step/pallas_call | solution.py:1042
  615.4 0.1 slice_bitcast_fusion.1
  615.5 0.7 copy.58
  616.3 0.7 reshape.251
  617.0 0.2 copy.55
  617.3 0.9 reshape.249
  618.2 0.7 reshape.250
  618.9 0.7 slice_reduce_fusion
  619.6 0.3 fusion
  619.9 0.5 convert_divide_fusion
  620.5 12.0 %place_units.1 = (f32[10,192,1024]{2,1,0:T(8,128)}, f32[10,192,512]{2,1,0:T(8,128)}) custom-call(s32[1]{0:T(128)} %bitcast.21.refs_0_, bf16[5,192,768]{2,1,0:T(8,128)(2,1)} %get-tuple-element.124.refs_1_.refs_7_, bf16[5,192,768]{2,1,0:T(8,128)(2,1)} %collective-permute-done.1.refs_2_.refs_8_, bf16[5,192,768]{2,1,0:T(8,128)(2,1)} %collective-permute-done.2.refs_3_.refs_9_, ...), custom_call_target="tpu_custom_call" | custom-call | tf_op jit(solution)/shard_map/place_units/pallas_call | solution.py:658
  632.5 0.7 copy.63
  633.2 0.9 copy.64
  634.1 0.7 copy.65
  (72 shorter events, 0.8 us)
Async XLA Ops:
  0.6 6.0 copy-start.23
  3.4 3.4 copy-start.19
  4.5 2.3 copy-start.21
  5.3 2.0 copy-start.3
  6.6 0.7 copy-start.16
  6.6 1.1 copy-start.1
  179.5 1.0 copy-start.13
  180.5 0.9 copy-start.14
  181.4 5.1 copy-start
  181.4 3.0 copy-start.25
  181.4 3.1 copy-start.24
  181.4 27.1 %collective-permute-start = (bf16[2,192,768]{2,1,0:T(8,128)(2,1)}, bf16[2,192,768]{2,1,0:T(8,128)(2,1)S(1)}, u32[]{:S(2)}, u32[]{:S(2)}) collective-permute-start(bf16[2,192,768]{2,1,0:T(8,128)(2,1)} %get-tuple-element.77), channel_id=1, source_target_pairs={{0,24},{8,16},{16,8},{24,0},{1,25},{9,17},{17,9},{25,1},{2,26},{10... | collective-permute-start | bytes 1769480 | tf_op jit(solution)/shard_map/ppermute | solution.py:1794
  208.5 57.9 %copy-start.5 = (bf16[2,192,768]{2,1,0:T(8,128)(2,1)}, bf16[2,192,768]{2,1,0:T(8,128)(2,1)S(1)}, u32[]{:S(2)}) copy-start(bf16[2,192,768]{2,1,0:T(8,128)(2,1)S(1)} %collective-permute-done.refs_5_.refs_8_) | copy-start | bytes 1769476
  208.5 1.3 copy-start.7
  266.4 1.2 copy-start.11
  267.6 0.8 copy-start.15
  283.8 1.0 copy-start.12
  458.6 6.7 %copy-start.2 = (bf16[3,192,768]{2,1,0:T(8,128)(2,1)}, bf16[3,192,768]{2,1,0:T(8,128)(2,1)S(1)}, u32[]{:S(2)}) copy-start(bf16[3,192,768]{2,1,0:T(8,128)(2,1)S(1)} %get-tuple-element.129.refs_5_.refs_11_) | copy-start | bytes 2654212
  458.6 6.7 %copy-start.6 = (bf16[4,2,128,192]{3,2,1,0:T(8,128)(2,1)}, bf16[4,2,128,192]{3,2,1,0:T(8,128)(2,1)S(1)}, u32[]{:S(2)}) copy-start(bf16[4,2,128,192]{3,2,1,0:T(8,128)(2,1)S(1)} %get-tuple-element.113) | copy-start | bytes 1179652
  458.6 6.7 %copy-start.8 = (bf16[128,1536]{1,0:T(8,128)(2,1)}, bf16[128,1536]{1,0:T(8,128)(2,1)S(1)}, u32[]{:S(2)}) copy-start(bf16[128,1536]{1,0:T(8,128)(2,1)S(1)} %get-tuple-element.102) | copy-start | bytes 1179652
  458.6 3.7 copy-start.18
  466.0 154.4 %collective-permute-start.4 = (bf16[2,192,768]{2,1,0:T(8,128)(2,1)}, bf16[2,192,768]{2,1,0:T(8,128)(2,1)}, u32[]{:S(2)}, u32[]{:S(2)}) collective-permute-start(bf16[2,192,768]{2,1,0:T(8,128)(2,1)} %add_convert_fusion.2), channel_id=1, source_target_pairs={{0,24},{8,16},{16,8},{24,0},{1,25},{9,17},{17,9},{25,1},{2,26},{10... | collective-permute-start | bytes 1769480 | tf_op jit(solution)/shard_map/ppermute | solution.py:1855
  466.1 154.3 %collective-permute-start.1 = (bf16[5,192,768]{2,1,0:T(8,128)(2,1)}, bf16[5,192,768]{2,1,0:T(8,128)(2,1)}, u32[]{:S(2)}, u32[]{:S(2)}) collective-permute-start(bf16[5,192,768]{2,1,0:T(8,128)(2,1)} %get-tuple-element.125), channel_id=1, source_target_pairs={{0,4},{4,0},{1,5},{5,1},{2,6},{6,2},{3,7},{7,3},{8,12},{12,8},{9,1... | collective-permute-start | bytes 4423688 | tf_op jit(solution)/shard_map/ppermute | solution.py:1857
  474.6 145.8 %collective-permute-start.3 = (bf16[5,192,768]{2,1,0:T(8,128)(2,1)}, bf16[5,192,768]{2,1,0:T(8,128)(2,1)}, u32[]{:S(2)}, u32[]{:S(2)}) collective-permute-start(bf16[5,192,768]{2,1,0:T(8,128)(2,1)} %add_convert_fusion.1), channel_id=1, source_target_pairs={{0,16},{8,24},{16,0},{24,8},{1,17},{9,25},{17,1},{25,9},{2,18},{10... | collective-permute-start | bytes 4423688 | tf_op jit(solution)/shard_map/ppermute | solution.py:1856
  479.4 141.0 %collective-permute-start.2 = (bf16[5,192,768]{2,1,0:T(8,128)(2,1)}, bf16[5,192,768]{2,1,0:T(8,128)(2,1)}, u32[]{:S(2)}, u32[]{:S(2)}) collective-permute-start(bf16[5,192,768]{2,1,0:T(8,128)(2,1)} %add_convert_fusion), channel_id=1, source_target_pairs={{0,8},{8,0},{16,24},{24,16},{1,9},{9,1},{17,25},{25,17},{2,10},{10... | collective-permute-start | bytes 4423688 | tf_op jit(solution)/shard_map/ppermute | solution.py:1858
  509.5 3.6 copy-start.4
  509.5 3.6 copy-start.10
  615.5 4.1 copy-start.17
  615.5 4.1 copy-start.20
  615.5 4.1 copy-start.22
  617.0 2.9 copy-start.26
  620.5 12.0 %copy-start.9 = (bf16[128,1536]{1,0:T(8,128)(2,1)S(1)}, bf16[128,1536]{1,0:T(8,128)(2,1)}, u32[]{:S(2)}) copy-start(bf16[128,1536]{1,0:T(8,128)(2,1)} %copy-done.8) | copy-start | bytes 1179652

commit v7 on v6

--- a/solution.py
+++ b/solution.py
@@ -519,7 +519,7 @@
     first = jnp.logical_or(j == 0, lax.rem(j + shift, 2) == 0)
     keep = jnp.where(first, 0.0, 1.0)
     pairs, _, rows, _ = x_ref.shape
-    step = 4
+    step = 8
 
     def forward(i, carry):
         at = pl.ds(i * step, step)
@@ -1046,7 +1046,7 @@
         out_specs=out_specs,
         scratch_shapes=sum(scratch, []),
         compiler_params=pltpu.CompilerParams(
-            collective_id=number, has_side_effects=True, vmem_limit_bytes=48 * 2**20
+            collective_id=number, has_side_effects=True, vmem_limit_bytes=50 * 2**20
         ),
         name=name,
     )(*inputs)
@@ -1557,7 +1557,8 @@
 
 
 def attention_forward_kernel(
-    tok, weight, gain, cosine, sine, rows, starts, key_rows, hidden, qk, keys, values, out, lse
+    experts, tok, weight, cosine, sine, rows, starts, key_rows,
+    hidden, qk, keys, values, out, lse, gains, router
 ):
     bf16, f32 = jnp.bfloat16, jnp.float32
     swap = half_swap()
@@ -1566,12 +1567,17 @@
     to_values = pick(128, 256, bf16, lambda r, c: (c < width) & (r == c % HEAD))
     block = 256
     steps = tok.shape[0] // block
+    first = width + 2 * HEAD
+    chosen = pick(8, weight.shape[1], bf16, lambda r, c: (r < 2) & (c == first + experts + r))
+    gains[...] = contract_cols(chosen, weight[...])
+    to_router = pick(128, 128, bf16, lambda r, c: (c < experts) & (r + 256 == first + c))
+    router[...] = jnp.dot(weight[:, 256:], to_router, preferred_element_type=f32).astype(bf16)
 
     def project(b, carry):
         at = pl.ds(pl.multiple_of(b * block, block), block)
         x = tok[at, :].astype(f32)
         normed = x * lax.rsqrt(jnp.mean(x * x, axis=-1, keepdims=True) + EPSILON)
-        h = (normed * gain[...]).astype(bf16)
+        h = (normed * gains[0:1, :]).astype(bf16)
         hidden[at, :] = h
         t = jnp.dot(h, weight[...], preferred_element_type=f32)
         u = t[:, :256]
@@ -1609,18 +1615,19 @@
     lax.fori_loop(0, steps, attend, 0)
 
 
-def attention_forward(tokens, weight, gain, cosine, sine, rows, starts):
+def attention_forward(experts, tokens, weight, cosine, sine, rows, starts):
     count, width = tokens.shape[0], HEADS // KV_HEADS * HEAD
     bf16, f32 = jnp.bfloat16, jnp.float32
     shape = jax.ShapeDtypeStruct
-    inputs = (tokens, weight, gain, cosine, sine, rows[:, None], starts[:, None], rows[None, :])
+    inputs = (tokens, weight, cosine, sine, rows[:, None], starts[:, None], rows[None, :])
     outs = (
         [shape((count, D), bf16)]
         + [shape((count, 256), bf16)] * 3
         + [shape((count, width), bf16), shape((count, 128), f32)]
+        + [shape((8, D), f32), shape((D, 128), bf16)]
     )
     return pl.pallas_call(
-        attention_forward_kernel,
+        lambda *refs: attention_forward_kernel(experts, *refs),
         grid=(1,),
         in_specs=[whole(a.shape) for a in inputs],
         out_specs=[whole(a.shape) for a in outs],
@@ -1795,10 +1802,6 @@
     token_all = token_all.reshape(group, D)
     slices = slices.reshape(D, -1)
     wo = wo.reshape(HEADS * HEAD, D)
-    small = slices[:, width + 2 * HEAD :]
-    weight_r = jnp.concatenate([small[:, :experts], jnp.zeros((D, 128 - experts), bf16)], axis=1)
-    gain_one_f = small[:, experts].astype(f32)[None, :]
-    gain_two_f = small[:, experts + 1].astype(f32)[None, :]
 
     perm_row = span_perm[0]
     first_len = lengths[0, 0]
@@ -1809,9 +1812,10 @@
     )
     angle = (rows - starts).astype(f32)[:, None] * freqs[None, :]
     cosine, sine = jnp.cos(angle), jnp.sin(angle)
-    hidden_all, queries, keys, values, attended_b, log_total = attention_forward(
-        token_all, slices, gain_one_f, cosine, sine, rows, starts
-    )
+    hidden_all, queries, keys, values, attended_b, log_total, gains, weight_r = attention_forward(
+        experts, token_all, slices, cosine, sine, rows, starts
+    )
+    gain_one_f, gain_two_f = gains[0:1], gains[1:2]
     own_attended, middle, hidden_blocks, *passed = middle_step(
         attended_b.reshape(n_z, n_y, count, width), tokens[0], wo, gain_two_f, [near[1], late]
     )

time: 642 us -> 637 us (level)
  starting transfers between devices: 14.4 us -> 6.75 us
    ppermute x1, starting transfers between devices: 8.49 us -> 0.07 us  [body_heads(): other = lax.ppermute(grads[4], 'y', swap_y)]
where the time goes in v7:
time: 637 us; the launch traced here: 628 us
  Pallas kernels  579 us (91%)
  other arithmetic  19.5 us (3%)
  local copies, waits for them, and re-layouts  16.3 us (3%)
  starting transfers between devices  6.75 us (1%)
    pallas_call x4, Pallas kernels, exchange(): pl.pallas_call(run, out_shape=outs, in_specs=specs, out_specs=out_specs,...  455 us
    pallas_call x1, Pallas kernels, run_experts(): pl.pallas_call(lambda *refs: expert_kernel(depth, *refs), grid_spec=pltpu...  39.8 us
    pallas_call x1, Pallas kernels, attention_backward(): pl.pallas_call(attention_backward_kernel, grid=(1,), in_specs=[whole(a.sh...  27 us
    pallas_call x1, Pallas kernels, attention_forward(): pl.pallas_call(lambda *refs: attention_forward_kernel(experts, *refs), gr...  17 us
    pallas_call x1, Pallas kernels, dispatch(): pl.pallas_call(dispatch_kernel, grid_spec=pltpu.PrefetchScalarGridSpec(nu...  15.6 us
  transfers between devices with their start and end apart: 5, of which 0 were waited for; matrix products, arithmetic and copies ran while one was open for 3% of the time, Pallas kernels for 23%

profile of v7, /device:TPU:0, one launch (start us, length us, event | category | flops | bytes accessed | tf_op | source)
XLA Modules:
  0.0 628.5 jit_solution(3330838251188188760)
XLA Ops:
  0.7 0.8 convert_element_type.92
  1.4 0.1 pad.11.clone
  1.5 0.7 convert_bitcast_fusion.1
  2.2 0.1 maximum_maximum_fusion
  2.3 0.1 copy.50
  2.4 0.9 convert_element_type.90
  3.3 0.1 reshape.209
  3.4 0.9 convert_element_type.91
  4.4 0.1 reshape.210
  4.5 0.8 copy.51
  5.3 1.0 convert_element_type.89
  6.4 0.2 reshape.208
  6.7 0.1 fusion.10
  6.8 0.1 pad_maximum_fusion.2
  7.0 0.3 copy-done.10
  7.3 0.1 concatenate.24.refs_3_
  7.4 0.3 copy-done
  7.7 171.8 %share_inputs.1 = (bf16[4,2,128,1536]{3,2,1,0:T(8,128)(2,1)}, bf16[4,2,2,2,48,384]{5,4,3,2,1,0:T(8,128)(2,1)}, bf16[4,2,2,2,48,1536]{5,4,3,2,1,0:T(8,128)(2,1)},...) custom-call(bf16[128,1536]{1,0:T(8,128)(2,1)S(1)} %bitcast.67, ...), custom_call_target="tpu_custom_call" | custom-call | tf_op jit(solution)/shard_map/share_inputs/pallas_call | solution.py:1042
  179.6 0.9 copy-done.7
  180.5 0.9 copy-done.8
  181.4 1.5 collective-permute-start
  182.9 0.1 select_reduce_fusion
  183.1 0.2 copy.52
  183.3 1.1 compare_select_fusion
  184.4 3.1 multiply_sine_fusion
  187.5 0.6 fusion.17.refs_6_.key_rows
  188.1 17.0 %attention_forward.1 = (bf16[1024,1536]{1,0:T(8,128)(2,1)}, bf16[1024,256]{1,0:T(8,128)(2,1)}, bf16[1024,256]{1,0:T(8,128)(2,1)}, bf16[1024,256]{1,0:T(8,128)(2,...) custom-call(bf16[1024,1536]{1,0:T(8,128)(2,1)} %bitcast.91, ...), custom_call_target="tpu_custom_call" | custom-call | tf_op jit(solution)/shard_map/attention_forward/pallas_call | solution.py:1629
  205.1 0.6 pad_add_fusion.refs_0_
  205.7 0.9 fusion.24
  206.6 1.2 copy-done.5
  207.9 56.7 %middle_step.1 = (bf16[4,2,128,192]{3,2,1,0:T(8,128)(2,1)S(1)}, f32[128,1536]{1,0:T(8,128)S(1)}, bf16[4,2,2,128,1536]{4,3,2,1,0:T(8,128)(2,1)}, bf16[5,192,768]{2,1,0:T(8,128)(2,1)}, bf16[2,192,768]{2,1,0:T(8,128)(2,1)S(1)}) custom-call(bf16[4,2,128,192]{3,2,1,0:T(8,128)(2,1)S(1)} %bitcast.76, bf16[128,1536]{1,0:T(8,128)(2,1)S(1)} %bitcast.68, ...), custom_call_target="tpu_custom_call" | custom-call | tf_op jit(solution)/shard_map/middle_step/pallas_call | solution.py:1042
  264.6 15.6 %dispatch.1 = (bf16[8,3,80,1536]{3,2,1,0:T(8,128)(2,1)}, bf16[8,3,80,1536]{3,2,1,0:T(8,128)(2,1)}, f32[8,3,80,1]{3,2,1,0:T(8,128)S(1)}, bf16[8,240,256]{2,1,0:T(8,128)(2,1)S(1)}, f32[16,128,128]{2,1,0:T(8,128)S(1)}) custom-call(s32[1]{0:T(128)} %bitcast.base, bf16[16,128,1536]{2,1,0:T(8,128)(2,1)} %bitcast.83, bf16[16,128,1664]{2,1,0:T(8,128)(2,1)} %bitcast.85, ...), custom_call_target="tpu_custom_call" | custom-call | tf_op jit(solution)/shard_map/dispatch/pallas_call | solution.py:446
  280.2 0.9 copy-done.6
  281.2 39.8 %experts.1 = (bf16[8,3,80,1536]{3,2,1,0:T(8,128)(2,1)}, bf16[8,3,80,1664]{3,2,1,0:T(8,128)(2,1)}, bf16[5,192,768]{2,1,0:T(8,128)(2,1)}, bf16[5,192,768]{2,1,0:T(...) custom-call(s32[4]{0:T(128)} %pad_add_fusion.refs_0_, ...), custom_call_target="tpu_custom_call" | custom-call | flops 22649241600 | bytes 62914560 | tf_op jit(solution)/shard_map/experts/pallas_call | solution.py:593
  321.0 12.6 %combine.1 = (bf16[16,128,1536]{2,1,0:T(8,128)(2,1)}, bf16[16,128,1664]{2,1,0:T(8,128)(2,1)}) custom-call(bf16[8,240,256]{2,1,0:T(8,128)(2,1)S(1)} %get-tuple-element.84.spread, bf16[8,3,80,1536]{3,2,1,0:T(8,128)(2,1)} %get-tuple-element.96.made, bf16[8,3,80,1664]{3,2,1,0:T(8,128)(2,1)} %get-tuple-element.97.back), custom_call_target="tpu_custom_call" | custom-call | tf_op jit(solution)/shard_map/combine/pallas_call | solution.py:483
  333.5 125.4 %router_step.1 = (bf16[128,128]{1,0:T(8,128)(2,1)S(1)}, f32[1,1536]{1,0:T(1,128)S(1)}, f32[128,1536]{1,0:T(8,128)S(1)}, bf16[4,2,128,192]{3,2,1,0:T(8,128)(2,1)S...) custom-call(bf16[4,2,2,128,1664]{4,3,2,1,0:T(8,128)(2,1)} %bitcast.8, ...), custom_call_target="tpu_custom_call" | custom-call | tf_op jit(solution)/shard_map/router_step/pallas_call | solution.py:1042
  459.0 1.5 fusion.5
  460.5 2.0 add_convert_fusion.2
  462.6 2.9 add_convert_fusion.1
  465.5 0.7 concatenate.28
  466.3 0.1 collective-permute-start.4
  466.3 0.1 collective-permute-start.1
  466.4 5.1 collective-permute-start.3
  471.5 3.3 add_convert_fusion
  474.8 0.2 pad_maximum_fusion.refs_6_
  475.0 27.0 %attention_backward.1 = (bf16[4,8,48,320]{3,2,1,0:T(8,128)(2,1)}, bf16[1024,1536]{1,0:T(8,128)(2,1)}) custom-call(bf16[1024,1536]{1,0:T(8,128)(2,1)} %get-tuple-element.107.hidden, bf16[1024,256]{1,0:T(8,128)(2,1)} %get-tuple-element.108.qk, bf16[1024,256]{1,0:T(8,128)(2,1)} %get-tuple-element.109.keys, bf16[1024,256]{1,0:T(8,128)(2,1)} %get-tuple-element.110.values, ...), custom_call_target="tpu_custom_call" | custom-call | tf_op jit(solution)/shard_map/attention_backward/pallas_call | solution.py:1715
  502.1 3.6 convolution_convert_fusion
  505.7 101.2 %last_step.1 = (f32[128,1536]{1,0:T(8,128)S(1)}, bf16[4,2,48,320]{3,2,1,0:T(8,128)(2,1)S(1)}, f32[48,1536]{1,0:T(8,128)S(1)}, f32[48,128]{1,0:T(8,128)S(1)}) custom-call(bf16[4,2,128,1536]{3,2,1,0:T(8,128)(2,1)} %bitcast.92, bf16[128,1536]{1,0:T(8,128)(2,1)S(1)} %bitcast.69, f32[128,1536]{1,0:T(8,128)S(1)} %get-tuple-element.119.refs_2_, ...), custom_call_target="tpu_custom_call" | custom-call | tf_op jit(solution)/shard_map/last_step/pallas_call | solution.py:1042
  606.8 0.1 bitcast_convert_fusion
  607.0 0.7 slice_bitcast_fusion.1
  607.7 0.7 copy.58
  608.4 1.0 copy.57
  609.4 0.7 reshape.227
  610.1 0.2 copy.55
  610.3 0.9 reshape.225
  611.2 0.1 copy.56
  611.3 0.7 reshape.226
  612.0 0.7 slice_reduce_fusion
  612.7 0.3 fusion
  613.0 0.5 convert_divide_fusion
  613.5 12.2 %place_units.1 = (f32[10,192,1024]{2,1,0:T(8,128)}, f32[10,192,512]{2,1,0:T(8,128)}) custom-call(s32[1]{0:T(128)} %bitcast.21.refs_0_, bf16[5,192,768]{2,1,0:T(8,128)(2,1)} %get-tuple-element.128.refs_1_.refs_7_, bf16[5,192,768]{2,1,0:T(8,128)(2,1)} %collective-permute-done.1.refs_2_.refs_8_, bf16[5,192,768]{2,1,0:T(8,128)(2,1)} %collective-permute-done.2.refs_3_.refs_9_, ...), custom_call_target="tpu_custom_call" | custom-call | tf_op jit(solution)/shard_map/place_units/pallas_call | solution.py:658
  625.7 0.7 copy.63
  626.5 0.9 copy.64
  627.3 0.7 copy.65
  (56 shorter events, 0.3 us)
Async XLA Ops:
  0.6 6.0 copy-start.17
  3.4 3.4 copy-start.13
  4.5 2.3 copy-start.15
  5.3 2.0 copy-start.1
  6.6 0.7 copy-start.10
  6.6 1.1 copy-start
  7.7 175.2 %copy-start.19 = (s32[1,16]{1,0:T(1,128)S(1)}, s32[1,16]{1,0:T(1,128)}, u32[]{:S(2)}) copy-start(s32[1,16]{1,0:T(1,128)} %param.17) | copy-start | bytes 196
  7.7 175.3 %copy-start.18 = (s32[1,2]{1,0:T(1,128)S(1)}, s32[1,2]{1,0:T(1,128)}, u32[]{:S(2)}) copy-start(s32[1,2]{1,0:T(1,128)} %param.16) | copy-start | bytes 28
  179.6 1.0 copy-start.7
  180.5 0.9 copy-start.8
  181.4 25.2 %collective-permute-start = (bf16[2,192,768]{2,1,0:T(8,128)(2,1)S(1)}, bf16[2,192,768]{2,1,0:T(8,128)(2,1)S(1)}, u32[]{:S(2)}, u32[]{:S(2)}) collective-permute-start(bf16[2,192,768]{2,1,0:T(8,128)(2,1)S(1)} %get-tuple-element.80), channel_id=1, source_target_pairs={{0,24},{8,16},{16,8},{24,0},{1,25},{9,17},{17,9},{25,1},{2,26},{10... | collective-permute-start | bytes 1769480 | tf_op jit(solution)/shard_map/ppermute | solution.py:1801
  206.6 57.9 %copy-start.3 = (bf16[2,192,768]{2,1,0:T(8,128)(2,1)}, bf16[2,192,768]{2,1,0:T(8,128)(2,1)S(1)}, u32[]{:S(2)}) copy-start(bf16[2,192,768]{2,1,0:T(8,128)(2,1)S(1)} %collective-permute-done.refs_5_.refs_8_) | copy-start | bytes 1769476
  206.6 1.3 copy-start.5
  207.9 56.7 %copy-start.2 = (bf16[1536,128]{1,0:T(8,128)(2,1)S(1)}, bf16[1536,128]{1,0:T(8,128)(2,1)}, u32[]{:S(2)}) copy-start(bf16[1536,128]{1,0:T(8,128)(2,1)} %get-tuple-element.83.router_ref.refs_5_) | copy-start | bytes 1179652
  264.6 15.6 %copy-start.9 = (bf16[2,192,768]{2,1,0:T(8,128)(2,1)}, bf16[2,192,768]{2,1,0:T(8,128)(2,1)S(1)}, u32[]{:S(2)}) copy-start(bf16[2,192,768]{2,1,0:T(8,128)(2,1)S(1)} %get-tuple-element.95.refs_13_) | copy-start | bytes 1769476
  280.2 1.0 copy-start.6
  459.0 6.5 %copy-start.4 = (bf16[4,2,128,192]{3,2,1,0:T(8,128)(2,1)}, bf16[4,2,128,192]{3,2,1,0:T(8,128)(2,1)S(1)}, u32[]{:S(2)}) copy-start(bf16[4,2,128,192]{3,2,1,0:T(8,128)(2,1)S(1)} %get-tuple-element.117) | copy-start | bytes 1179652
  459.0 3.6 copy-start.12
  466.3 147.3 %collective-permute-start.4 = (bf16[2,192,768]{2,1,0:T(8,128)(2,1)}, bf16[2,192,768]{2,1,0:T(8,128)(2,1)}, u32[]{:S(2)}, u32[]{:S(2)}) collective-permute-start(bf16[2,192,768]{2,1,0:T(8,128)(2,1)} %add_convert_fusion.2), channel_id=1, source_target_pairs={{0,24},{8,16},{16,8},{24,0},{1,25},{9,17},{17,9},{25,1},{2,26},{10... | collective-permute-start | bytes 1769480 | tf_op jit(solution)/shard_map/ppermute | solution.py:1859
  466.3 147.2 %collective-permute-start.1 = (bf16[5,192,768]{2,1,0:T(8,128)(2,1)}, bf16[5,192,768]{2,1,0:T(8,128)(2,1)}, u32[]{:S(2)}, u32[]{:S(2)}) collective-permute-start(bf16[5,192,768]{2,1,0:T(8,128)(2,1)} %get-tuple-element.129), channel_id=1, source_target_pairs={{0,4},{4,0},{1,5},{5,1},{2,6},{6,2},{3,7},{7,3},{8,12},{12,8},{9,1... | collective-permute-start | bytes 4423688 | tf_op jit(solution)/shard_map/ppermute | solution.py:1861
  466.4 147.1 %collective-permute-start.3 = (bf16[5,192,768]{2,1,0:T(8,128)(2,1)}, bf16[5,192,768]{2,1,0:T(8,128)(2,1)}, u32[]{:S(2)}, u32[]{:S(2)}) collective-permute-start(bf16[5,192,768]{2,1,0:T(8,128)(2,1)} %add_convert_fusion.1), channel_id=1, source_target_pairs={{0,16},{8,24},{16,0},{24,8},{1,17},{9,25},{17,1},{25,9},{2,18},{10... | collective-permute-start | bytes 4423688 | tf_op jit(solution)/shard_map/ppermute | solution.py:1860
  474.8 138.7 %collective-permute-start.2 = (bf16[5,192,768]{2,1,0:T(8,128)(2,1)}, bf16[5,192,768]{2,1,0:T(8,128)(2,1)}, u32[]{:S(2)}, u32[]{:S(2)}) collective-permute-start(bf16[5,192,768]{2,1,0:T(8,128)(2,1)} %add_convert_fusion), channel_id=1, source_target_pairs={{0,8},{8,0},{16,24},{24,16},{1,9},{9,1},{17,25},{25,17},{2,10},{10... | collective-permute-start | bytes 4423688 | tf_op jit(solution)/shard_map/ppermute | solution.py:1862
  607.7 5.0 copy-start.11
  607.7 5.0 copy-start.14
  607.7 5.0 copy-start.16
  610.1 2.9 copy-start.20
